TPU v7x, 32 devices: a whole 2x2x4 slice. The times are simulated.
32 devices in a mesh: dp: 16 (over z, x, core), tensor: 2 (over y).
Axes of the slice: x: 2, y: 2, z: 4, core: 2. Of those that a mesh axis runs over, the one named last changes fastest.
Arguments:
- token_ids: int32 [32, 1024], P(('dp', 'tensor')), may hold values from 0 to 30719
- lengths: int32 [16, 2], P('dp'), may hold values from 256 to 1024, as said below
- token_table: float32 [30720, 768], P(('dp', 'tensor')), may hold values from -0.75 to 0.75
- table_first: float32 [30720, 768], P(('dp', 'tensor')), may hold values from -1.0430813e-07 to 1.0430813e-07
- table_second: float32 [30720, 768], P(('dp', 'tensor')), may hold values from 3.3302913e-15 to 1.3321165e-14
- qkv_weight: float32 [768, 3, 768], P('dp', None, 'tensor'), may hold values from -0.21875 to 0.21875
- qkv_first: float32 [768, 3, 768], P('dp', None, 'tensor'), may hold values from -8.34465e-07 to 8.34465e-07
- qkv_second: float32 [768, 3, 768], P('dp', None, 'tensor'), may hold values from 3.3302914e-16 to 1.3321165e-15
- out_weight: float32 [768, 768], P('dp', 'tensor'), may hold values from -1.25 to 1.25
- out_first: float32 [768, 768], P('dp', 'tensor'), may hold values from -1.4901161e-07 to 1.4901161e-07
- out_second: float32 [768, 768], P('dp', 'tensor'), may hold values from 1.0899135e-17 to 4.359654e-17
- gate_up_weight: float32 [768, 2, 3072], P('dp', None, 'tensor'), may hold values from -0.21875 to 0.21875
- gate_up_first: float32 [768, 2, 3072], P('dp', None, 'tensor'), may hold values from -4.172325e-07 to 4.172325e-07
- gate_up_second: float32 [768, 2, 3072], P('dp', None, 'tensor'), may hold values from 8.7798585e-17 to 3.5119434e-16
- down_weight: float32 [768, 3072], P('dp', 'tensor'), may hold values from -0.109375 to 0.109375
- down_first: float32 [768, 3072], P('dp', 'tensor'), may hold values from -5.9604645e-07 to 5.9604645e-07
- down_second: float32 [768, 3072], P('dp', 'tensor'), may hold values from 1.6651457e-16 to 6.6605827e-16
- norm_params: float32 [6, 768], replicated, may hold values from -0.8 to 1.4
- norm_first: float32 [6, 768], replicated, may hold values from -9.536743e-07 to 9.536743e-07
- norm_second: float32 [6, 768], replicated, may hold values from 8.1743513e-16 to 3.2697405e-15
- log_inverse_warmth: float32 [], replicated, may hold values from 2 to 2.7
- scale_first: float32 [], replicated, may hold values from -2.2888184e-05 to 2.2888184e-05
- scale_second: float32 [], replicated, may hold values from 3.0275376e-11 to 1.211015e-10
Outputs:
- batch_loss: float32 [], replicated
- grad_norm: float32 [], replicated
- table_first_next: float32 [30720, 768], P(('dp', 'tensor'))
- table_second_next: float32 [30720, 768], P(('dp', 'tensor'))
- table_change: float32 [30720, 768], P(('dp', 'tensor'))
- qkv_first_next: float32 [768, 3, 768], P('dp', None, 'tensor')
- qkv_second_next: float32 [768, 3, 768], P('dp', None, 'tensor')
- qkv_change: float32 [768, 3, 768], P('dp', None, 'tensor')
- out_first_next: float32 [768, 768], P('dp', 'tensor')
- out_second_next: float32 [768, 768], P('dp', 'tensor')
- out_change: float32 [768, 768], P('dp', 'tensor')
- gate_up_first_moment_updated: float32 [768, 2, 3072], P('dp', None, 'tensor')
- gate_up_second_next: float32 [768, 2, 3072], P('dp', None, 'tensor')
- gate_up_change: float32 [768, 2, 3072], P('dp', None, 'tensor')
- down_first_next: float32 [768, 3072], P('dp', 'tensor')
- down_second_next: float32 [768, 3072], P('dp', 'tensor')
- down_change: float32 [768, 3072], P('dp', 'tensor')
- norm_first_next: float32 [6, 768], replicated
- norm_second_next: float32 [6, 768], replicated
- norm_change: float32 [6, 768], replicated
- scale_first_next: float32 [], replicated
- scale_second_next: float32 [], replicated
- scale_change: float32 [], replicated
Inputs may be any that keep to these rules, and one draw needn't show every extreme that they name: `lengths`: each sequence's real tokens come first in its slot of 1024; at least one sequence fills its slot.
All inputs are finite; a program needn't handle non-finite values.
Results may differ from a plain program's by a relative error of at most 0.0095.
Values may be sent and summed in bfloat16 or wider, within the bound.
A program may use at most 256 MiB of HBM per device.

v0:
```python
import jax
import jax.numpy as jnp
from jax import lax
from jax.sharding import PartitionSpec as P

HEAD = 64
STEP = 8


norm_epsilon = 1e-12
rope_base = 1000.0
beta_one = 0.9
beta_two = 0.999
adam_epsilon = 1e-08
learn_rate = 0.01
weight_decay = 0.01
clip_limit = 0.001
masked_score = -1e30


def layer_norm(values, gain, shift):
    centered = values - jnp.mean(values, axis=-1, keepdims=True)
    inverse = lax.rsqrt(jnp.mean(centered * centered, axis=-1, keepdims=True) + norm_epsilon)
    normal = centered * inverse
    return (normal * gain + shift, normal, inverse)


def layer_norm_back(grad_output, normal, inverse, gain):
    grad_normal = grad_output * gain
    mean_grad = jnp.mean(grad_normal, axis=-1, keepdims=True)
    mean_cross = jnp.mean(grad_normal * normal, axis=-1, keepdims=True)
    grad_input = inverse * (grad_normal - mean_grad - normal * mean_cross)
    return (grad_input, jnp.sum(grad_output * normal, axis=0), jnp.sum(grad_output, axis=0))


def rotary_tables(length, width):
    half_width = width // 2
    steps_half = jnp.arange(half_width, dtype=jnp.int32).astype(jnp.float32)
    frequency = rope_base ** (-2.0 * steps_half / width)
    positions = jnp.arange(length, dtype=jnp.int32).astype(jnp.float32)
    angles = positions[:, None] * frequency[None, :]
    return (jnp.cos(angles)[:, None, :], jnp.sin(angles)[:, None, :])


def rotate(values, cosine_table, sine_table):
    half_width = values.shape[-1] // 2
    leading = values[..., :half_width]
    trailing = values[..., half_width:]
    return jnp.concatenate(
        [
            leading * cosine_table - trailing * sine_table,
            trailing * cosine_table + leading * sine_table,
        ],
        axis=-1,
    )


def masked_scores(query_block, key_block, length):
    scores = jnp.einsum(
        "qhe,khe->hqk", query_block, key_block, preferred_element_type=jnp.float32
    ) * HEAD ** (-0.5)
    key_valid = jnp.arange(key_block.shape[0], dtype=jnp.int32) < length
    return jnp.where(key_valid[None, None, :], scores, masked_score)


def attend_one(operands):
    query_block, key_block, value_block, length = operands
    scores = masked_scores(query_block, key_block, length)
    row_max = jnp.max(scores, axis=-1, keepdims=True)
    exponent = jnp.exp(scores - row_max)
    row_total = jnp.sum(exponent, axis=-1, keepdims=True)
    attention_low = (exponent / row_total).astype(jnp.bfloat16)
    mixed_block = jnp.einsum(
        "hqk,khe->qhe", attention_low, value_block, preferred_element_type=jnp.float32
    )
    return (mixed_block, row_max[..., 0] + jnp.log(row_total[..., 0]))


def attention_backward(operands):
    query_block, key_block, value_block, length, log_total, grad_mixed = operands
    scores = masked_scores(query_block, key_block, length)
    probs_full = jnp.exp(scores - log_total[..., None])
    probs_low = probs_full.astype(jnp.bfloat16)
    grad_value = jnp.einsum(
        "hqk,qhe->khe", probs_low, grad_mixed, preferred_element_type=jnp.float32
    )
    grad_probs = jnp.einsum(
        "qhe,khe->hqk", grad_mixed, value_block, preferred_element_type=jnp.float32
    )
    inner_sum = jnp.sum(probs_full * grad_probs, axis=-1, keepdims=True)
    grad_scores = (probs_full * (grad_probs - inner_sum)).astype(jnp.bfloat16)
    grad_query = jnp.einsum(
        "hqk,khe->qhe", grad_scores, key_block, preferred_element_type=jnp.float32
    ) * HEAD ** (-0.5)
    grad_key = jnp.einsum(
        "hqk,qhe->khe", grad_scores, query_block, preferred_element_type=jnp.float32
    ) * HEAD ** (-0.5)
    return (grad_query, grad_key, grad_value)


def gather_tokens(values):
    return lax.all_gather(values, "tensor", axis=0, tiled=True)


def sum_tokens(values):
    return lax.psum_scatter(
        values.astype(jnp.bfloat16), "tensor", scatter_dimension=0, tiled=True
    ).astype(jnp.float32)


def adam_step(weight, first_moment, second_moment, gradient, factor):
    clipped = gradient * factor
    first_next = beta_one * first_moment + (1.0 - beta_one) * clipped
    second_next = beta_two * second_moment + (1.0 - beta_two) * clipped * clipped
    corrected_first = first_next / (1.0 - beta_one**STEP)
    corrected_second = second_next / (1.0 - beta_two**STEP)
    change = -learn_rate * (
        corrected_first / (jnp.sqrt(corrected_second) + adam_epsilon) + weight_decay * weight
    )
    return (first_next, second_next, change)


def per_device(
    token_ids,
    lengths,
    token_table,
    table_first,
    table_second,
    qkv_weight,
    qkv_first,
    qkv_second,
    out_weight,
    out_first,
    out_second,
    gate_up_weight,
    gate_up_first,
    gate_up_second,
    down_weight,
    down_first,
    down_second,
    norm_params,
    norm_first,
    norm_second,
    log_inverse_warmth,
    scale_first,
    scale_second,
):
    slot_ids = token_ids[0]
    pair_lengths = lengths[0]
    seq_rows = slot_ids.shape[0]
    model_width = token_table.shape[1]
    table_low = token_table.astype(jnp.bfloat16)
    vocab_rows = token_table.shape[0] * lax.axis_size("dp") * lax.axis_size("tensor")
    whole_table = lax.all_gather(table_low, ("dp", "tensor"), axis=0, tiled=True)
    embedded = jnp.take(whole_table, slot_ids, axis=0).astype(jnp.float32)
    qkv_shard = qkv_weight.astype(jnp.bfloat16)
    out_shard = out_weight.astype(jnp.bfloat16)
    gate_shard = gate_up_weight.astype(jnp.bfloat16)
    down_shard = down_weight.astype(jnp.bfloat16)
    qkv_full, out_full, gate_full, lowering_projection_complete = (
        lax.all_gather(qkv_shard, "dp", axis=0, tiled=True),
        lax.all_gather(out_shard, "dp", axis=0, tiled=True),
        lax.all_gather(gate_shard, "dp", axis=0, tiled=True),
        lax.all_gather(down_shard, "dp", axis=0, tiled=True),
    )
    cosine_table, sine_table = rotary_tables(seq_rows, HEAD)
    first_out, first_normal, first_inverse = layer_norm(embedded, norm_params[0], norm_params[1])
    first_all = gather_tokens(first_out.astype(jnp.bfloat16))
    qkv = jnp.einsum("td,dkc->tkc", first_all, qkv_full, preferred_element_type=jnp.float32)
    local_heads = qkv.shape[2] // HEAD
    qkv_view = qkv.reshape(2, seq_rows, 3, local_heads, HEAD)
    query_all = rotate(qkv_view[:, :, 0], cosine_table, sine_table).astype(jnp.bfloat16)
    key_all = rotate(qkv_view[:, :, 1], cosine_table, sine_table).astype(jnp.bfloat16)
    value_all = qkv_view[:, :, 2].astype(jnp.bfloat16)
    mixed_all, log_total = lax.map(attend_one, (query_all, key_all, value_all, pair_lengths))
    mixed_low = mixed_all.reshape(2 * seq_rows, local_heads * HEAD).astype(jnp.bfloat16)
    attended = sum_tokens(
        jnp.einsum("tc,oc->to", mixed_low, out_full, preferred_element_type=jnp.float32)
    )
    second_out, second_normal, latter_reciprocal = layer_norm(
        first_out + attended, norm_params[2], norm_params[3]
    )
    second_all = gather_tokens(second_out.astype(jnp.bfloat16))
    gate_up = jnp.einsum("td,dkf->tkf", second_all, gate_full, preferred_element_type=jnp.float32)
    gate_value = gate_up[:, 0]
    up_value = gate_up[:, 1]
    sigmoid_gate = jax.nn.sigmoid(gate_value)
    hidden_low = (gate_value * sigmoid_gate * up_value).astype(jnp.bfloat16)
    branch = sum_tokens(
        jnp.einsum(
            "tf,of->to",
            hidden_low,
            lowering_projection_complete,
            preferred_element_type=jnp.float32,
        )
    )
    third_out, third_normal, third_inverse = layer_norm(
        second_out + branch, norm_params[4], norm_params[5]
    )
    own_length = lax.dynamic_index_in_dim(pair_lengths, lax.axis_index("tensor"), 0, keepdims=False)
    own_valid = jnp.arange(seq_rows, dtype=jnp.int32) < own_length
    length_float = own_length.astype(jnp.float32)
    pooled = jnp.sum(jnp.where(own_valid[:, None], third_out, 0.0), axis=0) / length_float
    inverse_norm = lax.rsqrt(jnp.sum(pooled * pooled) + norm_epsilon)
    embedding_vec = pooled * inverse_norm
    vectors = lax.all_gather(embedding_vec[None, :], ("dp", "tensor"), axis=0, tiled=True)
    queries = vectors[0::2]
    documents = vectors[1::2]
    pair_count = queries.shape[0]
    sharpness_divisor = jnp.exp(log_inverse_warmth)
    cosine_match_matrix = sharpness_divisor * jnp.dot(
        queries, documents.T, precision=lax.Precision.HIGHEST, preferred_element_type=jnp.float32
    )
    row_max = jnp.max(cosine_match_matrix, axis=1, keepdims=True)
    row_exp = jnp.exp(cosine_match_matrix - row_max)
    row_sum = jnp.sum(row_exp, axis=1, keepdims=True)
    column_max = jnp.max(cosine_match_matrix, axis=0, keepdims=True)
    column_exp = jnp.exp(cosine_match_matrix - column_max)
    column_sum = jnp.sum(column_exp, axis=0, keepdims=True)
    diagonal = jnp.diagonal(cosine_match_matrix)
    row_lse = row_max[:, 0] + jnp.log(row_sum[:, 0])
    column_lse = column_max[0] + jnp.log(column_sum[0])
    batch_loss = 0.5 * (jnp.mean(row_lse - diagonal) + jnp.mean(column_lse - diagonal))
    identity = jnp.eye(pair_count, dtype=jnp.float32)
    grad_logits = 0.5 / pair_count * (row_exp / row_sum + column_exp / column_sum - 2.0 * identity)
    grad_log_scale = jnp.sum(grad_logits * cosine_match_matrix)
    question_derivative = sharpness_divisor * jnp.dot(
        grad_logits, documents, precision=lax.Precision.HIGHEST, preferred_element_type=jnp.float32
    )
    passage_derivative = sharpness_divisor * jnp.dot(
        grad_logits.T, queries, precision=lax.Precision.HIGHEST, preferred_element_type=jnp.float32
    )
    grad_vectors = jnp.stack([question_derivative, passage_derivative], axis=1).reshape(
        2 * pair_count, model_width
    )
    grad_own = lax.dynamic_index_in_dim(
        grad_vectors, lax.axis_index(("dp", "tensor")), 0, keepdims=False
    )
    grad_pooled = inverse_norm * (grad_own - embedding_vec * jnp.sum(grad_own * embedding_vec))
    grad_third = jnp.where(own_valid[:, None], grad_pooled[None, :] / length_float, 0.0)
    qkv_back, out_back, gate_back, down_back = (
        lax.all_gather(qkv_shard, "dp", axis=0, tiled=True),
        lax.all_gather(out_shard, "dp", axis=0, tiled=True),
        lax.all_gather(gate_shard, "dp", axis=0, tiled=True),
        lax.all_gather(down_shard, "dp", axis=0, tiled=True),
    )
    grad_second_res, grad_gain_five, grad_shift_five = layer_norm_back(
        grad_third, third_normal, third_inverse, norm_params[4]
    )
    grad_branch_all = gather_tokens(grad_second_res.astype(jnp.bfloat16))
    grad_down = jnp.einsum(
        "to,tf->of", grad_branch_all, hidden_low, preferred_element_type=jnp.float32
    )
    grad_hidden = jnp.einsum(
        "to,of->tf", grad_branch_all, down_back, preferred_element_type=jnp.float32
    )
    grad_up = grad_hidden * gate_value * sigmoid_gate
    grad_gate = grad_hidden * up_value * sigmoid_gate * (1.0 + gate_value * (1.0 - sigmoid_gate))
    grad_gate_up = jnp.stack([grad_gate, grad_up], axis=1).astype(jnp.bfloat16)
    grad_gate_weight = jnp.einsum(
        "td,tkf->dkf", second_all, grad_gate_up, preferred_element_type=jnp.float32
    )
    grad_second = grad_second_res + sum_tokens(
        jnp.einsum("tkf,dkf->td", grad_gate_up, gate_back, preferred_element_type=jnp.float32)
    )
    grad_first_res, grad_gain_three, grad_shift_three = layer_norm_back(
        grad_second, second_normal, latter_reciprocal, norm_params[2]
    )
    grad_attended_all = gather_tokens(grad_first_res.astype(jnp.bfloat16))
    grad_out_weight = jnp.einsum(
        "to,tc->oc", grad_attended_all, mixed_low, preferred_element_type=jnp.float32
    )
    grad_mixed = jnp.einsum(
        "to,oc->tc", grad_attended_all, out_back, preferred_element_type=jnp.float32
    ).astype(jnp.bfloat16)
    grad_mixed = grad_mixed.reshape(2, seq_rows, local_heads, HEAD)
    grad_query, grad_key, grad_value = lax.map(
        attention_backward, (query_all, key_all, value_all, pair_lengths, log_total, grad_mixed)
    )
    grad_query = rotate(grad_query, cosine_table, -sine_table)
    grad_key = rotate(grad_key, cosine_table, -sine_table)
    grad_qkv = (
        jnp.stack([grad_query, grad_key, grad_value], axis=2)
        .reshape(2 * seq_rows, 3, local_heads * HEAD)
        .astype(jnp.bfloat16)
    )
    grad_qkv_weight = jnp.einsum(
        "td,tkc->dkc", first_all, grad_qkv, preferred_element_type=jnp.float32
    )
    grad_first = grad_first_res + sum_tokens(
        jnp.einsum("tkc,dkc->td", grad_qkv, qkv_back, preferred_element_type=jnp.float32)
    )
    grad_embedded, grad_gain_one, grad_shift_one = layer_norm_back(
        grad_first, first_normal, first_inverse, norm_params[0]
    )
    table_summed = jax.ops.segment_sum(grad_embedded, slot_ids, num_segments=vocab_rows)
    grad_table = lax.psum_scatter(table_summed, ("dp", "tensor"), scatter_dimension=0, tiled=True)
    grad_qkv_own, grad_out_own, grad_gate_own, grad_down_own = (
        lax.psum_scatter(grad_qkv_weight, "dp", scatter_dimension=0, tiled=True),
        lax.psum_scatter(grad_out_weight, "dp", scatter_dimension=0, tiled=True),
        lax.psum_scatter(grad_gate_weight, "dp", scatter_dimension=0, tiled=True),
        lax.psum_scatter(grad_down, "dp", scatter_dimension=0, tiled=True),
    )
    grad_norm_rows = jnp.stack(
        [
            grad_gain_one,
            grad_shift_one,
            grad_gain_three,
            grad_shift_three,
            grad_gain_five,
            grad_shift_five,
        ],
        axis=0,
    )
    owned_squares = (
        jnp.sum(grad_table * grad_table)
        + jnp.sum(grad_qkv_own * grad_qkv_own)
        + jnp.sum(grad_out_own * grad_out_own)
    )
    owned_squares = (
        owned_squares
        + jnp.sum(grad_gate_own * grad_gate_own)
        + jnp.sum(grad_down_own * grad_down_own)
    )
    norm_grads, square_total = lax.psum((grad_norm_rows, owned_squares), ("dp", "tensor"))
    squares = square_total + jnp.sum(norm_grads * norm_grads) + grad_log_scale * grad_log_scale
    grad_norm = jnp.sqrt(squares)
    factor = jnp.minimum(1.0, clip_limit / (grad_norm + 1e-06))
    table_new = adam_step(token_table, table_first, table_second, grad_table, factor)
    qkv_new = adam_step(qkv_weight, qkv_first, qkv_second, grad_qkv_own, factor)
    out_new = adam_step(out_weight, out_first, out_second, grad_out_own, factor)
    gate_new = adam_step(gate_up_weight, gate_up_first, gate_up_second, grad_gate_own, factor)
    down_new = adam_step(down_weight, down_first, down_second, grad_down_own, factor)
    norm_new = adam_step(norm_params, norm_first, norm_second, norm_grads, factor)
    scale_new = adam_step(log_inverse_warmth, scale_first, scale_second, grad_log_scale, factor)
    return (
        batch_loss,
        grad_norm,
        table_new[0],
        table_new[1],
        table_new[2],
        qkv_new[0],
        qkv_new[1],
        qkv_new[2],
        out_new[0],
        out_new[1],
        out_new[2],
        gate_new[0],
        gate_new[1],
        gate_new[2],
        down_new[0],
        down_new[1],
        down_new[2],
        norm_new[0],
        norm_new[1],
        norm_new[2],
        scale_new[0],
        scale_new[1],
        scale_new[2],
    )


def solution(mesh):
    in_specs = (
        P(("dp", "tensor"), None),
        P("dp", None),
        P(("dp", "tensor"), None),
        P(("dp", "tensor"), None),
        P(("dp", "tensor"), None),
        P("dp", None, "tensor"),
        P("dp", None, "tensor"),
        P("dp", None, "tensor"),
        P("dp", "tensor"),
        P("dp", "tensor"),
        P("dp", "tensor"),
        P("dp", None, "tensor"),
        P("dp", None, "tensor"),
        P("dp", None, "tensor"),
        P("dp", "tensor"),
        P("dp", "tensor"),
        P("dp", "tensor"),
        P(),
        P(),
        P(),
        P(),
        P(),
        P(),
    )
    out_specs = (
        P(),
        P(),
        P(("dp", "tensor"), None),
        P(("dp", "tensor"), None),
        P(("dp", "tensor"), None),
        P("dp", None, "tensor"),
        P("dp", None, "tensor"),
        P("dp", None, "tensor"),
        P("dp", "tensor"),
        P("dp", "tensor"),
        P("dp", "tensor"),
        P("dp", None, "tensor"),
        P("dp", None, "tensor"),
        P("dp", None, "tensor"),
        P("dp", "tensor"),
        P("dp", "tensor"),
        P("dp", "tensor"),
        P(),
        P(),
        P(),
        P(),
        P(),
        P(),
    )
    return jax.shard_map(
        per_device, mesh=mesh, in_specs=in_specs, out_specs=out_specs, check_vma=False
    )
```

profile of v0, /device:TPU:0, one launch (start us, length us, event | category | flops | bytes accessed | tf_op | source)
XLA Modules:
  0.0 2523.6 jit_solution(5829402106242492807)
XLA Ops:
  12.0 262.7 %all-gather.11.cloned.1.call-done = bf16[30720,768]{1,0:T(8,128)(2,1)} async-done(((bf16[960,768]{1,0:T(8,128)(2,1)}), bf16[30720,768]{1,0:T(8,128)(2,1)}) %all-gather.11.cloned.1.call-update) | async-done | bytes 47185936 | tf_op jit(solution)/shard_map/all_gather | solution.py:154
  274.7 14.2 gather_fusion
  294.0 22.9 all_gather.37
  317.1 46.6 %all-gather.13.cloned.1.call-done = bf16[2048,768]{1,0:T(8,128)(2,1)} async-done(((bf16[1024,768]{1,0:T(8,128)(2,1)}), bf16[2048,768]{1,0:T(8,128)(2,1)}) %all-gather.13.cloned.1.call-update) | async-done | bytes 3145744 | tf_op jit(solution)/shard_map/all_gather | solution.py:102
  363.7 9.9 fusion.73
  373.6 13.5 reshape.314
  409.6 71.3 %while.26 = (s32[]{:T(128)}, bf16[2,1024,6,64]{1,3,2,0:T(8,128)(2,1)}, f32[2,6,1024]{2,1,0:T(8,128)S(1)}, bf16[2,1024,6,64]{1,3,2,0:T(8,128)(2,1)}, s32[2]{0:T(1...) while((s32[]{:T(128)}, bf16[2,1024,6,64]{1,3,2,0:T(8,128)(2,1)}, ...), condition=%wide.region_5.6_spmd, body=%wide.region_2.0_spmd.sunk | while | flops 1686105088 | bytes 180320400 | solution.py:175
  417.4 8.3 copy-done
  432.7 12.7 bitcast_dynamic-update-slice_fusion.6
  452.8 8.3 copy-done
  468.1 12.7 bitcast_dynamic-update-slice_fusion.6
  491.1 41.6 %reduce-scatter.10.cloned.1.call-done = bf16[1024,768]{1,0:T(8,128)(2,1)} async-done(((bf16[2048,768]{1,0:T(8,128)(2,1)}), bf16[1024,768]{1,0:T(8,128)(2,1)}) %reduce-scatter.10.cloned.1.call-update) | async-done | bytes 1572880 | tf_op jit(solution)/shard_map/reduce_scatter | solution.py:106
  539.0 49.9 %all-gather.19.cloned.1.call-done = bf16[768,2,1536]{2,0,1:T(8,128)(2,1)} async-done(((bf16[48,2,1536]{2,0,1:T(8,128)(2,1)}), bf16[768,2,1536]{2,0,1:T(8,128)(2,1)}) %all-gather.19.cloned.1.call-update) | async-done | bytes 4718608 | tf_op jit(solution)/shard_map/all_gather | solution.py:163
  588.9 45.6 %all-gather.17.cloned.1.call-done = bf16[2048,768]{1,0:T(8,128)(2,1)} async-done(((bf16[1024,768]{1,0:T(8,128)(2,1)}), bf16[2048,768]{1,0:T(8,128)(2,1)}) %all-gather.17.cloned.1.call-update) | async-done | bytes 3145744 | tf_op jit(solution)/shard_map/all_gather | solution.py:102
  634.5 17.5 fusion.69
  652.0 12.8 multiply_convert_fusion.3
  664.8 15.2 all-gather.21.cloned.1.call-done
  680.0 9.1 convolution_convert_fusion.1
  691.7 39.7 %reduce-scatter.12.cloned.1.call-done = bf16[1024,768]{1,0:T(8,128)(2,1)} async-done(((bf16[2048,768]{1,0:T(8,128)(2,1)}), bf16[1024,768]{1,0:T(8,128)(2,1)}) %reduce-scatter.12.cloned.1.call-update) | async-done | bytes 1572880 | tf_op jit(solution)/shard_map/reduce_scatter | solution.py:106
  736.8 67.4 %all-gather.1 = f32[32,1,768]{2,1,0:T(1,128)S(1)} all-gather(f32[1,1,768]{2,1,0:T(1,128)S(1)} %reshape.343), channel_id=2, replica_groups=mesh['dp'=16,'tensor'=2] {'dp','tensor'}, dimensions={0}, use_global_device_ids=true | all-gather | bytes 101376 | tf_op jit(solution)/shard_map/all_gather | solution.py:206
  813.5 40.9 %all-gather.23.cloned.1.call-done = bf16[2048,768]{1,0:T(8,128)(2,1)} async-done(((bf16[1024,768]{1,0:T(8,128)(2,1)}), bf16[2048,768]{1,0:T(8,128)(2,1)}) %all-gather.23.cloned.1.call-update) | async-done | bytes 3145744 | tf_op jit(solution)/shard_map/all_gather | solution.py:102
  854.5 19.1 fusion.46
  873.6 15.5 bitcast_convert_fusion.1
  889.2 43.5 %reduce-scatter.14.cloned.1.call-done = bf16[1024,768]{1,0:T(8,128)(2,1)} async-done(((bf16[2048,768]{1,0:T(8,128)(2,1)}), bf16[1024,768]{1,0:T(8,128)(2,1)}) %reduce-scatter.14.cloned.1.call-update) | async-done | bytes 1572880 | tf_op jit(solution)/shard_map/reduce_scatter | solution.py:106
  940.9 45.0 %all-gather.25.cloned.1.call-done = bf16[2048,768]{1,0:T(8,128)(2,1)} async-done(((bf16[1024,768]{1,0:T(8,128)(2,1)}), bf16[2048,768]{1,0:T(8,128)(2,1)}) %all-gather.25.cloned.1.call-update) | async-done | bytes 3145744 | tf_op jit(solution)/shard_map/all_gather | solution.py:102
  994.7 259.5 %while.27 = (s32[]{:T(128)}, f32[2,1024,6,64]{1,0,3,2:T(2,128)}, f32[2,1024,6,64]{1,0,3,2:T(2,128)}, bf16[2,1024,6,64]{1,3,2,0:T(8,128)(2,1)}, bf16[2,1024,6,64]...) while((s32[]{:T(128)}, f32[2,1024,6,64]{1,0,3,2:T(2,128)}, ...), condition=%wide.region_28.29_spmd, body=%wide.region_26.28_spmd.sunk | while | flops 4121684992 | bytes 218021040 | solution.py:277
  996.1 13.1 fusion.155
  1009.2 12.3 bitcast_dynamic-update-slice_fusion.8
  1021.5 17.2 multiply_reduce_fusion.17
  1038.8 17.5 multiply_convert_fusion.5
  1069.2 27.6 %dynamic_update_slice.29 = f32[2,1024,6,64]{1,0,3,2:T(2,128)} dynamic-update-slice(f32[2,1024,6,64]{1,0,3,2:T(2,128)} %get-tuple-element.494, f32[1,1024,6,64]{1,0,3,2:T(1,128)S(1)} %copy.193, s32[]{:T(128)S(6)} %copy.212, s32[]{:T(128)} %constant.75.clone.1..sunk, s32[]{:T(128)} %constant.75.clone.1..sunk, s32[]{:T(128)} %constant.75.clone.1..sunk) | dynamic-update-slice | bytes 3145732 | tf_op jit(solution)/shard_map/while/body/jit(dynamic_update_index_in_dim)/dynamic_update_slice | solution.py:175
  1096.8 27.5 %dynamic_update_slice.28 = f32[2,1024,6,64]{1,0,3,2:T(2,128)} dynamic-update-slice(f32[2,1024,6,64]{1,0,3,2:T(2,128)} %get-tuple-element.493, f32[1,1024,6,64]{1,0,3,2:T(1,128)S(1)} %copy-done.1, s32[]{:T(128)S(6)} %copy.212, s32[]{:T(128)} %constant.75.clone.1..sunk, s32[]{:T(128)} %constant.75.clone.1..sunk, s32[]{:T(128)} %constant.75.clone.1..sunk) | dynamic-update-slice | bytes 3145732 | tf_op jit(solution)/shard_map/while/body/jit(dynamic_update_index_in_dim)/dynamic_update_slice | solution.py:175
  1125.6 13.1 fusion.155
  1138.7 12.3 bitcast_dynamic-update-slice_fusion.8
  1151.0 17.2 multiply_reduce_fusion.17
  1168.2 17.5 multiply_convert_fusion.5
  1198.7 27.6 %dynamic_update_slice.29 = f32[2,1024,6,64]{1,0,3,2:T(2,128)} dynamic-update-slice(f32[2,1024,6,64]{1,0,3,2:T(2,128)} %get-tuple-element.494, f32[1,1024,6,64]{1,0,3,2:T(1,128)S(1)} %copy.193, s32[]{:T(128)S(6)} %copy.212, s32[]{:T(128)} %constant.75.clone.1..sunk, s32[]{:T(128)} %constant.75.clone.1..sunk, s32[]{:T(128)} %constant.75.clone.1..sunk) | dynamic-update-slice | bytes 3145732 | tf_op jit(solution)/shard_map/while/body/jit(dynamic_update_index_in_dim)/dynamic_update_slice | solution.py:175
  1226.3 27.5 %dynamic_update_slice.28 = f32[2,1024,6,64]{1,0,3,2:T(2,128)} dynamic-update-slice(f32[2,1024,6,64]{1,0,3,2:T(2,128)} %get-tuple-element.493, f32[1,1024,6,64]{1,0,3,2:T(1,128)S(1)} %copy-done.1, s32[]{:T(128)S(6)} %copy.212, s32[]{:T(128)} %constant.75.clone.1..sunk, s32[]{:T(128)} %constant.75.clone.1..sunk, s32[]{:T(128)} %constant.75.clone.1..sunk) | dynamic-update-slice | bytes 3145732 | tf_op jit(solution)/shard_map/while/body/jit(dynamic_update_index_in_dim)/dynamic_update_slice | solution.py:175
  1277.3 8.5 bitcast_convert_fusion
  1287.7 9.5 fusion.109
  1303.4 16.3 fusion.43
  1321.7 8.4 fusion.71
  1338.5 32.4 %broadcast_in_dim.123 = f32[30720,768]{1,0:T(8,128)} broadcast(f32[]{:T(128)} %constant.81.clone.1), dimensions={} | broadcast | bytes 94371840 | tf_op jit(solution)/shard_map/broadcast_in_dim | solution.py:296
  1371.0 131.1 %scatter_fusion = f32[30720,768]{1,0:T(8,128)} fusion(f32[30720,768]{1,0:T(8,128)} %broadcast_in_dim.123, s32[1024]{0:T(1024)S(1)} %bitcast.201, f32[1024,768]{1,0:T(8,128)S(1)} %copy-done.9), kind=kCustom, calls=%fused_computation.2 | custom fusion | flops 786432 | bytes 9441280 | tf_op jit(solution)/shard_map/scatter-add | solution.py:296
  1511.5 73.3 %reduce-scatter.24.cloned.1.call-done = f32[48,2,1536]{2,0,1:T(8,128)} async-done(((f32[768,2,1536]{2,0,1:T(8,128)}), f32[48,2,1536]{2,0,1:T(8,128)}) %reduce-scatter.24.cloned.1.call-update) | async-done | bytes 589840 | tf_op jit(solution)/shard_map/reduce_scatter | solution.py:301
  1586.7 69.6 %reduce-scatter.20.cloned.1.call-done = f32[48,3,384]{2,0,1:T(8,128)} async-done(((f32[768,3,384]{2,0,1:T(8,128)}), f32[48,3,384]{2,0,1:T(8,128)}) %reduce-scatter.20.cloned.1.call-update) | async-done | bytes 221200 | tf_op jit(solution)/shard_map/reduce_scatter | solution.py:299
  1657.9 784.1 %reduce-scatter.18.cloned.1.call-done = f32[960,768]{1,0:T(8,128)} async-done(((f32[30720,768]{1,0:T(8,128)}), f32[960,768]{1,0:T(8,128)}) %reduce-scatter.18.cloned.1.call-update) | async-done | bytes 2949136 | tf_op jit(solution)/shard_map/reduce_scatter | solution.py:297
  2448.5 40.3 %all-reduce = (f32[]{:T(128)}, f32[6,768]{1,0:T(8,128)S(1)}) all-reduce(f32[]{:T(128)S(6)} %add.336, f32[6,768]{1,0:T(8,128)S(1)} %stack.70), channel_id=1, replica_groups=mesh['dp'=16,'tensor'=2] {'dp','tensor'}, use_global_device_ids=true, to_apply=%region_43.44 | all-reduce | flops 4609 | bytes 36872 | tf_op jit(solution)/shard_map/psum | solution.py:325
  (314 shorter events, 211.4 us)
Async XLA Ops:
  7.2 267.4 %all-gather.11.cloned.1.call-start = ((), (), s32[]{:S(2)}) async-start(), calls=%async_computation.9 | async-start | bytes 48660480 | tf_op jit(solution)/shard_map/all_gather | solution.py:154
  10.4 306.7 %all-gather.15.cloned.1.call-start = ((), (), s32[]{:S(2)}) async-start(), calls=%async_computation.11 | async-start | bytes 1880064 | tf_op jit(solution)/shard_map/all_gather | solution.py:161
  11.2 352.5 %all-gather.13.cloned.1.call-start = ((), (), s32[]{:S(2)}) async-start(), calls=%async_computation.10 | async-start | bytes 4718592 | tf_op jit(solution)/shard_map/all_gather | solution.py:102
  11.9 278.3 %copy-start.39 = (f32[768]{0:T(1024)}, f32[768]{0:T(1024)S(1)}, u32[]{:S(2)}) copy-start(f32[768]{0:T(1024)S(1)} %get-tuple-element.247) | copy-start | bytes 9220
  11.9 278.3 %copy-start.49 = (f32[768]{0:T(1024)}, f32[768]{0:T(1024)S(1)}, u32[]{:S(2)}) copy-start(f32[768]{0:T(1024)S(1)} %get-tuple-element.246) | copy-start | bytes 9220
  11.9 278.3 %copy-start.45 = (pred[1024]{0:T(1024)(128)(4,1)}, pred[1024]{0:T(1024)(128)(4,1)S(1)}, u32[]{:S(2)}) copy-start(pred[1024]{0:T(1024)(128)(4,1)S(1)} %compare_and_fusion) | copy-start | bytes 3076
  292.7 240.0 %reduce-scatter.10.cloned.1.call-start = ((), (), s32[]{:S(2)}) async-start(), calls=%async_computation.12 | async-start | bytes 4718592 | tf_op jit(solution)/shard_map/reduce_scatter | solution.py:106
  294.0 103.5 %copy-start.21 = (f32[1024,32]{0,1:T(8,128)}, f32[1024,32]{0,1:T(8,128)S(1)}, u32[]{:S(2)}) copy-start(f32[1024,32]{0,1:T(8,128)S(1)} %get-tuple-element.340) | copy-start | bytes 393220
  417.4 8.3 copy-start
  452.8 8.3 copy-start
  480.9 4.7 copy-start.29
  489.1 43.6 %copy-start.33 = (f32[1024]{0:T(1024)S(1)}, f32[1024]{0:T(1024)}, u32[]{:S(2)}) copy-start(f32[1024]{0:T(1024)} %copy-done.32) | copy-start | bytes 12292
  489.1 43.6 %copy-start.37 = (f32[1024]{0:T(1024)S(1)}, f32[1024]{0:T(1024)}, u32[]{:S(2)}) copy-start(f32[1024]{0:T(1024)} %copy-done.36) | copy-start | bytes 12292
  489.1 43.6 %copy-start.40 = (f32[768]{0:T(1024)S(1)}, f32[768]{0:T(1024)}, u32[]{:S(2)}) copy-start(f32[768]{0:T(1024)} %copy-done.39) | copy-start | bytes 9220
  489.1 43.6 %copy-start.46 = (pred[1024]{0:T(1024)(128)(4,1)S(1)}, pred[1024]{0:T(1024)(128)(4,1)}, u32[]{:S(2)}) copy-start(pred[1024]{0:T(1024)(128)(4,1)} %copy-done.45) | copy-start | bytes 3076
  489.1 43.6 %copy-start.50 = (f32[768]{0:T(1024)S(1)}, f32[768]{0:T(1024)}, u32[]{:S(2)}) copy-start(f32[768]{0:T(1024)} %copy-done.49) | copy-start | bytes 9220
  489.2 99.8 %all-gather.19.cloned.1.call-start = ((), (), s32[]{:S(2)}) async-start(), calls=%async_computation.14 | async-start | bytes 5013504 | tf_op jit(solution)/shard_map/all_gather | solution.py:163
  491.0 143.5 %all-gather.17.cloned.1.call-start = ((), (), s32[]{:S(2)}) async-start(), calls=%async_computation.13 | async-start | bytes 4718592 | tf_op jit(solution)/shard_map/all_gather | solution.py:102
  538.2 141.8 %all-gather.21.cloned.1.call-start = ((), (), s32[]{:S(2)}) async-start(), calls=%async_computation.15 | async-start | bytes 2506752 | tf_op jit(solution)/shard_map/all_gather | solution.py:164
  539.0 192.4 %reduce-scatter.12.cloned.1.call-start = ((), (), s32[]{:S(2)}) async-start(), calls=%async_computation.16 | async-start | bytes 4718592 | tf_op jit(solution)/shard_map/reduce_scatter | solution.py:106
  689.1 165.4 %all-gather.23.cloned.1.call-start = ((), (), s32[]{:S(2)}) async-start(), calls=%async_computation.17 | async-start | bytes 4718592 | tf_op jit(solution)/shard_map/all_gather | solution.py:102
  804.6 8.8 copy-start.58
  804.6 8.8 copy-start.60
  804.8 8.6 copy-start.62
  804.8 8.6 copy-start.64
  805.6 5.7 copy-start.3
  813.5 119.1 %reduce-scatter.14.cloned.1.call-start = ((), (), s32[]{:S(2)}) async-start(), calls=%async_computation.18 | async-start | bytes 4718592 | tf_op jit(solution)/shard_map/reduce_scatter | solution.py:106
  889.1 96.8 %all-gather.25.cloned.1.call-start = ((), (), s32[]{:S(2)}) async-start(), calls=%async_computation.19 | async-start | bytes 4718592 | tf_op jit(solution)/shard_map/all_gather | solution.py:102
  940.9 389.4 %reduce-scatter.16.cloned.1.call-start = ((), (), s32[]{:S(2)}) async-start(), calls=%async_computation.20 | async-start | bytes 4718592 | tf_op jit(solution)/shard_map/reduce_scatter | solution.py:106
  1069.2 27.6 %copy-start.1 = (f32[1,1024,6,64]{1,0,3,2:T(1,128)S(1)}, f32[1,1024,6,64]{1,0,3,2:T(1,128)}, u32[]{:S(2)}) copy-start(f32[1,1024,6,64]{1,0,3,2:T(1,128)} %copy.192) | copy-start | bytes 4718596 | tf_op jit(solution)/shard_map/while
  1198.7 27.6 %copy-start.1 = (f32[1,1024,6,64]{1,0,3,2:T(1,128)S(1)}, f32[1,1024,6,64]{1,0,3,2:T(1,128)}, u32[]{:S(2)}) copy-start(f32[1,1024,6,64]{1,0,3,2:T(1,128)} %copy.192) | copy-start | bytes 4718596 | tf_op jit(solution)/shard_map/while
  1285.8 222.5 %reduce-scatter.26.cloned.1.call-start = ((), (), s32[]{:S(2)}) async-start(), calls=%async_computation.25 | async-start | bytes 5013504 | tf_op jit(solution)/shard_map/reduce_scatter | solution.py:302
  1297.2 212.8 %reduce-scatter.22.cloned.1.call-start = ((), (), s32[]{:S(2)}) async-start(), calls=%async_computation.23 | async-start | bytes 1253376 | tf_op jit(solution)/shard_map/reduce_scatter | solution.py:300
  1303.4 281.4 %reduce-scatter.24.cloned.1.call-start = ((), (), s32[]{:S(2)}) async-start(), calls=%async_computation.24 | async-start | bytes 10027008 | tf_op jit(solution)/shard_map/reduce_scatter | solution.py:301
  1319.7 336.6 %reduce-scatter.20.cloned.1.call-start = ((), (), s32[]{:S(2)}) async-start(), calls=%async_computation.22 | async-start | bytes 3760128 | tf_op jit(solution)/shard_map/reduce_scatter | solution.py:299
  1330.2 1111.9 %reduce-scatter.18.cloned.1.call-start = ((), (), s32[]{:S(2)}) async-start(), calls=%async_computation.21 | async-start | bytes 97320960 | tf_op jit(solution)/shard_map/reduce_scatter | solution.py:297
  1338.5 32.4 %copy-start.9 = (f32[1024,768]{1,0:T(8,128)S(1)}, f32[1024,768]{1,0:T(8,128)}, u32[]{:S(2)}) copy-start(f32[1024,768]{1,0:T(8,128)} %fusion.61) | copy-start | bytes 9437188
  1338.5 32.4 %copy-start.52 = (s32[1,1024]{1,0:T(1,128)S(1)}, s32[1,1024]{1,0:T(1,128)}, u32[]{:S(2)}) copy-start(s32[1,1024]{1,0:T(1,128)} %param.27) | copy-start | bytes 12292
  1502.1 6.2 copy-start.56
  1502.1 6.2 copy-start.55
  1502.1 989.3 %copy-start.14 = (f32[48,2,1536]{2,1,0:T(2,128)S(1)}, f32[48,2,1536]{2,1,0:T(2,128)}, u32[]{:S(2)}) copy-start(f32[48,2,1536]{2,1,0:T(2,128)} %param.38) | copy-start | bytes 1769476
  1502.2 989.3 %copy-start.27 = (f32[48,2,1536]{2,1,0:T(2,128)S(1)}, f32[48,2,1536]{2,1,0:T(2,128)}, u32[]{:S(2)}) copy-start(f32[48,2,1536]{2,1,0:T(2,128)} %param.40) | copy-start | bytes 1769476
  1502.2 989.3 %copy-start.28 = (f32[48,2,1536]{2,1,0:T(2,128)S(1)}, f32[48,2,1536]{2,1,0:T(2,128)}, u32[]{:S(2)}) copy-start(f32[48,2,1536]{2,1,0:T(2,128)} %param.39) | copy-start | bytes 1769476
  1584.8 906.7 %copy-start.15 = (f32[48,2,1536]{2,0,1:T(8,128)S(1)}, f32[48,2,1536]{2,0,1:T(8,128)}, u32[]{:S(2)}) copy-start(f32[48,2,1536]{2,0,1:T(8,128)} %reduce-scatter.24.cloned.1.call-done) | copy-start | bytes 1769476
  2492.1 9.4 copy-start.24
  2492.1 9.4 copy-start.25
  2493.4 10.2 copy-start.10
  2496.0 7.6 copy-start.11
  (39 other events, 85.6 us)
Sparse Core Ops, SparseCore 0:
  11.6 263.0 all-gather.10
  277.5 39.5 all-gather.14
  319.3 44.3 all-gather.12
  489.3 43.3 reduce-scatter.9
  535.6 53.2 all-gather.18
  591.0 43.4 all-gather.16
  637.6 42.3 all-gather.20
  689.2 42.1 reduce-scatter.11
  813.6 40.7 all-gather.22
  889.2 43.3 reduce-scatter.13
  941.0 44.9 all-gather.24
  1285.9 43.3 reduce-scatter.15
  1333.1 75.5 reduce-scatter.25
  1412.6 57.0 reduce-scatter.21
  1474.3 110.4 reduce-scatter.23
  1588.5 67.7 reduce-scatter.19
  1662.6 779.4 reduce-scatter.17
where the time goes:
time: 2540 us; the launch traced here: 2520 us
  waiting for transfers between devices  1560 us (61%)
  other arithmetic  284 us (11%)
  matrix products  267 us (11%)
  local copies, waits for them, and re-layouts  249 us (10%)
  blocking collectives  131 us (5%)
  between operations  32.4 us (1%)
    reduce_scatter x1, waiting for transfers between devices, per_device(): lax.psum_scatter(table_summed, ('dp', 'tensor'), scatter_dimension=0, til...  784 us
    all_gather x1, waiting for transfers between devices, per_device(): lax.all_gather(table_low, ('dp', 'tensor'), axis=0, tiled=True)  263 us
    all_gather x4, waiting for transfers between devices, gather_tokens(): return lax.all_gather(values, 'tensor', axis=0, tiled=True)  178 us
    scatter-add x1, other arithmetic, per_device(): jax.ops.segment_sum(grad_embedded, slot_ids, num_segments=vocab_rows)  131 us
    reduce_scatter x4, waiting for transfers between devices, sum_tokens(): lax.psum_scatter(values.astype(jnp.bfloat16), 'tensor', scatter_dimension...  125 us
    dynamic_update_slice x8, local copies, waits for them, and re-layouts, per_device(): lax.map(attend_one, (query_all, key_all, value_all, pair_lengths))  119 us
    reduce_scatter x1, waiting for transfers between devices, per_device(): lax.psum_scatter(grad_gate_weight, 'dp', scatter_dimension=0, tiled=True)  73.3 us
    reduce_scatter x1, waiting for transfers between devices, per_device(): lax.psum_scatter(grad_qkv_weight, 'dp', scatter_dimension=0, tiled=True)  69.6 us
  transfers between devices with their start and end apart: 17, of which 14 were waited for; matrix products, arithmetic and copies ran while one was open for 11% of the time, Pallas kernels for 0%

commit v1 on v0

v1 whole, which is shorter than its diff:
```python
import functools

import jax
import jax.numpy as jnp
from jax import lax
from jax.experimental import pallas as pl
from jax.experimental.pallas import tpu as pltpu
from jax.sharding import PartitionSpec as P

HEAD = 64
STEP = 8

norm_epsilon = 1e-12
rope_base = 1000.0
beta_one = 0.9
beta_two = 0.999
adam_epsilon = 1e-08
learn_rate = 0.01
weight_decay = 0.01
clip_limit = 0.001
masked_score = -1e30

AXES = ("dp", "tensor")
F32 = jnp.float32
BF16 = jnp.bfloat16
LANES = 128
VMEM_LIMIT = 58 * 1024 * 1024
ROW_BLOCK = 256
HIDDEN_BLOCK = 256


class Plan:
    def __init__(self, mesh, width):
        self.dp = mesh.shape["dp"]
        self.tensor = mesh.shape["tensor"]
        self.count = self.dp * self.tensor
        self.shard = width // self.dp
        self.stepped = self.dp % 4 == 0 and self.shard % 16 == 0
        if self.stepped:
            self.nc, self.nx, self.nz = 2, 2, self.dp // 4
        else:
            self.nc, self.nx, self.nz = 1, 1, 1
        self.rows = width // (self.nc * self.nx * self.nz)

    def places(self):
        dp_index, tensor_index = lax.axis_index("dp"), lax.axis_index("tensor")
        if not self.stepped:
            zero = jnp.int32(0)
            return zero, zero, zero, zero
        core = lax.rem(dp_index, self.nc)
        across = lax.rem(dp_index // self.nc, self.nx)
        return dp_index // (self.nc * self.nx), across, core, tensor_index

    def size(self, axis):
        return {"z": self.nz, "x": self.nx, "c": self.nc, "y": self.tensor}[axis]

    def shift(self, values, axis, by):
        pairs = []
        for z in range(self.nz):
            for x in range(self.nx):
                for c in range(self.nc):
                    for y in range(self.tensor):
                        place = {"z": z, "x": x, "c": c, "y": y}
                        source = self.flat(place)
                        place[axis] = (place[axis] + by) % self.size(axis)
                        pairs.append((source, self.flat(place)))
        return lax.ppermute(values, AXES, pairs)

    def flat(self, place):
        dp_index = (place["z"] * self.nx + place["x"]) * self.nc + place["c"]
        return dp_index * self.tensor + place["y"]

    def gather(self, values, order):
        if not self.stepped:
            whole = lax.all_gather(values, ("tensor", "dp"), axis=0, tiled=True)
            shape = (self.tensor, 1) if order == "yx" else (1, self.tensor)
            return whole.reshape((1,) + shape + (1, self.rows, values.shape[1]))
        stack = values
        for axis in ("z",) + tuple(reversed(order)) + ("c",):
            parts = [stack]
            for far in range(1, self.size(axis)):
                parts.append(self.shift(stack, axis, -far))
            stack = jnp.stack(parts)
        return stack

    def scatter(self, parts, order, scale):
        if not self.stepped:
            whole = parts[0].reshape(self.tensor * self.rows, parts[0].shape[-1])
            return lax.psum_scatter(
                whole.astype(F32), ("tensor", "dp"), scatter_dimension=0, tiled=True
            )
        keep, send = parts
        total = keep.astype(F32) + self.shift(send, "c", 1).astype(F32)
        for axis in tuple(order) + ("z",):
            kept = total[0]
            for far in range(1, self.size(axis)):
                sent = (total[far] * scale).astype(jnp.float16)
                kept = kept + self.shift(sent, axis, far).astype(F32) / scale
            total = kept
        return total


    def weight_spec(self, order, columns, locate):
        def index(i, place):
            part, column = locate(i)
            far = lax.rem(part - place[3] + self.tensor, self.tensor)
            if order == "yx":
                return (0, far, 0, 0, 0, column)
            return (0, 0, far, 0, 0, column)

        middle = (None, self.nx) if order == "yx" else (self.nx, None)
        return pl.BlockSpec((self.nc,) + middle + (self.nz, self.rows, columns), index)

    def grad_specs(self, order, columns, locate):
        def index(i, place):
            part, column = locate(i)
            far = lax.rem(part - place[3] + self.tensor, self.tensor)
            if order == "yx":
                return (far, 0, 0, 0, column)
            return (0, far, 0, 0, column)

        middle = (None, self.nx) if order == "yx" else (self.nx, None)
        spec = pl.BlockSpec(middle + (self.nz, self.rows, columns), index)
        return [spec] * self.nc

    def grad_shapes(self, order, columns):
        middle = (self.tensor, self.nx) if order == "yx" else (self.nx, self.tensor)
        shape = middle + (self.nz, self.rows, columns)
        return [jax.ShapeDtypeStruct(shape, F32)] * self.nc

    def assemble(self, place, block, target, first_column):
        columns = block.shape[-1]
        for z in range(self.nz):
            far_z = lax.rem(z - place[0] + self.nz, self.nz)
            for x in range(self.nx):
                far_x = lax.rem(x - place[1] + self.nx, self.nx)
                for c in range(self.nc):
                    far_c = lax.rem(c - place[2] + self.nc, self.nc)
                    start = ((z * self.nx + x) * self.nc + c) * self.rows
                    target[start : start + self.rows, first_column : first_column + columns] = (
                        block[far_c, far_x, far_z]
                    )

    def disperse(self, place, source, first_column, targets):
        columns = targets[0].shape[-1]
        for far_z in range(self.nz):
            z = lax.rem(place[0] + far_z, self.nz)
            for far_x in range(self.nx):
                x = lax.rem(place[1] + far_x, self.nx)
                for far_c in range(self.nc):
                    c = lax.rem(place[2] + far_c, self.nc)
                    start = ((z * self.nx + x) * self.nc + c) * self.rows
                    start = pl.multiple_of(start, 16)
                    targets[far_c][far_x, far_z] = source[
                        pl.ds(start, self.rows), first_column : first_column + columns
                    ]


def dot(left, right):
    return lax.dot_general(left, right, (((1,), (0,)), ((), ())), preferred_element_type=F32)


def dot_last(left, right):
    return lax.dot_general(left, right, (((1,), (1,)), ((), ())), preferred_element_type=F32)


def normalize(values):
    centered = values - jnp.mean(values, axis=-1, keepdims=True)
    inverse = lax.rsqrt(jnp.mean(centered * centered, axis=-1, keepdims=True) + norm_epsilon)
    return centered * inverse, inverse


def normalize_back(grad_output, normal, inverse, gain):
    grad_normal = grad_output * gain
    mean_grad = jnp.mean(grad_normal, axis=-1, keepdims=True)
    mean_cross = jnp.mean(grad_normal * normal, axis=-1, keepdims=True)
    return inverse * (grad_normal - mean_grad - normal * mean_cross)


def rotary_tables(length):
    half_width = HEAD // 2
    steps_half = jnp.arange(half_width, dtype=jnp.int32).astype(F32)
    frequency = rope_base ** (-2.0 * steps_half / HEAD)
    positions = jnp.arange(length, dtype=jnp.int32).astype(F32)
    angles = positions[:, None] * frequency[None, :]
    cosine, sine = jnp.cos(angles), jnp.sin(angles)
    heads = LANES // HEAD
    return (
        jnp.concatenate([cosine, cosine] * heads, axis=1),
        jnp.concatenate([-sine, sine] * heads, axis=1),
    )


def swap_halves(values):
    lane = lax.broadcasted_iota(jnp.int32, values.shape, 1)
    ahead = pltpu.roll(values, LANES - HEAD // 2, 1)
    behind = pltpu.roll(values, HEAD // 2, 1)
    return jnp.where(lax.rem(lane, HEAD) < HEAD // 2, ahead, behind)


def of_head(values, head):
    lane = lax.broadcasted_iota(jnp.int32, values.shape, 1)
    return jnp.where(lane // HEAD == head, values, jnp.zeros_like(values))


def note_peak(peak_out, product):
    largest = jnp.max(jnp.abs(product[...]), axis=0, keepdims=True)
    largest = jnp.broadcast_to(jnp.max(largest, axis=1, keepdims=True), peak_out.shape)

    @pl.when(pl.program_id(0) == 0)
    def _():
        peak_out[...] = largest

    @pl.when(pl.program_id(0) > 0)
    def _():
        peak_out[...] = jnp.maximum(peak_out[...], largest)


def params(**more):
    return pltpu.CompilerParams(vmem_limit_bytes=VMEM_LIMIT, **more)


def whole(shape):
    zeros = (0,) * len(shape)
    return pl.BlockSpec(shape, lambda i, place: zeros, pipeline_mode=pl.Buffered(1))


def result(shape):
    zeros = (0,) * len(shape)
    return pl.BlockSpec(shape, lambda i, place: zeros)


def exchange_partner(me, step):
    distance = 1 << step
    return me + distance - 2 * distance * lax.rem(me // distance, 2)


def exchange_barrier(me, steps, tensor):
    barrier = pltpu.get_barrier_semaphore()
    for step in range(steps):
        partner = exchange_partner(me, step)
        pl.semaphore_signal(
            barrier,
            inc=1,
            device_id=(partner // tensor, lax.rem(partner, tensor)),
            device_id_type=pl.DeviceIdType.MESH,
        )
    pl.semaphore_wait(barrier, steps)


def exchange_blocks(me, steps, tensor, held, send_sem, recv_sem):
    for step in range(steps):
        partner = exchange_partner(me, step)
        size = 1 << step
        base = (me // size) * size
        copy = pltpu.make_async_remote_copy(
            src_ref=held.at[pl.ds(base, size)],
            dst_ref=held.at[pl.ds(base, size)],
            send_sem=send_sem.at[step],
            recv_sem=recv_sem.at[step],
            device_id=(partner // tensor, lax.rem(partner, tensor)),
            device_id_type=pl.DeviceIdType.MESH,
        )
        copy.start()
        copy.wait()


def share_kernel(steps, tensor, block_ref, out_ref, held, send_sem, recv_sem):
    me = lax.axis_index("dp") * tensor + lax.axis_index("tensor")
    exchange_barrier(me, steps, tensor)
    held[pl.ds(me, 1)] = block_ref[...][None]
    exchange_blocks(me, steps, tensor, held, send_sem, recv_sem)
    out_ref[...] = held[...]


def share(plan, block):
    steps = plan.count.bit_length() - 1
    shape = (plan.count,) + block.shape
    return pl.pallas_call(
        functools.partial(share_kernel, steps, plan.tensor),
        name="share",
        out_shape=jax.ShapeDtypeStruct(shape, block.dtype),
        in_specs=[pl.BlockSpec(memory_space=pltpu.VMEM)],
        out_specs=pl.BlockSpec(memory_space=pltpu.VMEM),
        scratch_shapes=[
            pltpu.VMEM(shape, block.dtype),
            pltpu.SemaphoreType.DMA((steps,)),
            pltpu.SemaphoreType.DMA((steps,)),
        ],
        compiler_params=params(collective_id=0, has_side_effects=True),
    )(block)


def total_kernel(steps, tensor, block_ref, out_ref, held, came, send_sem, recv_sem):
    me = lax.axis_index("dp") * tensor + lax.axis_index("tensor")
    exchange_barrier(me, steps, tensor)
    held[0] = block_ref[...]
    for step in range(steps):
        partner = exchange_partner(me, step)
        copy = pltpu.make_async_remote_copy(
            src_ref=held.at[step],
            dst_ref=came.at[step],
            send_sem=send_sem.at[step],
            recv_sem=recv_sem.at[step],
            device_id=(partner // tensor, lax.rem(partner, tensor)),
            device_id_type=pl.DeviceIdType.MESH,
        )
        copy.start()
        copy.wait()
        held[step + 1] = held[step] + came[step]
    out_ref[...] = held[steps]


def total(plan, block, collective_id):
    steps = plan.count.bit_length() - 1
    return pl.pallas_call(
        functools.partial(total_kernel, steps, plan.tensor),
        name="total",
        out_shape=jax.ShapeDtypeStruct(block.shape, block.dtype),
        in_specs=[pl.BlockSpec(memory_space=pltpu.VMEM)],
        out_specs=pl.BlockSpec(memory_space=pltpu.VMEM),
        scratch_shapes=[
            pltpu.VMEM((steps + 1,) + block.shape, block.dtype),
            pltpu.VMEM((steps,) + block.shape, block.dtype),
            pltpu.SemaphoreType.DMA((steps,)),
            pltpu.SemaphoreType.DMA((steps,)),
        ],
        compiler_params=params(collective_id=collective_id, has_side_effects=True),
    )(block)


def wire_scale(plan, peak):
    bound = total(plan, peak, 3)[0, 0]
    exponent = jnp.floor(jnp.log2(32768.0 / jnp.maximum(bound, 1e-30)))
    return jnp.exp2(jnp.clip(exponent, -60.0, 60.0))


def token_places(slot_ids, length, vocab_shard):
    count = slot_ids.shape[0]
    order = jnp.arange(count, dtype=jnp.int32)
    key = jnp.where(order < length, slot_ids, -1)
    owner = key // vocab_shard
    row = key - owner * vocab_shard
    same = key[:, None] == key[None, :]
    first_at = jnp.min(jnp.where(same, order[None, :], count), axis=1)
    first = (first_at == order) & (key >= 0)
    earlier = first[None, :] & (owner[:, None] == owner[None, :])
    place = jnp.sum(
        (earlier & (order[None, :] < first_at[:, None])).astype(jnp.int32), axis=1
    )
    return owner, row, first, jnp.where(key >= 0, place, -1)


def round_slots(owner, place, room, turn):
    within = place - turn * room
    served = (within >= 0) & (within < room)
    return jnp.where(served, owner * room + within, -1)


def round_wants(slot, first, row, slots):
    wanted = first[None, :] & (slot[None, :] == jnp.arange(slots, dtype=jnp.int32)[:, None])
    return jnp.max(jnp.where(wanted, row[None, :], -1), axis=1)


def picked_rows(wants, table_low):
    chosen = wants.reshape(-1)[:, None] == jnp.arange(table_low.shape[0], dtype=jnp.int32)[None, :]
    return jnp.dot(chosen.astype(BF16), table_low, preferred_element_type=F32).astype(BF16)


def spread_rows(slot, rows):
    chosen = slot[:, None] == jnp.arange(rows.shape[0], dtype=jnp.int32)[None, :]
    return jnp.dot(chosen.astype(BF16), rows, preferred_element_type=F32)


def summed_rows(index, rows, count):
    chosen = jnp.arange(count, dtype=jnp.int32)[:, None] == index[None, :]
    return jnp.dot(chosen.astype(BF16), rows, preferred_element_type=F32)


def swap_rows(plan, rows):
    parts = rows.reshape(plan.count, rows.shape[0] // plan.count, rows.shape[1])
    return lax.all_to_all(parts, AXES, 0, 0, tiled=True).reshape(rows.shape)


def attend_kernel(plan, place, x, wq, wk, wv, cosine, sine, q, k, v, mixed, log_total, weights):
    rows = x.shape[0]
    plan.assemble(place, wq, weights, 0)
    plan.assemble(place, wk, weights, LANES)
    plan.assemble(place, wv, weights, 2 * LANES)
    for start in range(0, rows, ROW_BLOCK):
        at = slice(start, start + ROW_BLOCK)
        made = dot(x[at, :], weights[...])
        query, key = made[:, :LANES], made[:, LANES : 2 * LANES]
        query = query * cosine[at, :] + swap_halves(query) * sine[at, :]
        key = key * cosine[at, :] + swap_halves(key) * sine[at, :]
        q[at, :] = (query * HEAD**-0.5).astype(BF16)
        k[at, :] = key.astype(BF16)
        v[at, :] = made[:, 2 * LANES :].astype(BF16)
    position = lax.broadcasted_iota(jnp.int32, (rows, 1), 0)
    bias = jnp.where(position < place[4], 0.0, masked_score)
    keys = k[...]
    values = v[...].T
    for start in range(0, rows, ROW_BLOCK):
        at = slice(start, start + ROW_BLOCK)
        outs = []
        for head in range(LANES // HEAD):
            scores = dot_last(keys, of_head(q[at, :], head)) + bias
            top = jnp.max(scores, axis=0, keepdims=True)
            exponent = jnp.exp(scores - top)
            summed = jnp.sum(exponent, axis=0, keepdims=True)
            out = dot(values[head * HEAD : (head + 1) * HEAD, :], exponent.astype(BF16))
            outs.append(out / summed)
            log_total[head : head + 1, at] = top + jnp.log(summed)
        mixed[at, :] = jnp.concatenate(outs, axis=0).T.astype(BF16)


def attend(plan, place, x, wq, wk, wv, cosine, sine):
    rows, width = x.shape
    pairs = wq.shape[-1] // LANES
    steps = plan.tensor * pairs

    def locate(i):
        return i // pairs, lax.rem(i, pairs)

    by_pair = pl.BlockSpec((None, rows, LANES), lambda i, place: (i, 0, 0))
    shape = jax.ShapeDtypeStruct((steps, rows, LANES), BF16)
    return pl.pallas_call(
        functools.partial(attend_kernel, plan),
        name="attend",
        out_shape=[
            shape,
            shape,
            shape,
            jax.ShapeDtypeStruct((rows, steps * LANES), BF16),
            jax.ShapeDtypeStruct((steps, 8, rows), F32),
        ],
        grid_spec=pltpu.PrefetchScalarGridSpec(
            num_scalar_prefetch=1,
            grid=(steps,),
            in_specs=[
                whole((rows, width)),
                plan.weight_spec("yx", LANES, locate),
                plan.weight_spec("xy", LANES, locate),
                plan.weight_spec("yx", LANES, locate),
                whole((rows, LANES)),
                whole((rows, LANES)),
            ],
            out_specs=[
                by_pair,
                by_pair,
                by_pair,
                pl.BlockSpec((rows, LANES), lambda i, place: (0, i)),
                pl.BlockSpec((None, 8, rows), lambda i, place: (i, 0, 0)),
            ],
            scratch_shapes=[pltpu.VMEM((width, 3 * LANES), BF16)],
        ),
        compiler_params=params(),
        cost_estimate=pl.CostEstimate(
            flops=2 * rows * width * 3 * width + 16 * rows * rows * width,
            bytes_accessed=rows * width * 12,
            transcendentals=0,
        ),
    )(place, x, wq, wk, wv, cosine, sine)


def project_kernel(plan, place, mixed, wo, normal_one, norms, low_out, normal_out, inverse_out, weights):
    rows, width = mixed.shape
    part = wo.shape[-1]
    plan.assemble(place, wo, weights, 0)
    first = pl.program_id(0) == 0

    for start in range(0, rows, ROW_BLOCK):
        at = slice(start, start + ROW_BLOCK)
        product = dot_last(mixed[at, :], weights[...])

        @pl.when(first)
        def _():
            normal_out[at, :] = product

        @pl.when(jnp.logical_not(first))
        def _():
            normal_out[at, :] = normal_out[at, :] + product

    @pl.when(pl.program_id(0) == pl.num_programs(0) - 1)
    def _():
        for start in range(0, rows, ROW_BLOCK):
            at = slice(start, start + ROW_BLOCK)
            first_out = normal_one[at, :] * norms[0:1, :] + norms[1:2, :]
            normal, inverse = normalize(first_out + normal_out[at, :])
            normal_out[at, :] = normal
            inverse_out[at, :] = inverse
            low_out[at, :] = (normal * norms[2:3, :] + norms[3:4, :]).astype(BF16)


def project(plan, place, mixed, wo, normal_one, norms):
    rows, width = mixed.shape
    part = wo.shape[-1]
    return pl.pallas_call(
        functools.partial(project_kernel, plan),
        name="project",
        out_shape=[
            jax.ShapeDtypeStruct((rows, width), BF16),
            jax.ShapeDtypeStruct((rows, width), F32),
            jax.ShapeDtypeStruct((rows, 1), F32),
        ],
        grid_spec=pltpu.PrefetchScalarGridSpec(
            num_scalar_prefetch=1,
            grid=(plan.tensor,),
            in_specs=[
                pl.BlockSpec((rows, part), lambda i, place: (0, i)),
                plan.weight_spec("xy", part, lambda i: (i, 0)),
                whole((rows, width)),
                whole(norms.shape),
            ],
            out_specs=[result((rows, width)), result((rows, width)), result((rows, 1))],
            scratch_shapes=[pltpu.VMEM((width, part), BF16)],
        ),
        compiler_params=params(),
        cost_estimate=pl.CostEstimate(
            flops=2 * rows * width * width, bytes_accessed=rows * width * 14, transcendentals=0
        ),
    )(place, mixed, wo, normal_one, norms)


def feed_kernel(
    plan,
    place,
    x,
    wg,
    wu,
    wd,
    normal_two,
    norms,
    gate_out,
    up_out,
    hidden_out,
    normal_out,
    inverse_out,
    pool_out,
    weights,
    down,
):
    rows, width = x.shape
    plan.assemble(place, wg, weights, 0)
    plan.assemble(place, wu, weights, HIDDEN_BLOCK)
    plan.assemble(place, wd, down, 0)
    first = pl.program_id(0) == 0

    @pl.when(first)
    def _():
        normal_out[...] = jnp.zeros_like(normal_out)

    for start in range(0, rows, ROW_BLOCK):
        at = slice(start, start + ROW_BLOCK)
        made = dot(x[at, :], weights[...])
        gate, up = made[:, :HIDDEN_BLOCK], made[:, HIDDEN_BLOCK:]
        hidden = (gate * jax.nn.sigmoid(gate) * up).astype(BF16)
        gate_out[at, :] = gate.astype(BF16)
        up_out[at, :] = up.astype(BF16)
        hidden_out[at, :] = hidden
        normal_out[at, :] = normal_out[at, :] + dot_last(hidden, down[...])

    @pl.when(pl.program_id(0) == pl.num_programs(0) - 1)
    def _():
        pooled = jnp.zeros((1, width), F32)
        for start in range(0, rows, ROW_BLOCK):
            at = slice(start, start + ROW_BLOCK)
            second_out = normal_two[at, :] * norms[2:3, :] + norms[3:4, :]
            normal, inverse = normalize(second_out + normal_out[at, :])
            normal_out[at, :] = normal
            inverse_out[at, :] = inverse
            position = start + lax.broadcasted_iota(jnp.int32, (ROW_BLOCK, 1), 0)
            kept = jnp.where(position < place[4], normal, 0.0)
            pooled = pooled + jnp.sum(kept, axis=0, keepdims=True)
        pool_out[...] = pooled


def feed(plan, place, x, wg, wu, wd, normal_two, norms):
    rows, width = x.shape
    hidden = wg.shape[-1]
    chunks = hidden // HIDDEN_BLOCK
    steps = plan.tensor * chunks

    def locate(i):
        return i // chunks, lax.rem(i, chunks)

    by_chunk = pl.BlockSpec((rows, HIDDEN_BLOCK), lambda i, place: (0, i))
    shape = jax.ShapeDtypeStruct((rows, plan.tensor * hidden), BF16)
    return pl.pallas_call(
        functools.partial(feed_kernel, plan),
        name="feed",
        out_shape=[
            shape,
            shape,
            shape,
            jax.ShapeDtypeStruct((rows, width), F32),
            jax.ShapeDtypeStruct((rows, 1), F32),
            jax.ShapeDtypeStruct((1, width), F32),
        ],
        grid_spec=pltpu.PrefetchScalarGridSpec(
            num_scalar_prefetch=1,
            grid=(steps,),
            in_specs=[
                whole((rows, width)),
                plan.weight_spec("yx", HIDDEN_BLOCK, locate),
                plan.weight_spec("xy", HIDDEN_BLOCK, locate),
                plan.weight_spec("xy", HIDDEN_BLOCK, locate),
                whole((rows, width)),
                whole(norms.shape),
            ],
            out_specs=[
                by_chunk,
                by_chunk,
                by_chunk,
                result((rows, width)),
                result((rows, 1)),
                result((1, width)),
            ],
            scratch_shapes=[
                pltpu.VMEM((width, 2 * HIDDEN_BLOCK), BF16),
                pltpu.VMEM((width, HIDDEN_BLOCK), BF16),
            ],
        ),
        compiler_params=params(),
        cost_estimate=pl.CostEstimate(
            flops=6 * rows * width * plan.tensor * hidden,
            bytes_accessed=rows * width * 40,
            transcendentals=0,
        ),
    )(place, x, wg, wu, wd, normal_two, norms)


def contrast_kernel(
    steps, tensor, place, pool_ref, norms, scale_ref, loss_ref, grad_ref, held, send_sem, recv_sem
):
    count = held.shape[0]
    me = lax.axis_index("dp") * tensor + lax.axis_index("tensor")
    exchange_barrier(me, steps, tensor)
    length = jnp.full((1, 1), place[4], jnp.int32).astype(F32)
    pooled = pool_ref[...] / length * norms[4:5, :] + norms[5:6, :]
    inverse = lax.rsqrt(jnp.sum(pooled * pooled, axis=-1, keepdims=True) + norm_epsilon)
    vector = pooled * inverse
    held[pl.ds(me, 1)] = vector[None]
    exchange_blocks(me, steps, tensor, held, send_sem, recv_sem)
    vectors = held[...].reshape(count, held.shape[2])
    scale = jnp.exp(scale_ref[...])
    logits = scale * lax.dot_general(
        vectors,
        vectors,
        (((1,), (1,)), ((), ())),
        precision=lax.Precision.HIGHEST,
        preferred_element_type=F32,
    )
    row = lax.broadcasted_iota(jnp.int32, (count, count), 0)
    column = lax.broadcasted_iota(jnp.int32, (count, count), 1)
    crossed = (lax.rem(row, 2) == 0) & (lax.rem(column, 2) == 1)
    shown = jnp.where(crossed, logits, masked_score)
    row_max = jnp.max(shown, axis=1, keepdims=True)
    row_exp = jnp.where(crossed, jnp.exp(shown - row_max), 0.0)
    row_sum = jnp.sum(row_exp, axis=1, keepdims=True)
    column_max = jnp.max(shown, axis=0, keepdims=True)
    column_exp = jnp.where(crossed, jnp.exp(shown - column_max), 0.0)
    column_sum = jnp.sum(column_exp, axis=0, keepdims=True)
    even = lax.rem(lax.broadcasted_iota(jnp.int32, (count, 1), 0), 2) == 0
    odd = lax.rem(lax.broadcasted_iota(jnp.int32, (1, count), 1), 2) == 1
    row_safe = jnp.where(even, row_sum, 1.0)
    column_safe = jnp.where(odd, column_sum, 1.0)
    row_lse = jnp.where(even, row_max + jnp.log(row_safe), 0.0)
    column_lse = jnp.where(odd, column_max + jnp.log(column_safe), 0.0)
    own = crossed & (column == row + 1)
    diagonal = jnp.sum(jnp.where(own, logits, 0.0))
    half = 1.0 / count
    loss = half * (jnp.sum(row_lse) + jnp.sum(column_lse) - 2.0 * diagonal)
    grad_logits = half * (
        row_exp / row_safe + column_exp / column_safe - 2.0 * own.astype(F32)
    )
    grad_scale = jnp.sum(grad_logits * jnp.where(crossed, logits, 0.0))
    both = grad_logits + grad_logits.T
    grad_vectors = scale * lax.dot_general(
        both,
        vectors,
        (((1,), (0,)), ((), ())),
        precision=lax.Precision.HIGHEST,
        preferred_element_type=F32,
    )
    mine = lax.broadcasted_iota(jnp.int32, (count, 1), 0) == me
    grad_own = jnp.sum(jnp.where(mine, grad_vectors, 0.0), axis=0, keepdims=True)
    along = jnp.sum(grad_own * vector, axis=-1, keepdims=True)
    grad_ref[...] = inverse * (grad_own - vector * along) / length
    lane = lax.broadcasted_iota(jnp.int32, loss_ref.shape, 1)
    loss_ref[...] = jnp.where(lane == 0, loss, grad_scale)


def contrast(plan, place, pool, norms, log_scale):
    steps = plan.count.bit_length() - 1
    width = pool.shape[1]
    in_vmem = pl.BlockSpec(memory_space=pltpu.VMEM)
    loss, grad = pl.pallas_call(
        functools.partial(contrast_kernel, steps, plan.tensor),
        name="contrast",
        out_shape=[
            jax.ShapeDtypeStruct((1, LANES), F32),
            jax.ShapeDtypeStruct((1, width), F32),
        ],
        in_specs=[pl.BlockSpec(memory_space=pltpu.SMEM), in_vmem, in_vmem, in_vmem],
        out_specs=[in_vmem, in_vmem],
        scratch_shapes=[
            pltpu.VMEM((plan.count, 1, width), F32),
            pltpu.SemaphoreType.DMA((steps,)),
            pltpu.SemaphoreType.DMA((steps,)),
        ],
        compiler_params=params(collective_id=2, has_side_effects=True),
    )(place, pool, norms, log_scale.reshape(1, 1))
    return loss[0, 0], loss[0, 1], grad


def feed_back_body(plan, place, *refs):
    (
        grad_pool,
        x,
        gate_ref,
        up_ref,
        hidden_ref,
        wg,
        wu,
        wd,
        normal_three,
        inverse_three,
        normal_two,
        inverse_two,
        norms,
    ) = refs[:13]
    nc = plan.nc
    gate_grads = refs[13 : 13 + nc]
    up_grads = refs[13 + nc : 13 + 2 * nc]
    down_grads = refs[13 + 2 * nc : 13 + 3 * nc]
    grad_out, low_out, norm_out, peak_out = refs[13 + 3 * nc : 17 + 3 * nc]
    low, low_turned, x_turned, weights, down, made, product = refs[17 + 3 * nc :]
    rows, width = x.shape

    @pl.when(pl.program_id(0) == 0)
    def _():
        for start in range(0, rows, ROW_BLOCK):
            at = slice(start, start + ROW_BLOCK)
            position = start + lax.broadcasted_iota(jnp.int32, (ROW_BLOCK, 1), 0)
            grad_third = jnp.where(position < place[4], grad_pool[...], 0.0)
            grad = normalize_back(
                grad_third, normal_three[at, :], inverse_three[at, :], norms[4:5, :]
            )
            grad_out[at, :] = grad
            low[at, :] = grad.astype(BF16)
            low_turned[:, at] = grad.astype(BF16).T
            x_turned[:, at] = x[at, :].T

    plan.assemble(place, wg, weights, 0)
    plan.assemble(place, wu, weights, HIDDEN_BLOCK)
    plan.assemble(place, wd, down, 0)
    for start in range(0, rows, ROW_BLOCK):
        at = slice(start, start + ROW_BLOCK)
        grad_hidden = dot(low[at, :], down[...])
        gate = gate_ref[at, :].astype(F32)
        up = up_ref[at, :].astype(F32)
        share_gate = jax.nn.sigmoid(gate)
        grad_up = grad_hidden * gate * share_gate
        grad_gate = grad_hidden * up * share_gate * (1.0 + gate * (1.0 - share_gate))
        made[at, :HIDDEN_BLOCK] = grad_gate.astype(BF16)
        made[at, HIDDEN_BLOCK:] = grad_up.astype(BF16)
        grad_out[at, :] = grad_out[at, :] + dot_last(made[at, :], weights[...])
    product[:, : 2 * HIDDEN_BLOCK] = dot(x_turned[...], made[...])
    product[:, 2 * HIDDEN_BLOCK :] = dot(low_turned[...], hidden_ref[...])
    note_peak(peak_out, product)
    plan.disperse(place, product, 0, gate_grads)
    plan.disperse(place, product, HIDDEN_BLOCK, up_grads)
    plan.disperse(place, product, 2 * HIDDEN_BLOCK, down_grads)

    @pl.when(pl.program_id(0) == pl.num_programs(0) - 1)
    def _():
        gain_grad = jnp.zeros((1, width), F32)
        shift_grad = jnp.zeros((1, width), F32)
        for start in range(0, rows, ROW_BLOCK):
            at = slice(start, start + ROW_BLOCK)
            grad_second = grad_out[at, :]
            normal = normal_two[at, :]
            grad = normalize_back(grad_second, normal, inverse_two[at, :], norms[2:3, :])
            gain_grad = gain_grad + jnp.sum(grad_second * normal, axis=0, keepdims=True)
            shift_grad = shift_grad + jnp.sum(grad_second, axis=0, keepdims=True)
            grad_out[at, :] = grad
            low_out[at, :] = grad.astype(BF16)
        norm_out[0:1, :] = gain_grad
        norm_out[1:2, :] = shift_grad


def feed_back(
    plan,
    place,
    grad_pool,
    x,
    gate,
    up,
    hidden_low,
    wg,
    wu,
    wd,
    normal_three,
    inverse_three,
    normal_two,
    inverse_two,
    norms,
):
    rows, width = x.shape
    hidden = wg.shape[-1]
    chunks = hidden // HIDDEN_BLOCK
    steps = plan.tensor * chunks

    def locate(i):
        return i // chunks, lax.rem(i, chunks)

    by_chunk = pl.BlockSpec((rows, HIDDEN_BLOCK), lambda i, place: (0, i))
    outs = pl.pallas_call(
        functools.partial(feed_back_body, plan),
        name="feed_back",
        out_shape=plan.grad_shapes("yx", hidden)
        + plan.grad_shapes("xy", hidden)
        + plan.grad_shapes("xy", hidden)
        + [
            jax.ShapeDtypeStruct((rows, width), F32),
            jax.ShapeDtypeStruct((rows, width), BF16),
            jax.ShapeDtypeStruct((8, width), F32),
            jax.ShapeDtypeStruct((8, LANES), F32),
        ],
        grid_spec=pltpu.PrefetchScalarGridSpec(
            num_scalar_prefetch=1,
            grid=(steps,),
            in_specs=[
                whole((1, width)),
                whole((rows, width)),
                by_chunk,
                by_chunk,
                by_chunk,
                plan.weight_spec("yx", HIDDEN_BLOCK, locate),
                plan.weight_spec("xy", HIDDEN_BLOCK, locate),
                plan.weight_spec("xy", HIDDEN_BLOCK, locate),
                whole((rows, width)),
                whole((rows, 1)),
                whole((rows, width)),
                whole((rows, 1)),
                whole(norms.shape),
            ],
            out_specs=plan.grad_specs("yx", HIDDEN_BLOCK, locate)
            + plan.grad_specs("xy", HIDDEN_BLOCK, locate)
            + plan.grad_specs("xy", HIDDEN_BLOCK, locate)
            + [
                result((rows, width)),
                result((rows, width)),
                result((8, width)),
                result((8, LANES)),
            ],
            scratch_shapes=[
                pltpu.VMEM((rows, width), BF16),
                pltpu.VMEM((width, rows), BF16),
                pltpu.VMEM((width, rows), BF16),
                pltpu.VMEM((width, 2 * HIDDEN_BLOCK), BF16),
                pltpu.VMEM((width, HIDDEN_BLOCK), BF16),
                pltpu.VMEM((rows, 2 * HIDDEN_BLOCK), BF16),
                pltpu.VMEM((width, 3 * HIDDEN_BLOCK), F32),
            ],
        ),
        compiler_params=params(),
        cost_estimate=pl.CostEstimate(
            flops=12 * rows * width * plan.tensor * hidden,
            bytes_accessed=rows * width * 60,
            transcendentals=0,
        ),
    )(
        place,
        grad_pool,
        x,
        gate,
        up,
        hidden_low,
        wg,
        wu,
        wd,
        normal_three,
        inverse_three,
        normal_two,
        inverse_two,
        norms,
    )
    nc = plan.nc
    return (outs[:nc], outs[nc : 2 * nc], outs[2 * nc : 3 * nc]) + tuple(outs[3 * nc :])


def attend_back_kernel(plan, place, *refs):
    (
        ga,
        x,
        q,
        k,
        v,
        mixed,
        log_total,
        wq,
        wk,
        wv,
        wo,
        cosine,
        sine,
        grad_res,
        normal_one,
        inverse_one,
        norms,
    ) = refs[:17]
    nc = plan.nc
    grads = [refs[17 + n * nc : 17 + (n + 1) * nc] for n in range(4)]
    low_out, norm_out, peak_out = refs[17 + 4 * nc : 20 + 4 * nc]
    (
        ga_turned,
        x_turned,
        weights,
        out_weights,
        total_grad,
        gm,
        made,
        key_grad,
        value_grad,
        product,
    ) = refs[20 + 4 * nc :]
    rows, width = x.shape

    @pl.when(pl.program_id(0) == 0)
    def _():
        for start in range(0, rows, ROW_BLOCK):
            at = slice(start, start + ROW_BLOCK)
            ga_turned[:, at] = ga[at, :].T
            x_turned[:, at] = x[at, :].T
            total_grad[at, :] = grad_res[at, :]

    plan.assemble(place, wq, weights, 0)
    plan.assemble(place, wk, weights, LANES)
    plan.assemble(place, wv, weights, 2 * LANES)
    plan.assemble(place, wo, out_weights, 0)
    for start in range(0, rows, ROW_BLOCK):
        at = slice(start, start + ROW_BLOCK)
        gm[at, :] = dot(ga[at, :], out_weights[...]).astype(BF16)
    position = lax.broadcasted_iota(jnp.int32, (rows, 1), 0)
    bias = jnp.where(position < place[4], 0.0, masked_score)
    keys, values = k[...], v[...]
    keys_turned = keys.T
    for start in range(0, rows, ROW_BLOCK):
        at = slice(start, start + ROW_BLOCK)
        inner = (gm[at, :].astype(F32) * mixed[at, :].astype(F32)).T
        outs = []
        for head in range(LANES // HEAD):
            of = slice(head * HEAD, (head + 1) * HEAD)
            query = of_head(q[at, :], head)
            grad = of_head(gm[at, :], head)
            inner_sum = jnp.sum(inner[of, :], axis=0, keepdims=True)
            scores = dot_last(keys, query) + bias
            probs = jnp.exp(scores - log_total[head : head + 1, at])
            grad_probs = dot_last(values, grad)
            grad_scores = (probs * (grad_probs - inner_sum)).astype(BF16)
            value_part = dot(probs.astype(BF16), grad)
            key_part = dot(grad_scores, query)
            if start == 0 and head == 0:
                value_grad[...] = value_part
                key_grad[...] = key_part
            else:
                value_grad[...] = value_grad[...] + value_part
                key_grad[...] = key_grad[...] + key_part
            outs.append(dot(keys_turned[of, :], grad_scores))
        grad_query = jnp.concatenate(outs, axis=0).T * HEAD**-0.5
        grad_query = grad_query * cosine[at, :] - swap_halves(grad_query) * sine[at, :]
        made[at, :LANES] = grad_query.astype(BF16)
    for start in range(0, rows, ROW_BLOCK):
        at = slice(start, start + ROW_BLOCK)
        grad_key = key_grad[at, :]
        grad_key = grad_key * cosine[at, :] - swap_halves(grad_key) * sine[at, :]
        made[at, LANES : 2 * LANES] = grad_key.astype(BF16)
        made[at, 2 * LANES :] = value_grad[at, :].astype(BF16)
        total_grad[at, :] = total_grad[at, :] + dot_last(made[at, :], weights[...])
    product[:, : 3 * LANES] = dot(x_turned[...], made[...])
    product[:, 3 * LANES :] = dot(ga_turned[...], mixed[...])
    note_peak(peak_out, product)
    for n in range(4):
        plan.disperse(place, product, n * LANES, grads[n])

    @pl.when(pl.program_id(0) == pl.num_programs(0) - 1)
    def _():
        gain_grad = jnp.zeros((1, width), F32)
        shift_grad = jnp.zeros((1, width), F32)
        for start in range(0, rows, ROW_BLOCK):
            at = slice(start, start + ROW_BLOCK)
            grad_first = total_grad[at, :]
            normal = normal_one[at, :]
            grad = normalize_back(grad_first, normal, inverse_one[at, :], norms[0:1, :])
            gain_grad = gain_grad + jnp.sum(grad_first * normal, axis=0, keepdims=True)
            shift_grad = shift_grad + jnp.sum(grad_first, axis=0, keepdims=True)
            low_out[at, :] = grad.astype(BF16)
        norm_out[0:1, :] = gain_grad
        norm_out[1:2, :] = shift_grad


def attend_back(
    plan,
    place,
    ga,
    x,
    q,
    k,
    v,
    mixed,
    log_total,
    wq,
    wk,
    wv,
    wo,
    cosine,
    sine,
    grad_res,
    normal_one,
    inverse_one,
    norms,
):
    rows, width = x.shape
    part = wq.shape[-1]
    pairs = part // LANES
    steps = plan.tensor * pairs

    def locate(i):
        return i // pairs, lax.rem(i, pairs)

    by_pair = pl.BlockSpec((None, rows, LANES), lambda i, place: (i, 0, 0))
    orders = ("yx", "xy", "yx", "xy")
    shapes, specs = [], []
    for order in orders:
        shapes += plan.grad_shapes(order, part)
        specs += plan.grad_specs(order, LANES, locate)
    outs = pl.pallas_call(
        functools.partial(attend_back_kernel, plan),
        name="attend_back",
        out_shape=shapes
        + [
            jax.ShapeDtypeStruct((rows, width), BF16),
            jax.ShapeDtypeStruct((8, width), F32),
            jax.ShapeDtypeStruct((8, LANES), F32),
        ],
        grid_spec=pltpu.PrefetchScalarGridSpec(
            num_scalar_prefetch=1,
            grid=(steps,),
            in_specs=[
                whole((rows, width)),
                whole((rows, width)),
                by_pair,
                by_pair,
                by_pair,
                pl.BlockSpec((rows, LANES), lambda i, place: (0, i)),
                pl.BlockSpec((None, 8, rows), lambda i, place: (i, 0, 0)),
            ]
            + [plan.weight_spec(order, LANES, locate) for order in orders]
            + [
                whole((rows, LANES)),
                whole((rows, LANES)),
                whole((rows, width)),
                whole((rows, width)),
                whole((rows, 1)),
                whole(norms.shape),
            ],
            out_specs=specs + [result((rows, width)), result((8, width)), result((8, LANES))],
            scratch_shapes=[
                pltpu.VMEM((width, rows), BF16),
                pltpu.VMEM((width, rows), BF16),
                pltpu.VMEM((width, 3 * LANES), BF16),
                pltpu.VMEM((width, LANES), BF16),
                pltpu.VMEM((rows, width), F32),
                pltpu.VMEM((rows, LANES), BF16),
                pltpu.VMEM((rows, 3 * LANES), BF16),
                pltpu.VMEM((rows, LANES), F32),
                pltpu.VMEM((rows, LANES), F32),
                pltpu.VMEM((width, 4 * LANES), F32),
            ],
        ),
        compiler_params=params(),
        cost_estimate=pl.CostEstimate(
            flops=16 * rows * width * width + 40 * rows * rows * width,
            bytes_accessed=rows * width * 30,
            transcendentals=0,
        ),
    )(
        place,
        ga,
        x,
        q,
        k,
        v,
        mixed,
        log_total,
        wq,
        wk,
        wv,
        wo,
        cosine,
        sine,
        grad_res,
        normal_one,
        inverse_one,
        norms,
    )
    nc = plan.nc
    return tuple(outs[n * nc : (n + 1) * nc] for n in range(4)) + tuple(outs[4 * nc :])


def adam_step(weight, first_moment, second_moment, gradient, factor):
    clipped = gradient * factor
    first_next = beta_one * first_moment + (1.0 - beta_one) * clipped
    second_next = beta_two * second_moment + (1.0 - beta_two) * clipped * clipped
    corrected_first = first_next / (1.0 - beta_one**STEP)
    corrected_second = second_next / (1.0 - beta_two**STEP)
    change = -learn_rate * (
        corrected_first / (jnp.sqrt(corrected_second) + adam_epsilon) + weight_decay * weight
    )
    return (first_next, second_next, change)


def per_device(
    plan,
    token_ids,
    lengths,
    token_table,
    table_first,
    table_second,
    qkv_weight,
    qkv_first,
    qkv_second,
    out_weight,
    out_first,
    out_second,
    gate_up_weight,
    gate_up_first,
    gate_up_second,
    down_weight,
    down_first,
    down_second,
    norm_params,
    norm_first,
    norm_second,
    log_inverse_warmth,
    scale_first,
    scale_second,
):
    slot_ids = token_ids[0]
    rows = slot_ids.shape[0]
    vocab_shard, width = token_table.shape
    own_length = lax.dynamic_index_in_dim(
        lengths[0], lax.axis_index("tensor"), 0, keepdims=False
    ).astype(jnp.int32)
    place = jnp.stack([jnp.asarray(p, jnp.int32) for p in plan.places()] + [own_length])
    me = lax.axis_index(AXES)

    qkv_low = qkv_weight.astype(BF16)
    gate_up_low = gate_up_weight.astype(BF16)
    wq = plan.gather(qkv_low[:, 0], "yx")
    wk = plan.gather(qkv_low[:, 1], "xy")
    wv = plan.gather(qkv_low[:, 2], "yx")
    wo = plan.gather(out_weight.astype(BF16), "xy")
    wg = plan.gather(gate_up_low[:, 0], "yx")
    wu = plan.gather(gate_up_low[:, 1], "xy")
    wd = plan.gather(down_weight.astype(BF16), "xy")

    table_low = token_table.astype(BF16)
    room = 8 * -(-(5 * rows) // (4 * plan.count * 8))
    slots = room * plan.count
    owner, row, first, token_place = token_places(slot_ids, own_length, vocab_shard)
    slot = round_slots(owner, token_place, room, 0)
    wants = round_wants(slot, first, row, slots)
    rounds = jnp.max(token_place) // room + 1
    note_rows = 8 * -(-(slots + LANES) // (8 * LANES))
    note = jnp.concatenate(
        [wants, jnp.full((note_rows * LANES - slots,), rounds, jnp.int32)]
    ).reshape(note_rows, LANES)
    notes = share(plan, note).reshape(plan.count, note_rows * LANES)
    asked = lax.dynamic_slice_in_dim(notes, me * room, room, axis=1)
    rounds = jnp.max(notes[:, slots])
    embedded = spread_rows(slot, swap_rows(plan, picked_rows(asked, table_low)))

    def ask(turn):
        later = round_slots(owner, token_place, room, turn)
        later_wants = round_wants(later, first, row, slots).reshape(plan.count, room)
        return later, lax.all_to_all(later_wants, AXES, 0, 0, tiled=True)

    def fetch_more(turn, sofar):
        later, later_asked = ask(turn)
        return sofar + spread_rows(later, swap_rows(plan, picked_rows(later_asked, table_low)))

    embedded = lax.fori_loop(1, rounds, fetch_more, embedded)
    normal_one, inverse_one = normalize(embedded)
    first_low = (normal_one * norm_params[0] + norm_params[1]).astype(BF16)

    cosine, sine = rotary_tables(rows)
    q, k, v, mixed, log_total = attend(plan, place, first_low, wq, wk, wv, cosine, sine)
    second_low, normal_two, inverse_two = project(plan, place, mixed, wo, normal_one, norm_params)
    gate, up, hidden_low, normal_three, inverse_three, pool = feed(
        plan, place, second_low, wg, wu, wd, normal_two, norm_params
    )
    batch_loss, grad_log_scale, grad_pool = contrast(
        plan, place, pool, norm_params, log_inverse_warmth
    )
    gate_parts, up_parts, down_parts, grad_first_res, attended_low, norm_two, peak_two = feed_back(
        plan,
        place,
        grad_pool,
        second_low,
        gate,
        up,
        hidden_low,
        wg,
        wu,
        wd,
        normal_three,
        inverse_three,
        normal_two,
        inverse_two,
        norm_params,
    )
    scale_two = wire_scale(plan, peak_two)
    grad_gate = plan.scatter(gate_parts, "yx", scale_two)
    grad_up = plan.scatter(up_parts, "xy", scale_two)
    grad_down_own = plan.scatter(down_parts, "xy", scale_two)
    q_parts, k_parts, v_parts, out_parts, embedded_low, norm_one, peak_one = attend_back(
        plan,
        place,
        attended_low,
        first_low,
        q,
        k,
        v,
        mixed,
        log_total,
        wq,
        wk,
        wv,
        wo,
        cosine,
        sine,
        grad_first_res,
        normal_one,
        inverse_one,
        norm_params,
    )
    grad_rows = summed_rows(slot, embedded_low, slots).astype(BF16)
    grad_table = summed_rows(asked.reshape(-1), swap_rows(plan, grad_rows), vocab_shard)

    def return_more(turn, sofar):
        later, later_asked = ask(turn)
        later_rows = summed_rows(later, embedded_low, slots).astype(BF16)
        return sofar + summed_rows(
            later_asked.reshape(-1), swap_rows(plan, later_rows), vocab_shard
        )

    grad_table = lax.fori_loop(1, rounds, return_more, grad_table)
    scale_one = wire_scale(plan, peak_one)
    grad_qkv_own = jnp.stack(
        [
            plan.scatter(q_parts, "yx", scale_one),
            plan.scatter(k_parts, "xy", scale_one),
            plan.scatter(v_parts, "yx", scale_one),
        ],
        axis=1,
    )
    grad_out_own = plan.scatter(out_parts, "xy", scale_one)
    grad_gate_own = jnp.stack([grad_gate, grad_up], axis=1)

    owned_squares = (
        jnp.sum(grad_table * grad_table)
        + jnp.sum(grad_qkv_own * grad_qkv_own)
        + jnp.sum(grad_out_own * grad_out_own)
        + jnp.sum(grad_gate * grad_gate)
        + jnp.sum(grad_up * grad_up)
        + jnp.sum(grad_down_own * grad_down_own)
    )
    length_float = own_length.astype(F32)
    sums = total(
        plan,
        jnp.concatenate(
            [
                norm_one[0:2],
                norm_two[0:2],
                grad_pool * pool,
                grad_pool * length_float,
                jnp.full((1, width), owned_squares, F32),
                jnp.zeros((1, width), F32),
            ],
            axis=0,
        ),
        1,
    )
    norm_grads = sums[0:6]
    square_total = sums[6, 0]
    squares = square_total + jnp.sum(norm_grads * norm_grads) + grad_log_scale * grad_log_scale
    grad_norm = jnp.sqrt(squares)
    factor = jnp.minimum(1.0, clip_limit / (grad_norm + 1e-06))
    return (
        (batch_loss, grad_norm)
        + adam_step(token_table, table_first, table_second, grad_table, factor)
        + adam_step(qkv_weight, qkv_first, qkv_second, grad_qkv_own, factor)
        + adam_step(out_weight, out_first, out_second, grad_out_own, factor)
        + adam_step(gate_up_weight, gate_up_first, gate_up_second, grad_gate_own, factor)
        + adam_step(down_weight, down_first, down_second, grad_down_own, factor)
        + adam_step(norm_params, norm_first, norm_second, norm_grads, factor)
        + adam_step(log_inverse_warmth, scale_first, scale_second, grad_log_scale, factor)
    )


def solution(mesh):
    rows = P(AXES, None)
    deep = P("dp", None, "tensor")
    flat = P("dp", "tensor")
    in_specs = (
        (rows, P("dp", None)) + (rows,) * 3 + (deep,) * 3 + (flat,) * 3 + (deep,) * 3 + (flat,) * 3
    ) + (P(),) * 6
    out_specs = (
        (P(), P()) + (rows,) * 3 + (deep,) * 3 + (flat,) * 3 + (deep,) * 3 + (flat,) * 3
    ) + (P(),) * 6

    def run(*args):
        plan = Plan(mesh, args[2].shape[1])
        return jax.shard_map(
            functools.partial(per_device, plan),
            mesh=mesh,
            in_specs=in_specs,
            out_specs=out_specs,
            check_vma=False,
        )(*args)

    return run
```

time: 2540 us -> 788 us (0.31)
  waiting for transfers between devices: 1560 us -> 158 us
  Pallas kernels: 0 us -> 303 us
  matrix products: 267 us -> 20.2 us
  local copies, waits for them, and re-layouts: 249 us -> 23.7 us
  other arithmetic: 284 us -> 120 us
  blocking collectives: 131 us -> 0 us
  starting transfers between devices: 0.92 us -> 131 us
    reduce_scatter x9 -> x0, waiting for transfers between devices: 1050 us -> none  [the longest x1 784 us: per_device(): lax.psum_scatter(table_summed, ('dp', 'tensor'), scatter_dimension=0, til...]
    all_gather x8 -> x0, waiting for transfers between devices: 506 us -> none  [the longest x1 263 us: per_device(): lax.all_gather(table_low, ('dp', 'tensor'), axis=0, tiled=True)]
    pallas_call x0 -> x10, Pallas kernels: none -> 303 us  [the longest x1 65.5 us: attend_back(): pl.pallas_call(functools.partial(attend_back_kernel, plan), name='attend_...]
    dot_general x29 -> x4, matrix products: 267 us -> 20.2 us  [the longest x2 10.7 us: summed_rows(): return jnp.dot(chosen.astype(BF16), rows, preferred_element_type=F32)]
    ppermute x0 -> x84, waiting for transfers between devices: none -> 158 us  [shift(): return lax.ppermute(values, AXES, pairs)]
    scatter-add x1 -> x0, other arithmetic: 131 us -> none  [per_device(): jax.ops.segment_sum(grad_embedded, slot_ids, num_segments=vocab_rows)]
    ppermute x0 -> x84, starting transfers between devices: none -> 124 us  [shift(): return lax.ppermute(values, AXES, pairs)]
    dynamic_update_slice x8 -> x0, local copies, waits for them, and re-layouts: 119 us -> none  [per_device(): lax.map(attend_one, (query_all, key_all, value_all, pair_lengths))]
  transfers between devices with their start and end apart: 17 -> 86, of which waited for: 14 -> 31; matrix products, arithmetic and copies ran while one was open for 11% -> 17% of each run, Pallas kernels for 0% -> 14%
where the time goes in v1:
time: 788 us; the launch traced here: 778 us
  Pallas kernels  303 us (38%)
  waiting for transfers between devices  158 us (20%)
  starting transfers between devices  131 us (17%)
  other arithmetic  120 us (15%)
  local copies, waits for them, and re-layouts  23.7 us (3%)
  between operations  20.4 us (3%)
  matrix products  20.2 us (3%)
    ppermute x84, waiting for transfers between devices, shift(): return lax.ppermute(values, AXES, pairs)  158 us
    ppermute x84, starting transfers between devices, shift(): return lax.ppermute(values, AXES, pairs)  124 us
    pallas_call x1, Pallas kernels, attend_back(): pl.pallas_call(functools.partial(attend_back_kernel, plan), name='attend_...  65.5 us
    pallas_call x1, Pallas kernels, feed_back(): pl.pallas_call(functools.partial(feed_back_body, plan), name='feed_back',...  63.9 us
    pallas_call x3, Pallas kernels, total(): pl.pallas_call(functools.partial(total_kernel, steps, plan.tensor), name=...  48.8 us
    another operation x30, other arithmetic, gather(): stack = jnp.stack(parts)  43.5 us
    pallas_call x1, Pallas kernels, attend(): pl.pallas_call(functools.partial(attend_kernel, plan), name='attend', out...  42.9 us
    pallas_call x1, Pallas kernels, feed(): pl.pallas_call(functools.partial(feed_kernel, plan), name='feed', out_sha...  32.4 us
  transfers between devices with their start and end apart: 86, of which 31 were waited for; matrix products, arithmetic and copies ran while one was open for 17% of the time, Pallas kernels for 14%

profile of v1, /device:TPU:0, one launch (start us, length us, event | category | flops | bytes accessed | tf_op | source)
XLA Modules:
  0.0 778.1 jit_solution(16759937311911428851)
XLA Ops:
  1.7 5.1 collective-permute-start.6
  23.7 20.0 %share.1 = s32[32,16,128]{2,1,0:T(8,128)} custom-call(s32[16,128]{1,0:T(8,128)} %pad_bitcast_fusion.block_ref), custom_call_target="tpu_custom_call" | custom-call | tf_op jit(solution)/shard_map/share/pallas_call | solution.py:279
  48.2 3.7 fusion.21
  57.2 3.8 collective-permute-start
  67.5 3.8 collective-permute-start.30
  77.9 6.0 collective-permute-start.26
  83.9 8.9 %collective-permute-done.31 = bf16[48,1536]{1,0:T(8,128)(2,1)S(1)} collective-permute-done((bf16[48,1536]{1,0:T(8,128)(2,1)S(1)}, bf16[48,1536]{1,0:T(8,128)(2,1)S(1)}, u32[]{:S(2)}, u32[]{:S(2)}) %collective-permute-start.31) | collective-permute-done | bytes 147488 | tf_op jit(solution)/shard_map/ppermute | solution.py:67
  98.0 3.9 all-to-all-start.4
  106.0 8.7 %collective-permute-done.37 = bf16[48,1536]{1,0:T(8,128)(2,1)S(1)} collective-permute-done((bf16[48,1536]{1,0:T(8,128)(2,1)}, bf16[48,1536]{1,0:T(8,128)(2,1)S(1)}, u32[]{:S(2)}, u32[]{:S(2)}) %collective-permute-start.37) | collective-permute-done | bytes 147488 | tf_op jit(solution)/shard_map/ppermute | solution.py:67
  121.9 7.4 collective-permute-start.16
  129.5 21.5 %collective-permute-done.10 = bf16[2,4,48,384]{3,2,1,0:T(8,128)(2,1)S(1)} collective-permute-done((bf16[2,4,48,384]{3,2,1,0:T(8,128)(2,1)S(1)}, bf16[2,4,48,384]{3,2,1,0:T(8,128)(2,1)S(1)}, u32[]{:S(2)}, u32[]{:S(2)}) %collective-permute-start.10) | collective-permute-done | bytes 294944 | tf_op jit(solution)/shard_map/ppermute | solution.py:67
  164.0 5.8 collective-permute-done.39
  185.5 6.2 collective-permute-done.34
  191.7 3.8 fusion.164
  198.5 3.8 fusion.165
  202.3 13.8 %collective-permute-done.40 = bf16[2,4,48,1536]{3,2,1,0:T(8,128)(2,1)} collective-permute-done((bf16[2,4,48,1536]{3,2,1,0:T(8,128)(2,1)}, bf16[2,4,48,1536]{3,2,1,0:T(8,128)(2,1)}, u32[]{:S(2)}, u32[]{:S(2)}) %collective-permute-start.40) | collective-permute-done | bytes 1179680 | tf_op jit(solution)/shard_map/ppermute | solution.py:67
  216.1 3.7 fusion.163
  219.9 5.7 fusion.14
  233.6 42.9 %attend.1 = (bf16[6,1024,128]{2,1,0:T(8,128)(2,1)}, bf16[6,1024,128]{2,1,0:T(8,128)(2,1)}, bf16[6,1024,128]{2,1,0:T(8,128)(2,1)}, bf16[1024,768]{1,0:T(8,128)(2,1)}, f32[6,8,1024]{2,1,0:T(8,128)}) custom-call(s32[5]{0:T(128)} %stack.320.place, bf16[1024,768]{1,0:T(8,128)(2,1)} %get-tuple-element.337.x.refs_1_, ...), custom_call_target="tpu_custom_call" | custom-call | flops 16508780544 | bytes 9437184 | tf_op jit(solution)/shard_map/attend/pallas_call | solution.py:427
  276.6 11.0 %project.1 = (bf16[1024,768]{1,0:T(8,128)(2,1)}, f32[1024,768]{1,0:T(8,128)}, f32[1024,1]{1,0:T(8,128)}) custom-call(s32[5]{0:T(128)} %stack.320.place, bf16[1024,768]{1,0:T(8,128)(2,1)} %get-tuple-element.147.mixed.refs_5_, bf16[2,2,2,4,48,384]{5,4,3,2,1,0:T(8,128)(2,1)} %pad_maximum_fusion.9.wo.refs_10_, ...), custom_call_target="tpu_custom_call" | custom-call | flops 1207959552 | bytes 11010048 | tf_op jit(solution)/shard_map/project/pallas_call | solution.py:498
  287.6 4.4 pad_maximum_fusion.1.wu.refs_6_
  292.0 4.4 pad_maximum_fusion.wg.refs_5_
  296.4 4.3 pad_maximum_fusion.2.wd.refs_7_
  300.7 32.4 %feed.1 = (bf16[1024,3072]{1,0:T(8,128)(2,1)}, bf16[1024,3072]{1,0:T(8,128)(2,1)}, bf16[1024,3072]{1,0:T(8,128)(2,1)}, f32[1024,768]{1,0:T(8,128)}, f32[1024,1]{1,0:T(8,128)}, /*index=5*/f32[1,768]{1,0:T(1,128)}) custom-call(s32[5]{0:T(128)} %stack.320.place, bf16[1024,768]{1,0:T(8,128)(2,1)} %get-tuple-element.148.x.refs_1_, ...), custom_call_target="tpu_custom_call" | custom-call | flops 14495514624 | bytes 31457280 | tf_op jit(solution)/shard_map/feed/pallas_call | solution.py:589
  333.1 18.3 %contrast.1 = (f32[1,128]{1,0:T(1,128)}, f32[1,768]{1,0:T(1,128)}) custom-call(s32[5]{0:T(128)} %stack.320.place, f32[1,768]{1,0:T(1,128)} %get-tuple-element.150.pool_ref, f32[6,768]{1,0:T(8,128)} %refs_16_.1, f32[1,1]{1,0:T(1,128)} %bitcast.366.scale_ref), custom_call_target="tpu_custom_call" | custom-call | tf_op jit(solution)/shard_map/contrast/pallas_call | solution.py:698
  351.4 63.9 %feed_back.1 = (f32[2,2,4,48,1536]{4,3,2,1,0:T(8,128)}, f32[2,2,4,48,1536]{4,3,2,1,0:T(8,128)}, f32[2,2,4,48,1536]{4,3,2,1,0:T(8,128)}, f32[2,2,4,48,1536]{4,3,2...) custom-call(s32[5]{0:T(128)} %stack.320.place, ...), custom_call_target="tpu_custom_call" | custom-call | flops 28991029248 | bytes 47185920 | tf_op jit(solution)/shard_map/feed_back/pallas_call | solution.py:819
  415.3 65.5 %attend_back.1 = (f32[2,2,4,48,384]{4,3,2,1,0:T(8,128)}, f32[2,2,4,48,384]{4,3,2,1,0:T(8,128)}, f32[2,2,4,48,384]{4,3,2,1,0:T(8,128)}, f32[2,2,4,48,384]{4,3,2,1...) custom-call(s32[5]{0:T(128)} %stack.320.place, ...), custom_call_target="tpu_custom_call" | custom-call | flops 41875931136 | bytes 23592960 | tf_op jit(solution)/shard_map/attend_back/pallas_call | solution.py:1039
  483.4 17.1 %total.4 = f32[8,128]{1,0:T(8,128)} custom-call(f32[8,128]{1,0:T(8,128)} %get-tuple-element.180.block_ref), custom_call_target="tpu_custom_call" | custom-call | tf_op jit(solution)/shard_map/total/pallas_call | solution.py:316
  502.4 14.6 %total.3 = f32[8,128]{1,0:T(8,128)} custom-call(f32[8,128]{1,0:T(8,128)} %get-tuple-element.171.block_ref), custom_call_target="tpu_custom_call" | custom-call | tf_op jit(solution)/shard_map/total/pallas_call | solution.py:316
  525.5 5.2 fusion.20
  544.5 3.4 all-to-all-start.5
  553.4 10.7 %collective-permute-done.44 = f16[4,48,384]{2,1,0:T(8,128)(2,1)S(1)} collective-permute-done((f16[4,48,384]{2,1,0:T(8,128)(2,1)}, f16[4,48,384]{2,1,0:T(8,128)(2,1)S(1)}, u32[]{:S(2)}, u32[]{:S(2)}) %collective-permute-start.44) | collective-permute-done | bytes 147488 | tf_op jit(solution)/shard_map/ppermute | solution.py:67
  568.7 4.4 collective-permute-start.46
  573.8 3.6 collective-permute-start.47
  577.5 8.1 %collective-permute-done.45 = f16[48,384]{1,0:T(8,128)(2,1)S(1)} collective-permute-done((f16[48,384]{1,0:T(8,128)(2,1)S(1)}, f16[48,384]{1,0:T(8,128)(2,1)S(1)}, u32[]{:S(2)}, u32[]{:S(2)}) %collective-permute-start.45) | collective-permute-done | bytes 36896 | tf_op jit(solution)/shard_map/ppermute | solution.py:67
  585.6 9.0 %collective-permute-start.51 = (f16[48,384]{1,0:T(8,128)(2,1)S(1)}, f16[48,384]{1,0:T(8,128)(2,1)S(1)}, u32[]{:S(2)}, u32[]{:S(2)}) collective-permute-start(f16[48,384]{1,0:T(8,128)(2,1)S(1)} %get-tuple-element.389), channel_id=1, source_target_pairs={{0,8},{1,9},{2,10},{3,11},{4,12},{5,13},{6,14},{7,15},{8,16},{9,17... | collective-permute-start | bytes 110600 | tf_op jit(solution)/shard_map/ppermute | solution.py:67
  607.4 3.6 collective-permute-start.65
  613.9 5.5 fusion.18
  634.2 4.9 add.391
  645.3 9.8 %collective-permute-done.79 = f16[2,4,48,1536]{3,2,1,0:T(8,128)(2,1)S(1)} collective-permute-done((f16[2,4,48,1536]{3,2,1,0:T(8,128)(2,1)}, f16[2,4,48,1536]{3,2,1,0:T(8,128)(2,1)S(1)}, u32[]{:S(2)}, u32[]{:S(2)}) %collective-permute-start.79) | collective-permute-done | bytes 1179680 | tf_op jit(solution)/shard_map/ppermute | solution.py:67
  658.2 21.2 %collective-permute-done.73 = f16[2,4,48,1536]{3,2,1,0:T(8,128)(2,1)S(1)} collective-permute-done((f16[2,4,48,1536]{3,2,1,0:T(8,128)(2,1)S(1)}, f16[2,4,48,1536]{3,2,1,0:T(8,128)(2,1)S(1)}, u32[]{:S(2)}, u32[]{:S(2)}) %collective-permute-start.73) | collective-permute-done | bytes 1179680 | tf_op jit(solution)/shard_map/ppermute | solution.py:67
  690.1 6.3 collective-permute-done.68
  696.8 3.7 collective-permute-start.71
  701.6 3.6 collective-permute-done.69
  705.2 4.7 collective-permute-done.70
  709.9 4.8 collective-permute-start.77
  731.4 17.2 %total.5 = f32[8,768]{1,0:T(8,128)} custom-call(f32[8,768]{1,0:T(8,128)} %concatenate.15.block_ref), custom_call_target="tpu_custom_call" | custom-call | tf_op jit(solution)/shard_map/total/pallas_call | solution.py:316
  762.7 8.6 %add_multiply_fusion = (f32[960,768]{1,0:T(8,128)}, f32[960,768]{1,0:T(8,128)}, f32[960,768]{1,0:T(8,128)}) fusion(f32[960,768]{1,0:T(8,128)S(1)} %copy-done.4, f32[960,768]{1,0:T(8,128)} %get-tuple-element.168, f32[]{:T(128)S(6)} %min_shard_map.3, f32[960,768]{1,0:T(8,128)} %param.31, f32[960,768]{1,0:T(8,128)} %param.30), kind=kLoop, calls=%fused_computation.49 | loop fusion | flops 11059200 | bytes 20643844 | tf_op jit(solution)/shard_map/mul | solution.py:1119
  (392 shorter events, 204.7 us)
Async XLA Ops:
  1.7 55.5 %collective-permute-start.6 = (bf16[48,384]{1,0:T(8,128)(2,1)S(1)}, bf16[48,384]{1,0:T(8,128)(2,1)S(1)}, u32[]{:S(2)}, u32[]{:S(2)}) collective-permute-start(bf16[48,384]{1,0:T(8,128)(2,1)S(1)} %get-tuple-element.417), channel_id=1, source_target_pairs={{0,24},{1,25},{2,26},{3,27},{4,28},{5,29},{6,30},{7,31},{8,0},{9,1... | collective-permute-start | bytes 110600 | tf_op jit(solution)/shard_map/ppermute | solution.py:67
  6.8 50.5 %collective-permute-start.7 = (bf16[48,384]{1,0:T(8,128)(2,1)S(1)}, bf16[48,384]{1,0:T(8,128)(2,1)S(1)}, u32[]{:S(2)}, u32[]{:S(2)}) collective-permute-start(bf16[48,384]{1,0:T(8,128)(2,1)S(1)} %get-tuple-element.417), channel_id=1, source_target_pairs={{0,16},{1,17},{2,18},{3,19},{4,20},{5,21},{6,22},{7,23},{8,24},{9,... | collective-permute-start | bytes 110600 | tf_op jit(solution)/shard_map/ppermute | solution.py:67
  6.8 54.3 %collective-permute-start.8 = (bf16[48,384]{1,0:T(8,128)(2,1)S(1)}, bf16[48,384]{1,0:T(8,128)(2,1)S(1)}, u32[]{:S(2)}, u32[]{:S(2)}) collective-permute-start(bf16[48,384]{1,0:T(8,128)(2,1)S(1)} %get-tuple-element.417), channel_id=1, source_target_pairs={{0,8},{1,9},{2,10},{3,11},{4,12},{5,13},{6,14},{7,15},{8,16},{9,17... | collective-permute-start | bytes 110600 | tf_op jit(solution)/shard_map/ppermute | solution.py:67
  7.8 54.0 %collective-permute-start.12 = (bf16[48,384]{1,0:T(8,128)(2,1)S(1)}, bf16[48,384]{1,0:T(8,128)(2,1)S(1)}, u32[]{:S(2)}, u32[]{:S(2)}) collective-permute-start(bf16[48,384]{1,0:T(8,128)(2,1)S(1)} %get-tuple-element.418), channel_id=1, source_target_pairs={{0,24},{1,25},{2,26},{3,27},{4,28},{5,29},{6,30},{7,31},{8,0},{9,1... | collective-permute-start | bytes 110600 | tf_op jit(solution)/shard_map/ppermute | solution.py:67
  10.6 52.1 %collective-permute-start.13 = (bf16[48,384]{1,0:T(8,128)(2,1)S(1)}, bf16[48,384]{1,0:T(8,128)(2,1)S(1)}, u32[]{:S(2)}, u32[]{:S(2)}) collective-permute-start(bf16[48,384]{1,0:T(8,128)(2,1)S(1)} %get-tuple-element.418), channel_id=1, source_target_pairs={{0,16},{1,17},{2,18},{3,19},{4,20},{5,21},{6,22},{7,23},{8,24},{9,... | collective-permute-start | bytes 110600 | tf_op jit(solution)/shard_map/ppermute | solution.py:67
  71.2 21.6 %collective-permute-start.31 = (bf16[48,1536]{1,0:T(8,128)(2,1)S(1)}, bf16[48,1536]{1,0:T(8,128)(2,1)S(1)}, u32[]{:S(2)}, u32[]{:S(2)}) collective-permute-start(bf16[48,1536]{1,0:T(8,128)(2,1)S(1)} %get-tuple-element.397), channel_id=1, source_target_pairs={{0,16},{1,17},{2,18},{3,19},{4,20},{5,21},{6,22},{7,23},{8,24},{9,... | collective-permute-start | bytes 442376 | tf_op jit(solution)/shard_map/ppermute | solution.py:67
  71.2 21.6 %collective-permute-start.32 = (bf16[48,1536]{1,0:T(8,128)(2,1)S(1)}, bf16[48,1536]{1,0:T(8,128)(2,1)S(1)}, u32[]{:S(2)}, u32[]{:S(2)}) collective-permute-start(bf16[48,1536]{1,0:T(8,128)(2,1)S(1)} %get-tuple-element.397), channel_id=1, source_target_pairs={{0,8},{1,9},{2,10},{3,11},{4,12},{5,13},{6,14},{7,15},{8,16},{9,17... | collective-permute-start | bytes 442376 | tf_op jit(solution)/shard_map/ppermute | solution.py:67
  72.6 23.0 %collective-permute-start.24 = (bf16[48,1536]{1,0:T(8,128)(2,1)}, bf16[48,1536]{1,0:T(8,128)(2,1)S(1)}, u32[]{:S(2)}, u32[]{:S(2)}) collective-permute-start(bf16[48,1536]{1,0:T(8,128)(2,1)} %get-tuple-element.396), channel_id=1, source_target_pairs={{0,24},{1,25},{2,26},{3,27},{4,28},{5,29},{6,30},{7,31},{8,0},{9,1... | collective-permute-start | bytes 442376 | tf_op jit(solution)/shard_map/ppermute | solution.py:67
  75.8 27.9 %collective-permute-start.25 = (bf16[48,1536]{1,0:T(8,128)(2,1)}, bf16[48,1536]{1,0:T(8,128)(2,1)S(1)}, u32[]{:S(2)}, u32[]{:S(2)}) collective-permute-start(bf16[48,1536]{1,0:T(8,128)(2,1)} %get-tuple-element.396), channel_id=1, source_target_pairs={{0,16},{1,17},{2,18},{3,19},{4,20},{5,21},{6,22},{7,23},{8,24},{9,... | collective-permute-start | bytes 442376 | tf_op jit(solution)/shard_map/ppermute | solution.py:67
  77.9 25.9 %collective-permute-start.26 = (bf16[48,1536]{1,0:T(8,128)(2,1)}, bf16[48,1536]{1,0:T(8,128)(2,1)S(1)}, u32[]{:S(2)}, u32[]{:S(2)}) collective-permute-start(bf16[48,1536]{1,0:T(8,128)(2,1)} %get-tuple-element.396), channel_id=1, source_target_pairs={{0,8},{1,9},{2,10},{3,11},{4,12},{5,13},{6,14},{7,15},{8,16},{9,17... | collective-permute-start | bytes 442376 | tf_op jit(solution)/shard_map/ppermute | solution.py:67
  92.8 21.9 %collective-permute-start.37 = (bf16[48,1536]{1,0:T(8,128)(2,1)}, bf16[48,1536]{1,0:T(8,128)(2,1)S(1)}, u32[]{:S(2)}, u32[]{:S(2)}) collective-permute-start(bf16[48,1536]{1,0:T(8,128)(2,1)} %convert_element_type.410), channel_id=1, source_target_pairs={{0,16},{1,17},{2,18},{3,19},{4,20},{5,21},{6,22},{7,23},{8,24},{9,... | collective-permute-start | bytes 442376 | tf_op jit(solution)/shard_map/ppermute | solution.py:67
  95.6 19.2 %collective-permute-start.38 = (bf16[48,1536]{1,0:T(8,128)(2,1)}, bf16[48,1536]{1,0:T(8,128)(2,1)S(1)}, u32[]{:S(2)}, u32[]{:S(2)}) collective-permute-start(bf16[48,1536]{1,0:T(8,128)(2,1)} %convert_element_type.410), channel_id=1, source_target_pairs={{0,8},{1,9},{2,10},{3,11},{4,12},{5,13},{6,14},{7,15},{8,16},{9,17... | collective-permute-start | bytes 442376 | tf_op jit(solution)/shard_map/ppermute | solution.py:67
  98.0 121.9 %all-to-all-start.4 = ((bf16[32,40,768]{2,1,0:T(8,128)(2,1)}), bf16[32,40,768]{2,1,0:T(8,128)(2,1)}, u32[]{:S(2)}, u32[]{:S(2)}) async-start(bf16[32,40,768]{2,1,0:T(8,128)(2,1)} %bitcast.376), calls=%async_computation.4 | async-start | bytes 3932160 | tf_op jit(solution)/shard_map/all_to_all | solution.py:382
  103.8 17.5 %collective-permute-start.15 = (bf16[4,48,384]{2,1,0:T(8,128)(2,1)S(1)}, bf16[4,48,384]{2,1,0:T(8,128)(2,1)S(1)}, u32[]{:S(2)}, u32[]{:S(2)}) collective-permute-start(bf16[4,48,384]{2,1,0:T(8,128)(2,1)S(1)} %copy-done.38), channel_id=1, source_target_pairs={{0,4},{1,5},{2,6},{3,7},{4,0},{5,1},{6,2},{7,3},{8,12},{9,13},{10,... | collective-permute-start | bytes 442376 | tf_op jit(solution)/shard_map/ppermute | solution.py:67
  105.4 16.5 %collective-permute-start.3 = (bf16[4,48,384]{2,1,0:T(8,128)(2,1)S(1)}, bf16[4,48,384]{2,1,0:T(8,128)(2,1)S(1)}, u32[]{:S(2)}, u32[]{:S(2)}) collective-permute-start(bf16[4,48,384]{2,1,0:T(8,128)(2,1)S(1)} %copy-done.39), channel_id=1, source_target_pairs={{0,4},{1,5},{2,6},{3,7},{4,0},{5,1},{6,2},{7,3},{8,12},{9,13},{10,... | collective-permute-start | bytes 442376 | tf_op jit(solution)/shard_map/ppermute | solution.py:67
  114.8 46.2 %collective-permute-start.33 = (bf16[4,48,1536]{2,1,0:T(8,128)(2,1)S(1)}, bf16[4,48,1536]{2,1,0:T(8,128)(2,1)S(1)}, u32[]{:S(2)}, u32[]{:S(2)}) collective-permute-start(bf16[4,48,1536]{2,1,0:T(8,128)(2,1)S(1)} %get-tuple-element.372), channel_id=1, source_target_pairs={{0,1},{1,0},{2,3},{3,2},{4,5},{5,4},{6,7},{7,6},{8,9},{9,8},{10,11... | collective-permute-start | bytes 1769480 | tf_op jit(solution)/shard_map/ppermute | solution.py:67
  118.1 44.4 %collective-permute-start.27 = (bf16[4,48,1536]{2,1,0:T(8,128)(2,1)S(1)}, bf16[4,48,1536]{2,1,0:T(8,128)(2,1)S(1)}, u32[]{:S(2)}, u32[]{:S(2)}) collective-permute-start(bf16[4,48,1536]{2,1,0:T(8,128)(2,1)S(1)} %get-tuple-element.374), channel_id=1, source_target_pairs={{0,4},{1,5},{2,6},{3,7},{4,0},{5,1},{6,2},{7,3},{8,12},{9,13},{10,... | collective-permute-start | bytes 1769480 | tf_op jit(solution)/shard_map/ppermute | solution.py:67
  121.2 29.8 %collective-permute-start.10 = (bf16[2,4,48,384]{3,2,1,0:T(8,128)(2,1)S(1)}, bf16[2,4,48,384]{3,2,1,0:T(8,128)(2,1)S(1)}, u32[]{:S(2)}, u32[]{:S(2)}) collective-permute-start(bf16[2,4,48,384]{3,2,1,0:T(8,128)(2,1)S(1)} %get-tuple-element.404), channel_id=1, source_target_pairs={{0,4},{1,5},{2,6},{3,7},{4,0},{5,1},{6,2},{7,3},{8,12},{9,13},{10,... | collective-permute-start | bytes 884744 | tf_op jit(solution)/shard_map/ppermute | solution.py:67
  121.9 30.9 %collective-permute-start.16 = (bf16[2,4,48,384]{3,2,1,0:T(8,128)(2,1)S(1)}, bf16[2,4,48,384]{3,2,1,0:T(8,128)(2,1)S(1)}, u32[]{:S(2)}, u32[]{:S(2)}) collective-permute-start(bf16[2,4,48,384]{3,2,1,0:T(8,128)(2,1)S(1)} %get-tuple-element.402), channel_id=1, source_target_pairs={{0,1},{1,0},{2,3},{3,2},{4,5},{5,4},{6,7},{7,6},{8,9},{9,8},{10,11... | collective-permute-start | bytes 884744 | tf_op jit(solution)/shard_map/ppermute | solution.py:67
  129.4 28.9 %collective-permute-start.4 = (bf16[2,4,48,384]{3,2,1,0:T(8,128)(2,1)S(1)}, bf16[2,4,48,384]{3,2,1,0:T(8,128)(2,1)S(1)}, u32[]{:S(2)}, u32[]{:S(2)}) collective-permute-start(bf16[2,4,48,384]{3,2,1,0:T(8,128)(2,1)S(1)} %get-tuple-element.406), channel_id=1, source_target_pairs={{0,1},{1,0},{2,3},{3,2},{4,5},{5,4},{6,7},{7,6},{8,9},{9,8},{10,11... | collective-permute-start | bytes 884744 | tf_op jit(solution)/shard_map/ppermute | solution.py:67
  152.7 17.1 %collective-permute-start.39 = (bf16[4,48,1536]{2,1,0:T(8,128)(2,1)S(1)}, bf16[4,48,1536]{2,1,0:T(8,128)(2,1)S(1)}, u32[]{:S(2)}, u32[]{:S(2)}) collective-permute-start(bf16[4,48,1536]{2,1,0:T(8,128)(2,1)S(1)} %get-tuple-element.370), channel_id=1, source_target_pairs={{0,1},{1,0},{2,3},{3,2},{4,5},{5,4},{6,7},{7,6},{8,9},{9,8},{10,11... | collective-permute-start | bytes 1769480 | tf_op jit(solution)/shard_map/ppermute | solution.py:67
  161.0 20.1 %collective-permute-start.5 = (bf16[2,2,4,48,384]{4,3,2,1,0:T(8,128)(2,1)}, bf16[2,2,4,48,384]{4,3,2,1,0:T(8,128)(2,1)}, u32[]{:S(2)}, u32[]{:S(2)}) collective-permute-start(bf16[2,2,4,48,384]{4,3,2,1,0:T(8,128)(2,1)} %get-tuple-element.382), channel_id=1, source_target_pairs={{0,2},{1,3},{2,0},{3,1},{4,6},{5,7},{6,4},{7,5},{8,10},{9,11},{10,... | collective-permute-start | bytes 1769480 | tf_op jit(solution)/shard_map/ppermute | solution.py:67
  162.6 29.1 %collective-permute-start.34 = (bf16[2,4,48,1536]{3,2,1,0:T(8,128)(2,1)}, bf16[2,4,48,1536]{3,2,1,0:T(8,128)(2,1)}, u32[]{:S(2)}, u32[]{:S(2)}) collective-permute-start(bf16[2,4,48,1536]{3,2,1,0:T(8,128)(2,1)} %get-tuple-element.366), channel_id=1, source_target_pairs={{0,4},{1,5},{2,6},{3,7},{4,0},{5,1},{6,2},{7,3},{8,12},{9,13},{10,... | collective-permute-start | bytes 3538952 | tf_op jit(solution)/shard_map/ppermute | solution.py:67
  169.8 28.7 %collective-permute-start.28 = (bf16[2,4,48,1536]{3,2,1,0:T(8,128)(2,1)}, bf16[2,4,48,1536]{3,2,1,0:T(8,128)(2,1)}, u32[]{:S(2)}, u32[]{:S(2)}) collective-permute-start(bf16[2,4,48,1536]{3,2,1,0:T(8,128)(2,1)} %get-tuple-element.368), channel_id=1, source_target_pairs={{0,1},{1,0},{2,3},{3,2},{4,5},{5,4},{6,7},{7,6},{8,9},{9,8},{10,11... | collective-permute-start | bytes 3538952 | tf_op jit(solution)/shard_map/ppermute | solution.py:67
  172.4 43.7 %collective-permute-start.40 = (bf16[2,4,48,1536]{3,2,1,0:T(8,128)(2,1)}, bf16[2,4,48,1536]{3,2,1,0:T(8,128)(2,1)}, u32[]{:S(2)}, u32[]{:S(2)}) collective-permute-start(bf16[2,4,48,1536]{3,2,1,0:T(8,128)(2,1)} %get-tuple-element.364), channel_id=1, source_target_pairs={{0,4},{1,5},{2,6},{3,7},{4,0},{5,1},{6,2},{7,3},{8,12},{9,13},{10,... | collective-permute-start | bytes 3538952 | tf_op jit(solution)/shard_map/ppermute | solution.py:67
  195.4 92.1 %collective-permute-start.35 = (bf16[2,2,4,48,1536]{4,3,2,1,0:T(8,128)(2,1)}, bf16[2,2,4,48,1536]{4,3,2,1,0:T(8,128)(2,1)}, u32[]{:S(2)}, u32[]{:S(2)}) collective-permute-start(bf16[2,2,4,48,1536]{4,3,2,1,0:T(8,128)(2,1)} %get-tuple-element.351), channel_id=1, source_target_pairs={{0,2},{1,3},{2,0},{3,1},{4,6},{5,7},{6,4},{7,5},{8,10},{9,11},{10,... | collective-permute-start | bytes 7077896 | tf_op jit(solution)/shard_map/ppermute | solution.py:67
  202.3 89.7 %collective-permute-start.29 = (bf16[2,2,4,48,1536]{4,3,2,1,0:T(8,128)(2,1)}, bf16[2,2,4,48,1536]{4,3,2,1,0:T(8,128)(2,1)}, u32[]{:S(2)}, u32[]{:S(2)}) collective-permute-start(bf16[2,2,4,48,1536]{4,3,2,1,0:T(8,128)(2,1)} %get-tuple-element.353), channel_id=1, source_target_pairs={{0,2},{1,3},{2,0},{3,1},{4,6},{5,7},{6,4},{7,5},{8,10},{9,11},{10,... | collective-permute-start | bytes 7077896 | tf_op jit(solution)/shard_map/ppermute | solution.py:67
  219.9 76.6 %collective-permute-start.41 = (bf16[2,2,4,48,1536]{4,3,2,1,0:T(8,128)(2,1)}, bf16[2,2,4,48,1536]{4,3,2,1,0:T(8,128)(2,1)}, u32[]{:S(2)}, u32[]{:S(2)}) collective-permute-start(bf16[2,2,4,48,1536]{4,3,2,1,0:T(8,128)(2,1)} %get-tuple-element.349), channel_id=1, source_target_pairs={{0,2},{1,3},{2,0},{3,1},{4,6},{5,7},{6,4},{7,5},{8,10},{9,11},{10,... | collective-permute-start | bytes 7077896 | tf_op jit(solution)/shard_map/ppermute | solution.py:67
  480.7 50.0 %collective-permute-start.60 = (f32[2,2,4,48,384]{4,3,2,1,0:T(8,128)}, f32[2,2,4,48,384]{4,3,2,1,0:T(8,128)S(1)}, u32[]{:S(2)}, u32[]{:S(2)}) collective-permute-start(f32[2,2,4,48,384]{4,3,2,1,0:T(8,128)} %get-tuple-element.177), channel_id=1, source_target_pairs={{0,2},{1,3},{2,0},{3,1},{4,6},{5,7},{6,4},{7,5},{8,10},{9,11},{10,... | collective-permute-start | bytes 3538952 | tf_op jit(solution)/shard_map/ppermute | solution.py:67
  480.8 50.3 %collective-permute-start.42 = (f32[2,2,4,48,384]{4,3,2,1,0:T(8,128)}, f32[2,2,4,48,384]{4,3,2,1,0:T(8,128)S(1)}, u32[]{:S(2)}, u32[]{:S(2)}) collective-permute-start(f32[2,2,4,48,384]{4,3,2,1,0:T(8,128)} %get-tuple-element.170), channel_id=1, source_target_pairs={{0,2},{1,3},{2,0},{3,1},{4,6},{5,7},{6,4},{7,5},{8,10},{9,11},{10,... | collective-permute-start | bytes 3538952 | tf_op jit(solution)/shard_map/ppermute | solution.py:67
  483.3 136.2 %collective-permute-start.78 = (f32[2,2,4,48,1536]{4,3,2,1,0:T(8,128)}, f32[2,2,4,48,1536]{4,3,2,1,0:T(8,128)}, u32[]{:S(2)}, u32[]{:S(2)}) collective-permute-start(f32[2,2,4,48,1536]{4,3,2,1,0:T(8,128)} %get-tuple-element.184), channel_id=1, source_target_pairs={{0,2},{1,3},{2,0},{3,1},{4,6},{5,7},{6,4},{7,5},{8,10},{9,11},{10,... | collective-permute-start | bytes 14155784 | tf_op jit(solution)/shard_map/ppermute | solution.py:67
  519.1 17.0 %collective-permute-start.54 = (f32[2,2,4,48,384]{4,3,2,1,0:T(8,128)}, f32[2,2,4,48,384]{4,3,2,1,0:T(8,128)S(1)}, u32[]{:S(2)}, u32[]{:S(2)}) collective-permute-start(f32[2,2,4,48,384]{4,3,2,1,0:T(8,128)} %get-tuple-element.175), channel_id=1, source_target_pairs={{0,2},{1,3},{2,0},{3,1},{4,6},{5,7},{6,4},{7,5},{8,10},{9,11},{10,... | collective-permute-start | bytes 3538952 | tf_op jit(solution)/shard_map/ppermute | solution.py:67
  530.8 103.4 %collective-permute-start.72 = (f32[2,2,4,48,1536]{4,3,2,1,0:T(8,128)}, f32[2,2,4,48,1536]{4,3,2,1,0:T(8,128)}, u32[]{:S(2)}, u32[]{:S(2)}) collective-permute-start(f32[2,2,4,48,1536]{4,3,2,1,0:T(8,128)} %get-tuple-element.182), channel_id=1, source_target_pairs={{0,2},{1,3},{2,0},{3,1},{4,6},{5,7},{6,4},{7,5},{8,10},{9,11},{10,... | collective-permute-start | bytes 14155784 | tf_op jit(solution)/shard_map/ppermute | solution.py:67
  542.7 23.9 %collective-permute-start.62 = (f16[4,48,384]{2,1,0:T(8,128)(2,1)}, f16[4,48,384]{2,1,0:T(8,128)(2,1)}, u32[]{:S(2)}, u32[]{:S(2)}) collective-permute-start(f16[4,48,384]{2,1,0:T(8,128)(2,1)} %fusion.91), channel_id=1, source_target_pairs={{0,1},{1,0},{2,3},{3,2},{4,5},{5,4},{6,7},{7,6},{8,9},{9,8},{10,11... | collective-permute-start | bytes 442376 | tf_op jit(solution)/shard_map/ppermute | solution.py:67
  544.5 69.4 %all-to-all-start.5 = ((bf16[32,40,768]{2,1,0:T(8,128)(2,1)}), bf16[32,40,768]{2,1,0:T(8,128)(2,1)}, u32[]{:S(2)}, u32[]{:S(2)}) async-start(bf16[32,40,768]{2,1,0:T(8,128)(2,1)} %bitcast.377), calls=%async_computation.5 | async-start | bytes 3932160 | tf_op jit(solution)/shard_map/all_to_all | solution.py:382
  548.0 16.0 %collective-permute-start.44 = (f16[4,48,384]{2,1,0:T(8,128)(2,1)}, f16[4,48,384]{2,1,0:T(8,128)(2,1)S(1)}, u32[]{:S(2)}, u32[]{:S(2)}) collective-permute-start(f16[4,48,384]{2,1,0:T(8,128)(2,1)} %fusion.88), channel_id=1, source_target_pairs={{0,4},{1,5},{2,6},{3,7},{4,0},{5,1},{6,2},{7,3},{8,12},{9,13},{10,... | collective-permute-start | bytes 442376 | tf_op jit(solution)/shard_map/ppermute | solution.py:67
  551.2 17.4 %collective-permute-start.50 = (f16[4,48,384]{2,1,0:T(8,128)(2,1)S(1)}, f16[4,48,384]{2,1,0:T(8,128)(2,1)S(1)}, u32[]{:S(2)}, u32[]{:S(2)}) collective-permute-start(f16[4,48,384]{2,1,0:T(8,128)(2,1)S(1)} %fusion.89), channel_id=1, source_target_pairs={{0,1},{1,0},{2,3},{3,2},{4,5},{5,4},{6,7},{7,6},{8,9},{9,8},{10,11... | collective-permute-start | bytes 442376 | tf_op jit(solution)/shard_map/ppermute | solution.py:67
  566.7 18.9 %collective-permute-start.45 = (f16[48,384]{1,0:T(8,128)(2,1)S(1)}, f16[48,384]{1,0:T(8,128)(2,1)S(1)}, u32[]{:S(2)}, u32[]{:S(2)}) collective-permute-start(f16[48,384]{1,0:T(8,128)(2,1)S(1)} %get-tuple-element.386), channel_id=1, source_target_pairs={{0,8},{1,9},{2,10},{3,11},{4,12},{5,13},{6,14},{7,15},{8,16},{9,17... | collective-permute-start | bytes 110600 | tf_op jit(solution)/shard_map/ppermute | solution.py:67
  568.7 28.6 %collective-permute-start.46 = (f16[48,384]{1,0:T(8,128)(2,1)S(1)}, f16[48,384]{1,0:T(8,128)(2,1)S(1)}, u32[]{:S(2)}, u32[]{:S(2)}) collective-permute-start(f16[48,384]{1,0:T(8,128)(2,1)S(1)} %get-tuple-element.388), channel_id=1, source_target_pairs={{0,16},{1,17},{2,18},{3,19},{4,20},{5,21},{6,22},{7,23},{8,24},{9,... | collective-permute-start | bytes 110600 | tf_op jit(solution)/shard_map/ppermute | solution.py:67
  573.8 23.5 %collective-permute-start.47 = (f16[48,384]{1,0:T(8,128)(2,1)S(1)}, f16[48,384]{1,0:T(8,128)(2,1)S(1)}, u32[]{:S(2)}, u32[]{:S(2)}) collective-permute-start(f16[48,384]{1,0:T(8,128)(2,1)S(1)} %get-tuple-element.387), channel_id=1, source_target_pairs={{0,24},{1,25},{2,26},{3,27},{4,28},{5,29},{6,30},{7,31},{8,0},{9,1... | collective-permute-start | bytes 110600 | tf_op jit(solution)/shard_map/ppermute | solution.py:67
  611.8 27.7 %collective-permute-start.66 = (f32[2,2,4,48,1536]{4,3,2,1,0:T(8,128)}, f32[2,2,4,48,1536]{4,3,2,1,0:T(8,128)}, u32[]{:S(2)}, u32[]{:S(2)}) collective-permute-start(f32[2,2,4,48,1536]{4,3,2,1,0:T(8,128)} %get-tuple-element.179), channel_id=1, source_target_pairs={{0,2},{1,3},{2,0},{3,1},{4,6},{5,7},{6,4},{7,5},{8,10},{9,11},{10,... | collective-permute-start | bytes 14155784 | tf_op jit(solution)/shard_map/ppermute | solution.py:67
  626.1 29.1 %collective-permute-start.79 = (f16[2,4,48,1536]{3,2,1,0:T(8,128)(2,1)}, f16[2,4,48,1536]{3,2,1,0:T(8,128)(2,1)S(1)}, u32[]{:S(2)}, u32[]{:S(2)}) collective-permute-start(f16[2,4,48,1536]{3,2,1,0:T(8,128)(2,1)} %fusion.35), channel_id=1, source_target_pairs={{0,4},{1,5},{2,6},{3,7},{4,0},{5,1},{6,2},{7,3},{8,12},{9,13},{10,... | collective-permute-start | bytes 3538952 | tf_op jit(solution)/shard_map/ppermute | solution.py:67
  639.4 40.0 %collective-permute-start.73 = (f16[2,4,48,1536]{3,2,1,0:T(8,128)(2,1)S(1)}, f16[2,4,48,1536]{3,2,1,0:T(8,128)(2,1)S(1)}, u32[]{:S(2)}, u32[]{:S(2)}) collective-permute-start(f16[2,4,48,1536]{3,2,1,0:T(8,128)(2,1)S(1)} %fusion.34), channel_id=1, source_target_pairs={{0,4},{1,5},{2,6},{3,7},{4,0},{5,1},{6,2},{7,3},{8,12},{9,13},{10,... | collective-permute-start | bytes 3538952 | tf_op jit(solution)/shard_map/ppermute | solution.py:67
  643.0 39.1 %collective-permute-start.67 = (f16[2,4,48,1536]{3,2,1,0:T(8,128)(2,1)S(1)}, f16[2,4,48,1536]{3,2,1,0:T(8,128)(2,1)S(1)}, u32[]{:S(2)}, u32[]{:S(2)}) collective-permute-start(f16[2,4,48,1536]{3,2,1,0:T(8,128)(2,1)S(1)} %fusion.33), channel_id=1, source_target_pairs={{0,1},{1,0},{2,3},{3,2},{4,5},{5,4},{6,7},{7,6},{8,9},{9,8},{10,11... | collective-permute-start | bytes 3538952 | tf_op jit(solution)/shard_map/ppermute | solution.py:67
  655.7 28.9 %collective-permute-start.80 = (f16[4,48,1536]{2,1,0:T(8,128)(2,1)S(1)}, f16[4,48,1536]{2,1,0:T(8,128)(2,1)S(1)}, u32[]{:S(2)}, u32[]{:S(2)}) collective-permute-start(f16[4,48,1536]{2,1,0:T(8,128)(2,1)S(1)} %fusion.45), channel_id=1, source_target_pairs={{0,1},{1,0},{2,3},{3,2},{4,5},{5,4},{6,7},{7,6},{8,9},{9,8},{10,11... | collective-permute-start | bytes 1769480 | tf_op jit(solution)/shard_map/ppermute | solution.py:67
  679.9 16.9 %collective-permute-start.74 = (f16[4,48,1536]{2,1,0:T(8,128)(2,1)S(1)}, f16[4,48,1536]{2,1,0:T(8,128)(2,1)S(1)}, u32[]{:S(2)}, u32[]{:S(2)}) collective-permute-start(f16[4,48,1536]{2,1,0:T(8,128)(2,1)S(1)} %fusion.44), channel_id=1, source_target_pairs={{0,1},{1,0},{2,3},{3,2},{4,5},{5,4},{6,7},{7,6},{8,9},{9,8},{10,11... | collective-permute-start | bytes 1769480 | tf_op jit(solution)/shard_map/ppermute | solution.py:67
  685.6 40.7 %collective-permute-start.81 = (f16[48,1536]{1,0:T(8,128)(2,1)}, f16[48,1536]{1,0:T(8,128)(2,1)S(1)}, u32[]{:S(2)}, u32[]{:S(2)}) collective-permute-start(f16[48,1536]{1,0:T(8,128)(2,1)} %get-tuple-element.354), channel_id=1, source_target_pairs={{0,8},{1,9},{2,10},{3,11},{4,12},{5,13},{6,14},{7,15},{8,16},{9,17... | collective-permute-start | bytes 442376 | tf_op jit(solution)/shard_map/ppermute | solution.py:67
  686.7 39.6 %collective-permute-start.82 = (f16[48,1536]{1,0:T(8,128)(2,1)}, f16[48,1536]{1,0:T(8,128)(2,1)S(1)}, u32[]{:S(2)}, u32[]{:S(2)}) collective-permute-start(f16[48,1536]{1,0:T(8,128)(2,1)} %get-tuple-element.356), channel_id=1, source_target_pairs={{0,16},{1,17},{2,18},{3,19},{4,20},{5,21},{6,22},{7,23},{8,24},{9,... | collective-permute-start | bytes 442376 | tf_op jit(solution)/shard_map/ppermute | solution.py:67
  (94 other events, 804.4 us)

commit v2 on v1

--- a/solution.py
+++ b/solution.py
@@ -70,18 +70,15 @@
         dp_index = (place["z"] * self.nx + place["x"]) * self.nc + place["c"]
         return dp_index * self.tensor + place["y"]
 
-    def gather(self, values, order):
-        if not self.stepped:
-            whole = lax.all_gather(values, ("tensor", "dp"), axis=0, tiled=True)
-            shape = (self.tensor, 1) if order == "yx" else (1, self.tensor)
-            return whole.reshape((1,) + shape + (1, self.rows, values.shape[1]))
-        stack = values
-        for axis in ("z",) + tuple(reversed(order)) + ("c",):
-            parts = [stack]
-            for far in range(1, self.size(axis)):
-                parts.append(self.shift(stack, axis, -far))
-            stack = jnp.stack(parts)
-        return stack
+    def gather_whole(self, values):
+        whole = lax.all_gather(values, ("tensor", "dp"), axis=0, tiled=True)
+        return whole.reshape(self.tensor, -1, values.shape[1])
+
+    def gathered_shape(self, shard):
+        rows, columns = shard.shape
+        return jax.ShapeDtypeStruct(
+            (self.tensor, self.nz, self.nx, self.nc, rows, columns), shard.dtype
+        )
 
     def scatter(self, parts, order, scale):
         if not self.stepped:
@@ -100,16 +97,12 @@
         return total
 
 
-    def weight_spec(self, order, columns, locate):
+    def weight_spec(self, width, columns, locate):
         def index(i, place):
             part, column = locate(i)
-            far = lax.rem(part - place[3] + self.tensor, self.tensor)
-            if order == "yx":
-                return (0, far, 0, 0, 0, column)
-            return (0, 0, far, 0, 0, column)
-
-        middle = (None, self.nx) if order == "yx" else (self.nx, None)
-        return pl.BlockSpec((self.nc,) + middle + (self.nz, self.rows, columns), index)
+            return (part, 0, column)
+
+        return pl.BlockSpec((None, width, columns), index)
 
     def grad_specs(self, order, columns, locate):
         def index(i, place):
@@ -127,19 +120,6 @@
         middle = (self.tensor, self.nx) if order == "yx" else (self.nx, self.tensor)
         shape = middle + (self.nz, self.rows, columns)
         return [jax.ShapeDtypeStruct(shape, F32)] * self.nc
-
-    def assemble(self, place, block, target, first_column):
-        columns = block.shape[-1]
-        for z in range(self.nz):
-            far_z = lax.rem(z - place[0] + self.nz, self.nz)
-            for x in range(self.nx):
-                far_x = lax.rem(x - place[1] + self.nx, self.nx)
-                for c in range(self.nc):
-                    far_c = lax.rem(c - place[2] + self.nc, self.nc)
-                    start = ((z * self.nx + x) * self.nc + c) * self.rows
-                    target[start : start + self.rows, first_column : first_column + columns] = (
-                        block[far_c, far_x, far_z]
-                    )
 
     def disperse(self, place, source, first_column, targets):
         columns = targets[0].shape[-1]
@@ -230,107 +210,345 @@
     return pl.BlockSpec(shape, lambda i, place: zeros)
 
 
-def exchange_partner(me, step):
-    distance = 1 << step
-    return me + distance - 2 * distance * lax.rem(me // distance, 2)
-
-
-def exchange_barrier(me, steps, tensor):
+def own_index(tensor):
+    return lax.axis_index("dp") * tensor + lax.axis_index("tensor")
+
+
+def device_at(index, tensor):
+    return (index // tensor, lax.rem(index, tensor))
+
+
+def greet_all(me, count, tensor):
     barrier = pltpu.get_barrier_semaphore()
-    for step in range(steps):
-        partner = exchange_partner(me, step)
+
+    def greet(far, carry):
         pl.semaphore_signal(
             barrier,
             inc=1,
-            device_id=(partner // tensor, lax.rem(partner, tensor)),
+            device_id=device_at(lax.rem(me + far, count), tensor),
             device_id_type=pl.DeviceIdType.MESH,
         )
-    pl.semaphore_wait(barrier, steps)
-
-
-def exchange_blocks(me, steps, tensor, held, send_sem, recv_sem):
-    for step in range(steps):
-        partner = exchange_partner(me, step)
-        size = 1 << step
-        base = (me // size) * size
+        return carry
+
+    lax.fori_loop(1, count, greet, 0)
+    pl.semaphore_wait(barrier, count - 1)
+
+
+def for_all(me, count, tensor, source, target, send_sem, recv_sem, start):
+    def act(far, carry):
+        peer = lax.rem(me + far, count)
         copy = pltpu.make_async_remote_copy(
-            src_ref=held.at[pl.ds(base, size)],
-            dst_ref=held.at[pl.ds(base, size)],
-            send_sem=send_sem.at[step],
-            recv_sem=recv_sem.at[step],
-            device_id=(partner // tensor, lax.rem(partner, tensor)),
+            src_ref=source(peer),
+            dst_ref=target,
+            send_sem=send_sem.at[far - 1],
+            recv_sem=recv_sem.at[far - 1],
+            device_id=device_at(peer, tensor),
             device_id_type=pl.DeviceIdType.MESH,
         )
-        copy.start()
-        copy.wait()
-
-
-def share_kernel(steps, tensor, block_ref, out_ref, held, send_sem, recv_sem):
-    me = lax.axis_index("dp") * tensor + lax.axis_index("tensor")
-    exchange_barrier(me, steps, tensor)
-    held[pl.ds(me, 1)] = block_ref[...][None]
-    exchange_blocks(me, steps, tensor, held, send_sem, recv_sem)
+        if start:
+            copy.start()
+        else:
+            copy.wait()
+        return carry
+
+    lax.fori_loop(1, count, act, 0)
+
+
+def swap_blocks_kernel(tensor, block_ref, out_ref, held, send_sem, recv_sem):
+    count = held.shape[0]
+    me = own_index(tensor)
+    greet_all(me, count, tensor)
+    for start in (True, False):
+        for_all(
+            me,
+            count,
+            tensor,
+            lambda peer: block_ref.at[peer],
+            held.at[me],
+            send_sem,
+            recv_sem,
+            start,
+        )
+        if start:
+            held[pl.ds(me, 1)] = block_ref[pl.ds(me, 1)]
     out_ref[...] = held[...]
 
 
-def share(plan, block):
-    steps = plan.count.bit_length() - 1
-    shape = (plan.count,) + block.shape
+def in_vmem():
+    return pl.BlockSpec(memory_space=pltpu.VMEM)
+
+
+def in_place():
+    return pl.BlockSpec(memory_space=pl.ANY)
+
+
+def swap_blocks(plan, blocks):
     return pl.pallas_call(
-        functools.partial(share_kernel, steps, plan.tensor),
-        name="share",
-        out_shape=jax.ShapeDtypeStruct(shape, block.dtype),
-        in_specs=[pl.BlockSpec(memory_space=pltpu.VMEM)],
-        out_specs=pl.BlockSpec(memory_space=pltpu.VMEM),
+        functools.partial(swap_blocks_kernel, plan.tensor),
+        name="swap_blocks",
+        out_shape=jax.ShapeDtypeStruct(blocks.shape, blocks.dtype),
+        in_specs=[in_vmem()],
+        out_specs=in_vmem(),
         scratch_shapes=[
-            pltpu.VMEM(shape, block.dtype),
-            pltpu.SemaphoreType.DMA((steps,)),
-            pltpu.SemaphoreType.DMA((steps,)),
+            pltpu.VMEM(blocks.shape, blocks.dtype),
+            pltpu.SemaphoreType.DMA((plan.count - 1,)),
+            pltpu.SemaphoreType.DMA((plan.count - 1,)),
         ],
         compiler_params=params(collective_id=0, has_side_effects=True),
+    )(blocks)
+
+
+def largest_sum_kernel(count, tensor, block_ref, out_ref, held, send_sem, recv_sem):
+    me = own_index(tensor)
+    greet_all(me, count, tensor)
+    for start in (True, False):
+        for_all(
+            me, count, tensor, lambda peer: block_ref, held.at[me], send_sem, recv_sem, start
+        )
+        if start:
+            held[pl.ds(me, 1)] = block_ref[...][None]
+    out_ref[...] = jnp.sum(held[...], axis=0)
+
+
+def largest_sum(plan, block):
+    return pl.pallas_call(
+        functools.partial(largest_sum_kernel, plan.count, plan.tensor),
+        name="largest_sum",
+        out_shape=jax.ShapeDtypeStruct(block.shape, block.dtype),
+        in_specs=[in_vmem()],
+        out_specs=in_vmem(),
+        scratch_shapes=[
+            pltpu.VMEM((plan.count,) + block.shape, block.dtype),
+            pltpu.SemaphoreType.DMA((plan.count - 1,)),
+            pltpu.SemaphoreType.DMA((plan.count - 1,)),
+        ],
+        compiler_params=params(collective_id=3, has_side_effects=True),
     )(block)
 
 
-def total_kernel(steps, tensor, block_ref, out_ref, held, came, send_sem, recv_sem):
-    me = lax.axis_index("dp") * tensor + lax.axis_index("tensor")
-    exchange_barrier(me, steps, tensor)
-    held[0] = block_ref[...]
-    for step in range(steps):
-        partner = exchange_partner(me, step)
-        copy = pltpu.make_async_remote_copy(
-            src_ref=held.at[step],
-            dst_ref=came.at[step],
-            send_sem=send_sem.at[step],
-            recv_sem=recv_sem.at[step],
-            device_id=(partner // tensor, lax.rem(partner, tensor)),
+def total_kernel(
+    tensor, block_ref, out_ref, came, held, own, send_sem, recv_sem, late_send, late_recv
+):
+    count = held.shape[0]
+    me = own_index(tensor)
+    greet_all(me, count, tensor)
+    for start in (True, False):
+        for_all(
+            me,
+            count,
+            tensor,
+            lambda peer: block_ref.at[peer],
+            came.at[me],
+            send_sem,
+            recv_sem,
+            start,
+        )
+        if start:
+            came[pl.ds(me, 1)] = block_ref[pl.ds(me, 1)]
+    summed = jnp.sum(came[...], axis=0)
+    own[...] = summed
+    for start in (True, False):
+        for_all(me, count, tensor, lambda peer: own, held.at[me], late_send, late_recv, start)
+        if start:
+            held[pl.ds(me, 1)] = summed[None]
+    out_ref[...] = held[...]
+
+
+def total(plan, values, scalar):
+    count = plan.count
+    part = -(-values.shape[0] // count)
+    padded = jnp.pad(values, (0, part * count - values.shape[0])).reshape(count, part)
+    tail = jnp.full((count, 8 * LANES - part), scalar, values.dtype)
+    blocks = jnp.concatenate([padded, tail], axis=1).reshape(count, 8, LANES)
+    sums = pl.pallas_call(
+        functools.partial(total_kernel, plan.tensor),
+        name="total",
+        out_shape=jax.ShapeDtypeStruct(blocks.shape, blocks.dtype),
+        in_specs=[in_vmem()],
+        out_specs=in_vmem(),
+        scratch_shapes=[
+            pltpu.VMEM(blocks.shape, blocks.dtype),
+            pltpu.VMEM(blocks.shape, blocks.dtype),
+            pltpu.VMEM(blocks.shape[1:], blocks.dtype),
+        ]
+        + [pltpu.SemaphoreType.DMA((count - 1,))] * 4,
+        compiler_params=params(collective_id=1, has_side_effects=True),
+    )(blocks).reshape(count, 8 * LANES)
+    return sums[:, :part].reshape(-1)[: values.shape[0]], sums[0, part]
+
+
+class Transport:
+    def __init__(self, plan, shard, out, at, order, send_sem, recv_sem):
+        self.plan, self.shard, self.out, self.at, self.order = plan, shard, out, at, order
+        self.send_sem, self.recv_sem = send_sem, recv_sem
+        self.dp_index, self.y = lax.axis_index("dp"), lax.axis_index("tensor")
+        self.c = lax.rem(self.dp_index, plan.nc)
+        self.x = lax.rem(self.dp_index // plan.nc, plan.nx)
+        self.z = self.dp_index // (plan.nc * plan.nx)
+
+    def device(self, z, x, c, y):
+        return ((z * self.plan.nx + x) * self.plan.nc + c, y)
+
+    def copies(self, stage):
+        plan = self.plan
+        z, x, c, y = self.z, self.x, self.c, self.y
+        if stage == 0:
+            target = self.out.at[y, z, x, c, self.at]
+            return [
+                pltpu.make_async_remote_copy(
+                    src_ref=self.shard.at[self.at],
+                    dst_ref=target,
+                    send_sem=self.send_sem.at[far - 1],
+                    recv_sem=self.recv_sem.at[far - 1],
+                    device_id=self.device(lax.rem(z + far, plan.nz), x, c, y),
+                    device_id_type=pl.DeviceIdType.MESH,
+                )
+                for far in range(1, plan.nz)
+            ]
+        path = self.order + ("c",)
+        done = path[: stage - 1]
+        axis = path[stage - 1]
+        every = slice(None)
+        block = self.out.at[
+            every if "y" in done else y,
+            every,
+            every if "x" in done else x,
+            every if "c" in done else c,
+            self.at,
+        ]
+        device = {
+            "x": self.device(z, 1 - x, c, y),
+            "y": self.device(z, x, c, 1 - y),
+            "c": self.device(z, x, 1 - c, y),
+        }[axis]
+        slot = plan.nz - 2 + stage
+        return [
+            pltpu.make_async_remote_copy(
+                src_ref=block,
+                dst_ref=block,
+                send_sem=self.send_sem.at[slot],
+                recv_sem=self.recv_sem.at[slot],
+                device_id=device,
+                device_id_type=pl.DeviceIdType.MESH,
+            )
+        ]
+
+    def own(self):
+        slot = self.plan.nz + 2
+        return pltpu.make_async_copy(
+            self.shard.at[self.at],
+            self.out.at[self.y, self.z, self.x, self.c, self.at],
+            self.send_sem.at[slot],
+        )
+
+    def advance(self, stage):
+        if stage == 0:
+            self.own().start()
+        elif stage == 1:
+            self.own().wait()
+        if stage > 0:
+            for copy in self.copies(stage - 1):
+                copy.wait_recv()
+        if stage < 4:
+            for copy in self.copies(stage):
+                copy.start()
+        else:
+            for earlier in range(4):
+                for copy in self.copies(earlier):
+                    copy.wait_send()
+
+
+def greet_neighbours(plan):
+    dp_index, y = lax.axis_index("dp"), lax.axis_index("tensor")
+    c = lax.rem(dp_index, plan.nc)
+    x = lax.rem(dp_index // plan.nc, plan.nx)
+    z = dp_index // (plan.nc * plan.nx)
+    places = [(lax.rem(z + far, plan.nz), x, c, y) for far in range(1, plan.nz)]
+    places += [(z, 1 - x, c, y), (z, x, c, 1 - y), (z, x, 1 - c, y)]
+    barrier = pltpu.get_barrier_semaphore()
+    for to_z, to_x, to_c, to_y in places:
+        pl.semaphore_signal(
+            barrier,
+            inc=1,
+            device_id=((to_z * plan.nx + to_x) * plan.nc + to_c, to_y),
             device_id_type=pl.DeviceIdType.MESH,
         )
-        copy.start()
-        copy.wait()
-        held[step + 1] = held[step] + came[step]
-    out_ref[...] = held[steps]
-
-
-def total(plan, block, collective_id):
-    steps = plan.count.bit_length() - 1
-    return pl.pallas_call(
-        functools.partial(total_kernel, steps, plan.tensor),
-        name="total",
-        out_shape=jax.ShapeDtypeStruct(block.shape, block.dtype),
-        in_specs=[pl.BlockSpec(memory_space=pltpu.VMEM)],
-        out_specs=pl.BlockSpec(memory_space=pltpu.VMEM),
+    pl.semaphore_wait(barrier, len(places))
+
+
+def transport_slots(plan):
+    return plan.nz + 3
+
+
+def fetch_kernel(plan, orders, rows_ref, *refs):
+    number = len(orders)
+    shards, came = refs[:number], refs[number]
+    outs = refs[number + 1 : 2 * number + 1]
+    send_sem, recv_sem, own_sem, weight_send, weight_recv = refs[2 * number + 1 :]
+    count, tensor = plan.count, plan.tensor
+    me = own_index(tensor)
+    greet_all(me, count, tensor)
+    units = [
+        Transport(
+            plan,
+            shards[n],
+            outs[n],
+            slice(None),
+            orders[n],
+            weight_send.at[n],
+            weight_recv.at[n],
+        )
+        for n in range(number)
+    ]
+    for unit in units:
+        unit.advance(0)
+    own = pltpu.make_async_copy(rows_ref.at[me], came.at[me], own_sem)
+    own.start()
+
+    def rows(start):
+        for_all(
+            me,
+            count,
+            tensor,
+            lambda peer: rows_ref.at[peer],
+            came.at[me],
+            send_sem,
+            recv_sem,
+            start,
+        )
+
+    rows(True)
+    for stage in range(1, 5):
+        for unit in units:
+            unit.advance(stage)
+    own.wait()
+    rows(False)
+
+
+def fetch(plan, rows, shards, orders):
+    number = len(shards)
+    slots = transport_slots(plan)
+    outs = pl.pallas_call(
+        functools.partial(fetch_kernel, plan, orders),
+        name="fetch",
+        out_shape=[jax.ShapeDtypeStruct(rows.shape, rows.dtype)]
+        + [plan.gathered_shape(shard) for shard in shards],
+        in_specs=[in_place()] * (1 + number),
+        out_specs=[in_place()] * (1 + number),
         scratch_shapes=[
-            pltpu.VMEM((steps + 1,) + block.shape, block.dtype),
-            pltpu.VMEM((steps,) + block.shape, block.dtype),
-            pltpu.SemaphoreType.DMA((steps,)),
-            pltpu.SemaphoreType.DMA((steps,)),
+            pltpu.SemaphoreType.DMA((plan.count - 1,)),
+            pltpu.SemaphoreType.DMA((plan.count - 1,)),
+            pltpu.SemaphoreType.DMA(()),
+            pltpu.SemaphoreType.DMA((number, slots)),
+            pltpu.SemaphoreType.DMA((number, slots)),
         ],
-        compiler_params=params(collective_id=collective_id, has_side_effects=True),
-    )(block)
+        compiler_params=params(collective_id=4, has_side_effects=True),
+    )(rows, *shards)
+    return outs[0], [w.reshape(plan.tensor, -1, w.shape[-1]) for w in outs[1:]]
 
 
 def wire_scale(plan, peak):
-    bound = total(plan, peak, 3)[0, 0]
+    bound = largest_sum(plan, peak)[0, 0]
     exponent = jnp.floor(jnp.log2(32768.0 / jnp.maximum(bound, 1e-30)))
     return jnp.exp2(jnp.clip(exponent, -60.0, 60.0))
 
@@ -382,14 +600,100 @@
     return lax.all_to_all(parts, AXES, 0, 0, tiled=True).reshape(rows.shape)
 
 
-def attend_kernel(plan, place, x, wq, wk, wv, cosine, sine, q, k, v, mixed, log_total, weights):
-    rows = x.shape[0]
-    plan.assemble(place, wq, weights, 0)
-    plan.assemble(place, wk, weights, LANES)
-    plan.assemble(place, wv, weights, 2 * LANES)
+def transport_units(plan, shards, outs, send_sem, recv_sem):
+    units = []
+    for n in range(len(shards)):
+        rows = shards[n].shape[0]
+        cut = 16 * (rows // 16 * 2 // 3)
+        orders = (("x", "y"), ("y", "x")) if n % 2 == 0 else (("y", "x"), ("x", "y"))
+        ranges = ((0, cut), (cut, rows - cut))
+        for (start, size), order in zip(ranges, orders):
+            number = len(units)
+            units.append(
+                Transport(
+                    plan,
+                    shards[n],
+                    outs[n],
+                    pl.ds(start, size),
+                    order,
+                    send_sem.at[number],
+                    recv_sem.at[number],
+                )
+            )
+    return units
+
+
+SLOTS_PER_STEP = 2
+TRANSPORT_SLOTS = {
+    3: ((0, 1),),
+    4: ((1, 1),),
+    6: ((2, 1), (0, 2), (1, 2)),
+    7: ((3, 1),),
+    8: ((2, 2),),
+    9: ((3, 2), (0, 3), (1, 3)),
+    10: ((4, 1),),
+    11: ((5, 1), (2, 3)),
+}
+TRANSPORT_END = (
+    (4, 2),
+    (5, 2),
+    (3, 3),
+    (4, 3),
+    (5, 3),
+    (0, 4),
+    (1, 4),
+    (2, 4),
+    (3, 4),
+    (4, 4),
+    (5, 4),
+)
+
+
+def attend_kernel(plan, number, place, *refs):
+    (embedded, wq, wk, wv, wo, cosine, sine, norms) = refs[:8]
+    shards = refs[8 : 8 + number]
+    (q, k, v, mixed_out, log_total, low_one, normal_one, inverse_one) = refs[8 + number : 16 + number]
+    (low_two, normal_two, inverse_two) = refs[16 + number : 19 + number]
+    gathered = refs[19 + number : 19 + 2 * number]
+    scratch = refs[19 + 2 * number :]
+    weights, mixed = scratch[:2]
+    rows = embedded.shape[0]
+    step = pl.program_id(0)
+    if number:
+        units = transport_units(plan, shards, gathered, *scratch[2:4])
+
+        @pl.when(step == 0)
+        def _():
+            greet_neighbours(plan)
+            for unit in units:
+                unit.advance(0)
+
+    def transport(part):
+        if number:
+            for slot, events in TRANSPORT_SLOTS.items():
+                if slot % SLOTS_PER_STEP == part:
+
+                    @pl.when(step == slot // SLOTS_PER_STEP)
+                    def _():
+                        for unit, stage in events:
+                            units[unit].advance(stage)
+
+    @pl.when(step == 0)
+    def _():
+        for start in range(0, rows, ROW_BLOCK):
+            at = slice(start, start + ROW_BLOCK)
+            normal, inverse = normalize(embedded[at, :])
+            normal_one[at, :] = normal
+            inverse_one[at, :] = inverse
+            low_one[at, :] = (normal * norms[0:1, :] + norms[1:2, :]).astype(BF16)
+
+    transport(0)
+    weights[:, :LANES] = wq[...]
+    weights[:, LANES : 2 * LANES] = wk[...]
+    weights[:, 2 * LANES :] = wv[...]
     for start in range(0, rows, ROW_BLOCK):
         at = slice(start, start + ROW_BLOCK)
-        made = dot(x[at, :], weights[...])
+        made = dot(low_one[at, :], weights[...])
         query, key = made[:, :LANES], made[:, LANES : 2 * LANES]
         query = query * cosine[at, :] + swap_halves(query) * sine[at, :]
         key = key * cosine[at, :] + swap_halves(key) * sine[at, :]
@@ -402,6 +706,8 @@
     values = v[...].T
     for start in range(0, rows, ROW_BLOCK):
         at = slice(start, start + ROW_BLOCK)
+        if start == rows // 2:
+            transport(1)
         outs = []
         for head in range(LANES // HEAD):
             scores = dot_last(keys, of_head(q[at, :], head)) + bias
@@ -411,21 +717,55 @@
             out = dot(values[head * HEAD : (head + 1) * HEAD, :], exponent.astype(BF16))
             outs.append(out / summed)
             log_total[head : head + 1, at] = top + jnp.log(summed)
-        mixed[at, :] = jnp.concatenate(outs, axis=0).T.astype(BF16)
-
-
-def attend(plan, place, x, wq, wk, wv, cosine, sine):
-    rows, width = x.shape
+        made = jnp.concatenate(outs, axis=0).T.astype(BF16)
+        mixed_out[at, :] = made
+        mixed[step, at, :] = made
+
+    @pl.when(step == pl.num_programs(0) - 1)
+    def _():
+        per_part = wo.shape[2] // LANES
+        for start in range(0, rows, ROW_BLOCK):
+            at = slice(start, start + ROW_BLOCK)
+            product = normal_one[at, :] * norms[0:1, :] + norms[1:2, :]
+            for part in range(plan.tensor):
+                whole_mixed = jnp.concatenate(
+                    [mixed[part * per_part + n, at, :] for n in range(per_part)], axis=1
+                )
+                product = product + dot_last(whole_mixed, wo[part])
+            normal, inverse = normalize(product)
+            normal_two[at, :] = normal
+            inverse_two[at, :] = inverse
+            low_two[at, :] = (normal * norms[2:3, :] + norms[3:4, :]).astype(BF16)
+        if number:
+            for unit, stage in TRANSPORT_END:
+                units[unit].advance(stage)
+
+
+def attend(plan, place, embedded, wq, wk, wv, wo, cosine, sine, norms, shards):
+    rows, width = embedded.shape
     pairs = wq.shape[-1] // LANES
     steps = plan.tensor * pairs
+    number = len(shards)
 
     def locate(i):
         return i // pairs, lax.rem(i, pairs)
 
     by_pair = pl.BlockSpec((None, rows, LANES), lambda i, place: (i, 0, 0))
     shape = jax.ShapeDtypeStruct((steps, rows, LANES), BF16)
-    return pl.pallas_call(
-        functools.partial(attend_kernel, plan),
+    normed = [
+        jax.ShapeDtypeStruct((rows, width), BF16),
+        jax.ShapeDtypeStruct((rows, width), F32),
+        jax.ShapeDtypeStruct((rows, 1), F32),
+    ]
+    normed_specs = [result((rows, width)), result((rows, width)), result((rows, 1))]
+    scratch = [pltpu.VMEM((width, 3 * LANES), BF16), pltpu.VMEM((steps, rows, LANES), BF16)]
+    more = {}
+    if number:
+        slots = transport_slots(plan)
+        scratch += [pltpu.SemaphoreType.DMA((2 * number, slots))] * 2
+        more = dict(collective_id=5, has_side_effects=True)
+    outs = pl.pallas_call(
+        functools.partial(attend_kernel, plan, number),
         name="attend",
         out_shape=[
             shape,
@@ -433,93 +773,42 @@
             shape,
             jax.ShapeDtypeStruct((rows, steps * LANES), BF16),
             jax.ShapeDtypeStruct((steps, 8, rows), F32),
-        ],
+        ]
+        + normed
+        + normed
+        + [plan.gathered_shape(shard) for shard in shards],
         grid_spec=pltpu.PrefetchScalarGridSpec(
             num_scalar_prefetch=1,
             grid=(steps,),
-            in_specs=[
-                whole((rows, width)),
-                plan.weight_spec("yx", LANES, locate),
-                plan.weight_spec("xy", LANES, locate),
-                plan.weight_spec("yx", LANES, locate),
+            in_specs=[whole((rows, width))]
+            + [plan.weight_spec(width, LANES, locate)] * 3
+            + [
+                whole(wo.shape),
                 whole((rows, LANES)),
                 whole((rows, LANES)),
-            ],
+                whole(norms.shape),
+            ]
+            + [in_place()] * number,
             out_specs=[
                 by_pair,
                 by_pair,
                 by_pair,
                 pl.BlockSpec((rows, LANES), lambda i, place: (0, i)),
                 pl.BlockSpec((None, 8, rows), lambda i, place: (i, 0, 0)),
-            ],
-            scratch_shapes=[pltpu.VMEM((width, 3 * LANES), BF16)],
+            ]
+            + normed_specs
+            + normed_specs
+            + [in_place()] * number,
+            scratch_shapes=scratch,
         ),
-        compiler_params=params(),
+        compiler_params=params(**more),
         cost_estimate=pl.CostEstimate(
-            flops=2 * rows * width * 3 * width + 16 * rows * rows * width,
-            bytes_accessed=rows * width * 12,
+            flops=8 * rows * width * width + 16 * rows * rows * width,
+            bytes_accessed=rows * width * 30,
             transcendentals=0,
         ),
-    )(place, x, wq, wk, wv, cosine, sine)
-
-
-def project_kernel(plan, place, mixed, wo, normal_one, norms, low_out, normal_out, inverse_out, weights):
-    rows, width = mixed.shape
-    part = wo.shape[-1]
-    plan.assemble(place, wo, weights, 0)
-    first = pl.program_id(0) == 0
-
-    for start in range(0, rows, ROW_BLOCK):
-        at = slice(start, start + ROW_BLOCK)
-        product = dot_last(mixed[at, :], weights[...])
-
-        @pl.when(first)
-        def _():
-            normal_out[at, :] = product
-
-        @pl.when(jnp.logical_not(first))
-        def _():
-            normal_out[at, :] = normal_out[at, :] + product
-
-    @pl.when(pl.program_id(0) == pl.num_programs(0) - 1)
-    def _():
-        for start in range(0, rows, ROW_BLOCK):
-            at = slice(start, start + ROW_BLOCK)
-            first_out = normal_one[at, :] * norms[0:1, :] + norms[1:2, :]
-            normal, inverse = normalize(first_out + normal_out[at, :])
-            normal_out[at, :] = normal
-            inverse_out[at, :] = inverse
-            low_out[at, :] = (normal * norms[2:3, :] + norms[3:4, :]).astype(BF16)
-
-
-def project(plan, place, mixed, wo, normal_one, norms):
-    rows, width = mixed.shape
-    part = wo.shape[-1]
-    return pl.pallas_call(
-        functools.partial(project_kernel, plan),
-        name="project",
-        out_shape=[
-            jax.ShapeDtypeStruct((rows, width), BF16),
-            jax.ShapeDtypeStruct((rows, width), F32),
-            jax.ShapeDtypeStruct((rows, 1), F32),
-        ],
-        grid_spec=pltpu.PrefetchScalarGridSpec(
-            num_scalar_prefetch=1,
-            grid=(plan.tensor,),
-            in_specs=[
-                pl.BlockSpec((rows, part), lambda i, place: (0, i)),
-                plan.weight_spec("xy", part, lambda i: (i, 0)),
-                whole((rows, width)),
-                whole(norms.shape),
-            ],
-            out_specs=[result((rows, width)), result((rows, width)), result((rows, 1))],
-            scratch_shapes=[pltpu.VMEM((width, part), BF16)],
-        ),
-        compiler_params=params(),
-        cost_estimate=pl.CostEstimate(
-            flops=2 * rows * width * width, bytes_accessed=rows * width * 14, transcendentals=0
-        ),
-    )(place, mixed, wo, normal_one, norms)
+    )(place, embedded, wq, wk, wv, wo, cosine, sine, norms, *shards)
+    return outs[:11], [w.reshape(plan.tensor, -1, w.shape[-1]) for w in outs[11:]]
 
 
 def feed_kernel(
@@ -537,13 +826,8 @@
     normal_out,
     inverse_out,
     pool_out,
-    weights,
-    down,
 ):
     rows, width = x.shape
-    plan.assemble(place, wg, weights, 0)
-    plan.assemble(place, wu, weights, HIDDEN_BLOCK)
-    plan.assemble(place, wd, down, 0)
     first = pl.program_id(0) == 0
 
     @pl.when(first)
@@ -552,13 +836,12 @@
 
     for start in range(0, rows, ROW_BLOCK):
         at = slice(start, start + ROW_BLOCK)
-        made = dot(x[at, :], weights[...])
-        gate, up = made[:, :HIDDEN_BLOCK], made[:, HIDDEN_BLOCK:]
+        gate, up = dot(x[at, :], wg[...]), dot(x[at, :], wu[...])
         hidden = (gate * jax.nn.sigmoid(gate) * up).astype(BF16)
         gate_out[at, :] = gate.astype(BF16)
         up_out[at, :] = up.astype(BF16)
         hidden_out[at, :] = hidden
-        normal_out[at, :] = normal_out[at, :] + dot_last(hidden, down[...])
+        normal_out[at, :] = normal_out[at, :] + dot_last(hidden, wd[...])
 
     @pl.when(pl.program_id(0) == pl.num_programs(0) - 1)
     def _():
@@ -602,9 +885,9 @@
             grid=(steps,),
             in_specs=[
                 whole((rows, width)),
-                plan.weight_spec("yx", HIDDEN_BLOCK, locate),
-                plan.weight_spec("xy", HIDDEN_BLOCK, locate),
-                plan.weight_spec("xy", HIDDEN_BLOCK, locate),
+                plan.weight_spec(width, HIDDEN_BLOCK, locate),
+                plan.weight_spec(width, HIDDEN_BLOCK, locate),
+                plan.weight_spec(width, HIDDEN_BLOCK, locate),
                 whole((rows, width)),
                 whole(norms.shape),
             ],
@@ -616,10 +899,6 @@
                 result((rows, 1)),
                 result((1, width)),
             ],
-            scratch_shapes=[
-                pltpu.VMEM((width, 2 * HIDDEN_BLOCK), BF16),
-                pltpu.VMEM((width, HIDDEN_BLOCK), BF16),
-            ],
         ),
         compiler_params=params(),
         cost_estimate=pl.CostEstimate(
@@ -631,17 +910,20 @@
 
 
 def contrast_kernel(
-    steps, tensor, place, pool_ref, norms, scale_ref, loss_ref, grad_ref, held, send_sem, recv_sem
+    tensor, place, pool_ref, norms, scale_ref, loss_ref, grad_ref, held, own, send_sem, recv_sem
 ):
     count = held.shape[0]
-    me = lax.axis_index("dp") * tensor + lax.axis_index("tensor")
-    exchange_barrier(me, steps, tensor)
+    me = own_index(tensor)
+    greet_all(me, count, tensor)
     length = jnp.full((1, 1), place[4], jnp.int32).astype(F32)
     pooled = pool_ref[...] / length * norms[4:5, :] + norms[5:6, :]
     inverse = lax.rsqrt(jnp.sum(pooled * pooled, axis=-1, keepdims=True) + norm_epsilon)
     vector = pooled * inverse
-    held[pl.ds(me, 1)] = vector[None]
-    exchange_blocks(me, steps, tensor, held, send_sem, recv_sem)
+    own[...] = vector
+    for start in (True, False):
+        for_all(me, count, tensor, lambda peer: own, held.at[me], send_sem, recv_sem, start)
+        if start:
+            held[pl.ds(me, 1)] = vector[None]
     vectors = held[...].reshape(count, held.shape[2])
     scale = jnp.exp(scale_ref[...])
     logits = scale * lax.dot_general(
@@ -692,22 +974,21 @@
 
 
 def contrast(plan, place, pool, norms, log_scale):
-    steps = plan.count.bit_length() - 1
     width = pool.shape[1]
-    in_vmem = pl.BlockSpec(memory_space=pltpu.VMEM)
     loss, grad = pl.pallas_call(
-        functools.partial(contrast_kernel, steps, plan.tensor),
+        functools.partial(contrast_kernel, plan.tensor),
         name="contrast",
         out_shape=[
             jax.ShapeDtypeStruct((1, LANES), F32),
             jax.ShapeDtypeStruct((1, width), F32),
         ],
-        in_specs=[pl.BlockSpec(memory_space=pltpu.SMEM), in_vmem, in_vmem, in_vmem],
-        out_specs=[in_vmem, in_vmem],
+        in_specs=[pl.BlockSpec(memory_space=pltpu.SMEM)] + [in_vmem()] * 3,
+        out_specs=[in_vmem()] * 2,
         scratch_shapes=[
             pltpu.VMEM((plan.count, 1, width), F32),
-            pltpu.SemaphoreType.DMA((steps,)),
-            pltpu.SemaphoreType.DMA((steps,)),
+            pltpu.VMEM((1, width), F32),
+            pltpu.SemaphoreType.DMA((plan.count - 1,)),
+            pltpu.SemaphoreType.DMA((plan.count - 1,)),
         ],
         compiler_params=params(collective_id=2, has_side_effects=True),
     )(place, pool, norms, log_scale.reshape(1, 1))
@@ -735,7 +1016,7 @@
     up_grads = refs[13 + nc : 13 + 2 * nc]
     down_grads = refs[13 + 2 * nc : 13 + 3 * nc]
     grad_out, low_out, norm_out, peak_out = refs[13 + 3 * nc : 17 + 3 * nc]
-    low, low_turned, x_turned, weights, down, made, product = refs[17 + 3 * nc :]
+    low, low_turned, x_turned, made, product = refs[17 + 3 * nc :]
     rows, width = x.shape
 
     @pl.when(pl.program_id(0) == 0)
@@ -752,12 +1033,9 @@
             low_turned[:, at] = grad.astype(BF16).T
             x_turned[:, at] = x[at, :].T
 
-    plan.assemble(place, wg, weights, 0)
-    plan.assemble(place, wu, weights, HIDDEN_BLOCK)
-    plan.assemble(place, wd, down, 0)
     for start in range(0, rows, ROW_BLOCK):
         at = slice(start, start + ROW_BLOCK)
-        grad_hidden = dot(low[at, :], down[...])
+        grad_hidden = dot(low[at, :], wd[...])
         gate = gate_ref[at, :].astype(F32)
         up = up_ref[at, :].astype(F32)
         share_gate = jax.nn.sigmoid(gate)
@@ -765,7 +1043,11 @@
         grad_gate = grad_hidden * up * share_gate * (1.0 + gate * (1.0 - share_gate))
         made[at, :HIDDEN_BLOCK] = grad_gate.astype(BF16)
         made[at, HIDDEN_BLOCK:] = grad_up.astype(BF16)
-        grad_out[at, :] = grad_out[at, :] + dot_last(made[at, :], weights[...])
+        grad_out[at, :] = (
+            grad_out[at, :]
+            + dot_last(made[at, :HIDDEN_BLOCK], wg[...])
+            + dot_last(made[at, HIDDEN_BLOCK:], wu[...])
+        )
     product[:, : 2 * HIDDEN_BLOCK] = dot(x_turned[...], made[...])
     product[:, 2 * HIDDEN_BLOCK :] = dot(low_turned[...], hidden_ref[...])
     note_peak(peak_out, product)
@@ -837,9 +1119,9 @@
                 by_chunk,
                 by_chunk,
                 by_chunk,
-                plan.weight_spec("yx", HIDDEN_BLOCK, locate),
-                plan.weight_spec("xy", HIDDEN_BLOCK, locate),
-                plan.weight_spec("xy", HIDDEN_BLOCK, locate),
+                plan.weight_spec(width, HIDDEN_BLOCK, locate),
+                plan.weight_spec(width, HIDDEN_BLOCK, locate),
+                plan.weight_spec(width, HIDDEN_BLOCK, locate),
                 whole((rows, width)),
                 whole((rows, 1)),
                 whole((rows, width)),
@@ -859,8 +1141,6 @@
                 pltpu.VMEM((rows, width), BF16),
                 pltpu.VMEM((width, rows), BF16),
                 pltpu.VMEM((width, rows), BF16),
-                pltpu.VMEM((width, 2 * HIDDEN_BLOCK), BF16),
-                pltpu.VMEM((width, HIDDEN_BLOCK), BF16),
                 pltpu.VMEM((rows, 2 * HIDDEN_BLOCK), BF16),
                 pltpu.VMEM((width, 3 * HIDDEN_BLOCK), F32),
             ],
@@ -918,7 +1198,6 @@
         ga_turned,
         x_turned,
         weights,
-        out_weights,
         total_grad,
         gm,
         made,
@@ -936,13 +1215,12 @@
             x_turned[:, at] = x[at, :].T
             total_grad[at, :] = grad_res[at, :]
 
-    plan.assemble(place, wq, weights, 0)
-    plan.assemble(place, wk, weights, LANES)
-    plan.assemble(place, wv, weights, 2 * LANES)
-    plan.assemble(place, wo, out_weights, 0)
+    weights[:, :LANES] = wq[...]
+    weights[:, LANES : 2 * LANES] = wk[...]
+    weights[:, 2 * LANES :] = wv[...]
     for start in range(0, rows, ROW_BLOCK):
         at = slice(start, start + ROW_BLOCK)
-        gm[at, :] = dot(ga[at, :], out_weights[...]).astype(BF16)
+        gm[at, :] = dot(ga[at, :], wo[...]).astype(BF16)
     position = lax.broadcasted_iota(jnp.int32, (rows, 1), 0)
     bias = jnp.where(position < place[4], 0.0, masked_score)
     keys, values = k[...], v[...]
@@ -1057,7 +1335,7 @@
                 pl.BlockSpec((rows, LANES), lambda i, place: (0, i)),
                 pl.BlockSpec((None, 8, rows), lambda i, place: (i, 0, 0)),
             ]
-            + [plan.weight_spec(order, LANES, locate) for order in orders]
+            + [plan.weight_spec(width, LANES, locate)] * 4
             + [
                 whole((rows, LANES)),
                 whole((rows, LANES)),
@@ -1071,7 +1349,6 @@
                 pltpu.VMEM((width, rows), BF16),
                 pltpu.VMEM((width, rows), BF16),
                 pltpu.VMEM((width, 3 * LANES), BF16),
-                pltpu.VMEM((width, LANES), BF16),
                 pltpu.VMEM((rows, width), F32),
                 pltpu.VMEM((rows, LANES), BF16),
                 pltpu.VMEM((rows, 3 * LANES), BF16),
@@ -1159,29 +1436,40 @@
 
     qkv_low = qkv_weight.astype(BF16)
     gate_up_low = gate_up_weight.astype(BF16)
-    wq = plan.gather(qkv_low[:, 0], "yx")
-    wk = plan.gather(qkv_low[:, 1], "xy")
-    wv = plan.gather(qkv_low[:, 2], "yx")
-    wo = plan.gather(out_weight.astype(BF16), "xy")
-    wg = plan.gather(gate_up_low[:, 0], "yx")
-    wu = plan.gather(gate_up_low[:, 1], "xy")
-    wd = plan.gather(down_weight.astype(BF16), "xy")
+    early = [qkv_low[:, 0], qkv_low[:, 1], qkv_low[:, 2], out_weight.astype(BF16)]
+    late = [gate_up_low[:, 0], gate_up_low[:, 1], down_weight.astype(BF16)]
 
     table_low = token_table.astype(BF16)
     room = 8 * -(-(5 * rows) // (4 * plan.count * 8))
     slots = room * plan.count
     owner, row, first, token_place = token_places(slot_ids, own_length, vocab_shard)
     slot = round_slots(owner, token_place, room, 0)
-    wants = round_wants(slot, first, row, slots)
+    wants = round_wants(slot, first, row, slots).reshape(plan.count, room)
     rounds = jnp.max(token_place) // room + 1
-    note_rows = 8 * -(-(slots + LANES) // (8 * LANES))
     note = jnp.concatenate(
-        [wants, jnp.full((note_rows * LANES - slots,), rounds, jnp.int32)]
-    ).reshape(note_rows, LANES)
-    notes = share(plan, note).reshape(plan.count, note_rows * LANES)
-    asked = lax.dynamic_slice_in_dim(notes, me * room, room, axis=1)
-    rounds = jnp.max(notes[:, slots])
-    embedded = spread_rows(slot, swap_rows(plan, picked_rows(asked, table_low)))
+        [wants, jnp.broadcast_to(rounds, (plan.count, 8 * LANES - room))], axis=1
+    )
+    notes = swap_blocks(plan, note.reshape(plan.count, 8, LANES)).reshape(plan.count, 8 * LANES)
+    asked = notes[:, :room]
+    rounds = jnp.max(notes[:, room])
+    picked = picked_rows(asked, table_low)
+    if plan.stepped:
+        half = width // 2
+        folded = jnp.concatenate(
+            [
+                picked[:, :half].reshape(plan.count, room, half),
+                picked[:, half:].reshape(plan.count, room, half),
+            ],
+            axis=1,
+        )
+        came, (wq, wk, wv, wo) = fetch(
+            plan, folded, early, (("x", "y"), ("y", "x"), ("x", "y"), ("y", "x"))
+        )
+        came = jnp.concatenate([came[:, :room], came[:, room:]], axis=2).reshape(slots, width)
+    else:
+        came = swap_rows(plan, picked)
+        wq, wk, wv, wo = [plan.gather_whole(shard) for shard in early]
+    embedded = spread_rows(slot, came)
 
     def ask(turn):
         later = round_slots(owner, token_place, room, turn)
@@ -1193,12 +1481,26 @@
         return sofar + spread_rows(later, swap_rows(plan, picked_rows(later_asked, table_low)))
 
     embedded = lax.fori_loop(1, rounds, fetch_more, embedded)
-    normal_one, inverse_one = normalize(embedded)
-    first_low = (normal_one * norm_params[0] + norm_params[1]).astype(BF16)
-
     cosine, sine = rotary_tables(rows)
-    q, k, v, mixed, log_total = attend(plan, place, first_low, wq, wk, wv, cosine, sine)
-    second_low, normal_two, inverse_two = project(plan, place, mixed, wo, normal_one, norm_params)
+    made, gathered = attend(
+        plan,
+        place,
+        embedded,
+        wq,
+        wk,
+        wv,
+        wo,
+        cosine,
+        sine,
+        norm_params,
+        late if plan.stepped else [],
+    )
+    q, k, v, mixed, log_total, first_low, normal_one, inverse_one = made[:8]
+    second_low, normal_two, inverse_two = made[8:]
+    if plan.stepped:
+        wg, wu, wd = gathered
+    else:
+        wg, wu, wd = [plan.gather_whole(shard) for shard in late]
     gate, up, hidden_low, normal_three, inverse_three, pool = feed(
         plan, place, second_low, wg, wu, wd, normal_two, norm_params
     )
@@ -1279,7 +1581,7 @@
         + jnp.sum(grad_down_own * grad_down_own)
     )
     length_float = own_length.astype(F32)
-    sums = total(
+    norm_grads, square_total = total(
         plan,
         jnp.concatenate(
             [
@@ -1287,15 +1589,12 @@
                 norm_two[0:2],
                 grad_pool * pool,
                 grad_pool * length_float,
-                jnp.full((1, width), owned_squares, F32),
-                jnp.zeros((1, width), F32),
             ],
             axis=0,
-        ),
-        1,
-    )
-    norm_grads = sums[0:6]
-    square_total = sums[6, 0]
+        ).reshape(-1),
+        owned_squares,
+    )
+    norm_grads = norm_grads.reshape(norm_params.shape)
     squares = square_total + jnp.sum(norm_grads * norm_grads) + grad_log_scale * grad_log_scale
     grad_norm = jnp.sqrt(squares)
     factor = jnp.minimum(1.0, clip_limit / (grad_norm + 1e-06))

time: 788 us -> 689 us (0.87)
  Pallas kernels: 303 us -> 386 us
  waiting for transfers between devices: 158 us -> 80.2 us
  starting transfers between devices: 131 us -> 67.9 us
  other arithmetic: 120 us -> 71 us
    pallas_call x7, Pallas kernels: 141 us -> 233 us  [the longest x1 101 us: attend(): pl.pallas_call(functools.partial(attend_kernel, plan, number), name='atte...]
    ppermute x84 -> x42, waiting for transfers between devices: 158 us -> 80.2 us  [shift(): return lax.ppermute(values, AXES, pairs)]
    ppermute x84 -> x42, starting transfers between devices: 124 us -> 63.7 us  [shift(): return lax.ppermute(values, AXES, pairs)]
    another operation x30 -> x0, other arithmetic: 43.5 us -> none  [gather(): stack = jnp.stack(parts)]
  transfers between devices with their start and end apart: 86 -> 43, of which waited for: 31 -> 20; matrix products, arithmetic and copies ran while one was open for 17% -> 8% of each run, Pallas kernels for 14% -> 3%
where the time goes in v2:
time: 689 us; the launch traced here: 678 us
  Pallas kernels  386 us (56%)
  waiting for transfers between devices  80.2 us (12%)
  other arithmetic  71 us (10%)
  starting transfers between devices  67.9 us (10%)
  local copies, waits for them, and re-layouts  27.2 us (4%)
  between operations  20.2 us (3%)
  matrix products  17.3 us (3%)
  loops' own time  8.71 us (1%)
    pallas_call x1, Pallas kernels, attend(): pl.pallas_call(functools.partial(attend_kernel, plan, number), name='atte...  101 us
    ppermute x42, waiting for transfers between devices, shift(): return lax.ppermute(values, AXES, pairs)  80.2 us
    pallas_call x1, Pallas kernels, fetch(): pl.pallas_call(functools.partial(fetch_kernel, plan, orders), name='fetch...  66.1 us
    pallas_call x1, Pallas kernels, attend_back(): pl.pallas_call(functools.partial(attend_back_kernel, plan), name='attend_...  64.9 us
    ppermute x42, starting transfers between devices, shift(): return lax.ppermute(values, AXES, pairs)  63.7 us
    pallas_call x1, Pallas kernels, feed_back(): pl.pallas_call(functools.partial(feed_back_body, plan), name='feed_back',...  56.8 us
    pallas_call x1, Pallas kernels, feed(): pl.pallas_call(functools.partial(feed_kernel, plan), name='feed', out_sha...  30.7 us
    pallas_call x2, Pallas kernels, largest_sum(): pl.pallas_call(functools.partial(largest_sum_kernel, plan.count, plan.ten...  20.4 us
  transfers between devices with their start and end apart: 43, of which 20 were waited for; matrix products, arithmetic and copies ran while one was open for 8% of the time, Pallas kernels for 3%

profile of v2, /device:TPU:0, one launch (start us, length us, event | category | flops | bytes accessed | tf_op | source)
XLA Modules:
  0.0 678.1 jit_solution(10910782865901153915)
XLA Ops:
  12.3 12.2 %swap_blocks.1 = s32[32,8,128]{2,1,0:T(8,128)} custom-call(s32[32,8,128]{2,1,0:T(8,128)} %bitcast.299), custom_call_target="tpu_custom_call" | custom-call | tf_op jit(solution)/shard_map/swap_blocks/pallas_call | solution.py:286
  26.3 2.0 convert_element_type.399
  29.4 2.5 fusion.21
  35.6 66.1 %fetch.1 = (bf16[32,80,384]{2,1,0:T(8,128)(2,1)}, bf16[2,4,2,2,48,384]{5,4,3,2,1,0:T(8,128)(2,1)}, bf16[2,4,2,2,48,384]{5,4,3,2,1,0:T(8,128)(2,1)}, bf16[2,4,2,2...) custom-call(bf16[32,80,384]{2,1,0:T(8,128)(2,1)} %pad_maximum_fusion.rows_ref, ...), custom_call_target="tpu_custom_call" | custom-call | tf_op jit(solution)/shard_map/fetch/pallas_call | solution.py:531
  101.7 1.8 fusion.157
  105.9 4.1 fusion.14
  110.0 1.9 fusion.87
  111.9 1.8 pad_maximum_fusion.2
  115.0 7.8 %while.20 = (s32[]{:T(128)}, f32[1024,768]{1,0:T(8,128)}, s32[]{:T(128)}, s32[1024]{0:T(1024)S(1)}, s32[1024]{0:T(1024)S(1)}, /*index=5*/pred[1024]{0:T(1024)(12...) while((s32[]{:T(128)}, f32[1024,768]{1,0:T(8,128)}, ...), condition=%wide.region_7.8_spmd, body=%wide.region_5.7_spmd.sunk | while | flops 3910260480 | bytes 17673384 | solution.py:1483
  122.8 101.1 %attend.1 = (bf16[6,1024,128]{2,1,0:T(8,128)(2,1)}, bf16[6,1024,128]{2,1,0:T(8,128)(2,1)}, bf16[6,1024,128]{2,1,0:T(8,128)(2,1)}, bf16[1024,768]{1,0:T(8,128)(2,...) custom-call(s32[5]{0:T(128)} %stack.41.place, ...), custom_call_target="tpu_custom_call" | custom-call | flops 17716740096 | bytes 23592960 | tf_op jit(solution)/shard_map/attend/pallas_call | solution.py:767
  223.9 30.7 %feed.1 = (bf16[1024,3072]{1,0:T(8,128)(2,1)}, bf16[1024,3072]{1,0:T(8,128)(2,1)}, bf16[1024,3072]{1,0:T(8,128)(2,1)}, f32[1024,768]{1,0:T(8,128)}, f32[1024,1]{1,0:T(8,128)}, /*index=5*/f32[1,768]{1,0:T(1,128)}) custom-call(s32[5]{0:T(128)} %stack.41.place, bf16[1024,768]{1,0:T(8,128)(2,1)} %get-tuple-element.163.x.refs_1_, ...), custom_call_target="tpu_custom_call" | custom-call | flops 14495514624 | bytes 31457280 | tf_op jit(solution)/shard_map/feed/pallas_call | solution.py:872
  254.7 14.5 %contrast.1 = (f32[1,128]{1,0:T(1,128)}, f32[1,768]{1,0:T(1,128)}) custom-call(s32[5]{0:T(128)} %stack.41.place, f32[1,768]{1,0:T(1,128)} %get-tuple-element.168.pool_ref, f32[6,768]{1,0:T(8,128)} %refs_16_.1, f32[1,1]{1,0:T(1,128)} %bitcast.283.scale_ref), custom_call_target="tpu_custom_call" | custom-call | tf_op jit(solution)/shard_map/contrast/pallas_call | solution.py:978
  269.2 56.8 %feed_back.1 = (f32[2,2,4,48,1536]{4,3,2,1,0:T(8,128)}, f32[2,2,4,48,1536]{4,3,2,1,0:T(8,128)}, f32[2,2,4,48,1536]{4,3,2,1,0:T(8,128)}, f32[2,2,4,48,1536]{4,3,2...) custom-call(s32[5]{0:T(128)} %stack.41.place, ...), custom_call_target="tpu_custom_call" | custom-call | flops 28991029248 | bytes 47185920 | tf_op jit(solution)/shard_map/feed_back/pallas_call | solution.py:1101
  326.1 64.9 %attend_back.1 = (f32[2,2,4,48,384]{4,3,2,1,0:T(8,128)}, f32[2,2,4,48,384]{4,3,2,1,0:T(8,128)}, f32[2,2,4,48,384]{4,3,2,1,0:T(8,128)}, f32[2,2,4,48,384]{4,3,2,1...) custom-call(s32[5]{0:T(128)} %stack.41.place, ...), custom_call_target="tpu_custom_call" | custom-call | flops 41875931136 | bytes 23592960 | tf_op jit(solution)/shard_map/attend_back/pallas_call | solution.py:1317
  392.9 10.2 %largest_sum.3 = f32[8,128]{1,0:T(8,128)} custom-call(f32[8,128]{1,0:T(8,128)} %get-tuple-element.202.block_ref), custom_call_target="tpu_custom_call" | custom-call | tf_op jit(solution)/shard_map/largest_sum/pallas_call | solution.py:314
  405.0 10.3 %largest_sum.2 = f32[8,128]{1,0:T(8,128)} custom-call(f32[8,128]{1,0:T(8,128)} %get-tuple-element.193.block_ref), custom_call_target="tpu_custom_call" | custom-call | tf_op jit(solution)/shard_map/largest_sum/pallas_call | solution.py:314
  422.7 5.2 fusion.20
  429.6 1.9 collective-permute-start.19
  444.1 4.3 all-to-all-start.4
  453.9 10.6 %collective-permute-done.2 = f16[4,48,384]{2,1,0:T(8,128)(2,1)S(1)} collective-permute-done((f16[4,48,384]{2,1,0:T(8,128)(2,1)}, f16[4,48,384]{2,1,0:T(8,128)(2,1)S(1)}, u32[]{:S(2)}, u32[]{:S(2)}) %collective-permute-start.2) | collective-permute-done | bytes 147488 | tf_op jit(solution)/shard_map/ppermute | solution.py:67
  464.5 2.5 collective-permute-start.14
  469.2 4.6 collective-permute-start.4
  474.2 3.4 collective-permute-start.5
  477.7 8.3 %collective-permute-done.3 = f16[48,384]{1,0:T(8,128)(2,1)S(1)} collective-permute-done((f16[48,384]{1,0:T(8,128)(2,1)S(1)}, f16[48,384]{1,0:T(8,128)(2,1)S(1)}, u32[]{:S(2)}, u32[]{:S(2)}) %collective-permute-start.3) | collective-permute-done | bytes 36896 | tf_op jit(solution)/shard_map/ppermute | solution.py:67
  485.9 11.0 %collective-permute-start.10 = (f16[48,384]{1,0:T(8,128)(2,1)S(1)}, f16[48,384]{1,0:T(8,128)(2,1)S(1)}, u32[]{:S(2)}, u32[]{:S(2)}) collective-permute-start(f16[48,384]{1,0:T(8,128)(2,1)S(1)} %get-tuple-element.364), channel_id=1, source_target_pairs={{0,16},{1,17},{2,18},{3,19},{4,20},{5,21},{6,22},{7,23},{8,24},{9,... | collective-permute-start | bytes 110600 | tf_op jit(solution)/shard_map/ppermute | solution.py:67
  500.9 2.2 collective-permute-start.16
  514.2 5.5 fusion.18
  519.7 3.1 add.361
  522.8 2.2 copy-done.2
  528.8 3.2 multiply_reduce_fusion
  533.9 4.9 add.354
  539.6 3.4 add.347
  544.9 10.5 %collective-permute-done.37 = f16[2,4,48,1536]{3,2,1,0:T(8,128)(2,1)S(1)} collective-permute-done((f16[2,4,48,1536]{3,2,1,0:T(8,128)(2,1)}, f16[2,4,48,1536]{3,2,1,0:T(8,128)(2,1)S(1)}, u32[]{:S(2)}, u32[]{:S(2)}) %collective-permute-start.37) | collective-permute-done | bytes 1179680 | tf_op jit(solution)/shard_map/ppermute | solution.py:67
  555.9 1.9 collective-permute-start.38
  557.9 20.9 %collective-permute-done.31 = f16[2,4,48,1536]{3,2,1,0:T(8,128)(2,1)S(1)} collective-permute-done((f16[2,4,48,1536]{3,2,1,0:T(8,128)(2,1)S(1)}, f16[2,4,48,1536]{3,2,1,0:T(8,128)(2,1)S(1)}, u32[]{:S(2)}, u32[]{:S(2)}) %collective-permute-start.31) | collective-permute-done | bytes 1179680 | tf_op jit(solution)/shard_map/ppermute | solution.py:67
  579.3 2.3 collective-permute-start.32
  586.5 3.0 collective-permute-start.40
  589.5 6.1 collective-permute-done.26
  596.2 3.6 collective-permute-start.29
  600.8 3.4 collective-permute-done.27
  604.3 7.8 %collective-permute-done.28 = f16[48,1536]{1,0:T(8,128)(2,1)S(1)} collective-permute-done((f16[48,1536]{1,0:T(8,128)(2,1)S(1)}, f16[48,1536]{1,0:T(8,128)(2,1)S(1)}, u32[]{:S(2)}, u32[]{:S(2)}) %collective-permute-start.28) | collective-permute-done | bytes 147488 | tf_op jit(solution)/shard_map/ppermute | solution.py:67
  612.1 3.3 collective-permute-start.35
  618.1 3.4 collective-permute-done.34
  622.2 2.5 multiply_reduce_fusion.2
  626.7 1.8 multiply_reduce_fusion.1
  630.6 18.8 %total.1 = f32[32,8,128]{2,1,0:T(8,128)} custom-call(f32[32,8,128]{2,1,0:T(8,128)} %bitcast.301), custom_call_target="tpu_custom_call" | custom-call | tf_op jit(solution)/shard_map/total/pallas_call | solution.py:363
  659.9 2.1 add_multiply_fusion.3
  662.0 8.6 %add_multiply_fusion = (f32[960,768]{1,0:T(8,128)}, f32[960,768]{1,0:T(8,128)}, f32[960,768]{1,0:T(8,128)}) fusion(f32[960,768]{1,0:T(8,128)S(1)} %copy-done.3, f32[960,768]{1,0:T(8,128)} %get-tuple-element.190, f32[]{:T(128)S(6)} %min_shard_map.3, f32[960,768]{1,0:T(8,128)} %param.31, f32[960,768]{1,0:T(8,128)} %param.30), kind=kLoop, calls=%fused_computation.43 | loop fusion | flops 11059200 | bytes 20643844 | tf_op jit(solution)/shard_map/mul | solution.py:1396
  (267 shorter events, 93.0 us)
Async XLA Ops:
  326.1 92.7 %copy-start.37 = (f32[1,768]{1,0:T(1,128)S(1)}, f32[1,768]{1,0:T(1,128)}, u32[]{:S(2)}) copy-start(f32[1,768]{1,0:T(1,128)} %get-tuple-element.168.pool_ref) | copy-start | bytes 9220
  326.1 92.7 %copy-start.42 = (f32[1,768]{1,0:T(1,128)S(1)}, f32[1,768]{1,0:T(1,128)}, u32[]{:S(2)}) copy-start(f32[1,768]{1,0:T(1,128)} %get-tuple-element.170.refs_0_) | copy-start | bytes 9220
  326.1 93.4 %copy-start.43 = (f32[1,128]{1,0:T(1,128)S(1)}, f32[1,128]{1,0:T(1,128)}, u32[]{:S(2)}) copy-start(f32[1,128]{1,0:T(1,128)} %get-tuple-element.169) | copy-start | bytes 1540
  326.1 96.6 %copy-start.41 = (s32[1,1024]{1,0:T(1,128)S(1)}, s32[1,1024]{1,0:T(1,128)}, u32[]{:S(2)}) copy-start(s32[1,1024]{1,0:T(1,128)} %copy-done.40) | copy-start | bytes 12292
  391.0 36.9 %collective-permute-start.18 = (f32[2,2,4,48,384]{4,3,2,1,0:T(8,128)}, f32[2,2,4,48,384]{4,3,2,1,0:T(8,128)}, u32[]{:S(2)}, u32[]{:S(2)}) collective-permute-start(f32[2,2,4,48,384]{4,3,2,1,0:T(8,128)} %get-tuple-element.199), channel_id=1, source_target_pairs={{0,2},{1,3},{2,0},{3,1},{4,6},{5,7},{6,4},{7,5},{8,10},{9,11},{10,... | collective-permute-start | bytes 3538952 | tf_op jit(solution)/shard_map/ppermute | solution.py:67
  391.2 128.5 %collective-permute-start.36 = (f32[2,2,4,48,1536]{4,3,2,1,0:T(8,128)}, f32[2,2,4,48,1536]{4,3,2,1,0:T(8,128)}, u32[]{:S(2)}, u32[]{:S(2)}) collective-permute-start(f32[2,2,4,48,1536]{4,3,2,1,0:T(8,128)} %get-tuple-element.206), channel_id=1, source_target_pairs={{0,2},{1,3},{2,0},{3,1},{4,6},{5,7},{6,4},{7,5},{8,10},{9,11},{10,... | collective-permute-start | bytes 14155784 | tf_op jit(solution)/shard_map/ppermute | solution.py:67
  391.5 38.1 %collective-permute-start = (f32[2,2,4,48,384]{4,3,2,1,0:T(8,128)}, f32[2,2,4,48,384]{4,3,2,1,0:T(8,128)}, u32[]{:S(2)}, u32[]{:S(2)}) collective-permute-start(f32[2,2,4,48,384]{4,3,2,1,0:T(8,128)} %get-tuple-element.192), channel_id=1, source_target_pairs={{0,2},{1,3},{2,0},{3,1},{4,6},{5,7},{6,4},{7,5},{8,10},{9,11},{10,... | collective-permute-start | bytes 3538952 | tf_op jit(solution)/shard_map/ppermute | solution.py:67
  391.7 41.3 %collective-permute-start.6 = (f32[2,2,4,48,384]{4,3,2,1,0:T(8,128)}, f32[2,2,4,48,384]{4,3,2,1,0:T(8,128)S(1)}, u32[]{:S(2)}, u32[]{:S(2)}) collective-permute-start(f32[2,2,4,48,384]{4,3,2,1,0:T(8,128)} %get-tuple-element.195), channel_id=1, source_target_pairs={{0,2},{1,3},{2,0},{3,1},{4,6},{5,7},{6,4},{7,5},{8,10},{9,11},{10,... | collective-permute-start | bytes 3538952 | tf_op jit(solution)/shard_map/ppermute | solution.py:67
  392.0 44.5 %collective-permute-start.12 = (f32[2,2,4,48,384]{4,3,2,1,0:T(8,128)}, f32[2,2,4,48,384]{4,3,2,1,0:T(8,128)S(1)}, u32[]{:S(2)}, u32[]{:S(2)}) collective-permute-start(f32[2,2,4,48,384]{4,3,2,1,0:T(8,128)} %get-tuple-element.197), channel_id=1, source_target_pairs={{0,2},{1,3},{2,0},{3,1},{4,6},{5,7},{6,4},{7,5},{8,10},{9,11},{10,... | collective-permute-start | bytes 3538952 | tf_op jit(solution)/shard_map/ppermute | solution.py:67
  427.9 106.0 %collective-permute-start.30 = (f32[2,2,4,48,1536]{4,3,2,1,0:T(8,128)}, f32[2,2,4,48,1536]{4,3,2,1,0:T(8,128)}, u32[]{:S(2)}, u32[]{:S(2)}) collective-permute-start(f32[2,2,4,48,1536]{4,3,2,1,0:T(8,128)} %get-tuple-element.204), channel_id=1, source_target_pairs={{0,2},{1,3},{2,0},{3,1},{4,6},{5,7},{6,4},{7,5},{8,10},{9,11},{10,... | collective-permute-start | bytes 14155784 | tf_op jit(solution)/shard_map/ppermute | solution.py:67
  429.6 10.1 %collective-permute-start.19 = (f16[2,4,48,384]{3,2,1,0:T(8,128)(2,1)S(1)}, f16[2,4,48,384]{3,2,1,0:T(8,128)(2,1)S(1)}, u32[]{:S(2)}, u32[]{:S(2)}) collective-permute-start(f16[2,4,48,384]{3,2,1,0:T(8,128)(2,1)S(1)} %fusion.59), channel_id=1, source_target_pairs={{0,4},{1,5},{2,6},{3,7},{4,0},{5,1},{6,2},{7,3},{8,12},{9,13},{10,... | collective-permute-start | bytes 884744 | tf_op jit(solution)/shard_map/ppermute | solution.py:67
  433.0 9.0 %collective-permute-start.1 = (f16[2,4,48,384]{3,2,1,0:T(8,128)(2,1)S(1)}, f16[2,4,48,384]{3,2,1,0:T(8,128)(2,1)S(1)}, u32[]{:S(2)}, u32[]{:S(2)}) collective-permute-start(f16[2,4,48,384]{3,2,1,0:T(8,128)(2,1)S(1)} %fusion.56), channel_id=1, source_target_pairs={{0,1},{1,0},{2,3},{3,2},{4,5},{5,4},{6,7},{7,6},{8,9},{9,8},{10,11... | collective-permute-start | bytes 884744 | tf_op jit(solution)/shard_map/ppermute | solution.py:67
  436.5 11.8 %collective-permute-start.7 = (f16[2,4,48,384]{3,2,1,0:T(8,128)(2,1)}, f16[2,4,48,384]{3,2,1,0:T(8,128)(2,1)}, u32[]{:S(2)}, u32[]{:S(2)}) collective-permute-start(f16[2,4,48,384]{3,2,1,0:T(8,128)(2,1)} %fusion.57), channel_id=1, source_target_pairs={{0,4},{1,5},{2,6},{3,7},{4,0},{5,1},{6,2},{7,3},{8,12},{9,13},{10,... | collective-permute-start | bytes 884744 | tf_op jit(solution)/shard_map/ppermute | solution.py:67
  439.7 11.5 %collective-permute-start.13 = (f16[2,4,48,384]{3,2,1,0:T(8,128)(2,1)}, f16[2,4,48,384]{3,2,1,0:T(8,128)(2,1)}, u32[]{:S(2)}, u32[]{:S(2)}) collective-permute-start(f16[2,4,48,384]{3,2,1,0:T(8,128)(2,1)} %fusion.58), channel_id=1, source_target_pairs={{0,1},{1,0},{2,3},{3,2},{4,5},{5,4},{6,7},{7,6},{8,9},{9,8},{10,11... | collective-permute-start | bytes 884744 | tf_op jit(solution)/shard_map/ppermute | solution.py:67
  442.0 25.1 %collective-permute-start.20 = (f16[4,48,384]{2,1,0:T(8,128)(2,1)}, f16[4,48,384]{2,1,0:T(8,128)(2,1)}, u32[]{:S(2)}, u32[]{:S(2)}) collective-permute-start(f16[4,48,384]{2,1,0:T(8,128)(2,1)} %fusion.91), channel_id=1, source_target_pairs={{0,1},{1,0},{2,3},{3,2},{4,5},{5,4},{6,7},{7,6},{8,9},{9,8},{10,11... | collective-permute-start | bytes 442376 | tf_op jit(solution)/shard_map/ppermute | solution.py:67
  444.1 70.1 %all-to-all-start.4 = ((bf16[32,40,768]{2,1,0:T(8,128)(2,1)}), bf16[32,40,768]{2,1,0:T(8,128)(2,1)}, u32[]{:S(2)}, u32[]{:S(2)}) async-start(bf16[32,40,768]{2,1,0:T(8,128)(2,1)} %bitcast.295), calls=%async_computation.4 | async-start | bytes 3932160 | tf_op jit(solution)/shard_map/all_to_all | solution.py:600
  448.4 16.1 %collective-permute-start.2 = (f16[4,48,384]{2,1,0:T(8,128)(2,1)}, f16[4,48,384]{2,1,0:T(8,128)(2,1)S(1)}, u32[]{:S(2)}, u32[]{:S(2)}) collective-permute-start(f16[4,48,384]{2,1,0:T(8,128)(2,1)} %fusion.88), channel_id=1, source_target_pairs={{0,4},{1,5},{2,6},{3,7},{4,0},{5,1},{6,2},{7,3},{8,12},{9,13},{10,... | collective-permute-start | bytes 442376 | tf_op jit(solution)/shard_map/ppermute | solution.py:67
  451.2 17.9 %collective-permute-start.8 = (f16[4,48,384]{2,1,0:T(8,128)(2,1)S(1)}, f16[4,48,384]{2,1,0:T(8,128)(2,1)S(1)}, u32[]{:S(2)}, u32[]{:S(2)}) collective-permute-start(f16[4,48,384]{2,1,0:T(8,128)(2,1)S(1)} %fusion.89), channel_id=1, source_target_pairs={{0,1},{1,0},{2,3},{3,2},{4,5},{5,4},{6,7},{7,6},{8,9},{9,8},{10,11... | collective-permute-start | bytes 442376 | tf_op jit(solution)/shard_map/ppermute | solution.py:67
  464.5 9.7 %collective-permute-start.14 = (f16[4,48,384]{2,1,0:T(8,128)(2,1)S(1)}, f16[4,48,384]{2,1,0:T(8,128)(2,1)S(1)}, u32[]{:S(2)}, u32[]{:S(2)}) collective-permute-start(f16[4,48,384]{2,1,0:T(8,128)(2,1)S(1)} %fusion.90), channel_id=1, source_target_pairs={{0,4},{1,5},{2,6},{3,7},{4,0},{5,1},{6,2},{7,3},{8,12},{9,13},{10,... | collective-permute-start | bytes 442376 | tf_op jit(solution)/shard_map/ppermute | solution.py:67
  467.1 18.8 %collective-permute-start.3 = (f16[48,384]{1,0:T(8,128)(2,1)S(1)}, f16[48,384]{1,0:T(8,128)(2,1)S(1)}, u32[]{:S(2)}, u32[]{:S(2)}) collective-permute-start(f16[48,384]{1,0:T(8,128)(2,1)S(1)} %get-tuple-element.359), channel_id=1, source_target_pairs={{0,8},{1,9},{2,10},{3,11},{4,12},{5,13},{6,14},{7,15},{8,16},{9,17... | collective-permute-start | bytes 110600 | tf_op jit(solution)/shard_map/ppermute | solution.py:67
  469.2 27.8 %collective-permute-start.4 = (f16[48,384]{1,0:T(8,128)(2,1)S(1)}, f16[48,384]{1,0:T(8,128)(2,1)S(1)}, u32[]{:S(2)}, u32[]{:S(2)}) collective-permute-start(f16[48,384]{1,0:T(8,128)(2,1)S(1)} %get-tuple-element.361), channel_id=1, source_target_pairs={{0,16},{1,17},{2,18},{3,19},{4,20},{5,21},{6,22},{7,23},{8,24},{9,... | collective-permute-start | bytes 110600 | tf_op jit(solution)/shard_map/ppermute | solution.py:67
  474.2 24.5 %collective-permute-start.5 = (f16[48,384]{1,0:T(8,128)(2,1)S(1)}, f16[48,384]{1,0:T(8,128)(2,1)S(1)}, u32[]{:S(2)}, u32[]{:S(2)}) collective-permute-start(f16[48,384]{1,0:T(8,128)(2,1)S(1)} %get-tuple-element.360), channel_id=1, source_target_pairs={{0,24},{1,25},{2,26},{3,27},{4,28},{5,29},{6,30},{7,31},{8,0},{9,1... | collective-permute-start | bytes 110600 | tf_op jit(solution)/shard_map/ppermute | solution.py:67
  485.9 13.7 %collective-permute-start.10 = (f16[48,384]{1,0:T(8,128)(2,1)S(1)}, f16[48,384]{1,0:T(8,128)(2,1)S(1)}, u32[]{:S(2)}, u32[]{:S(2)}) collective-permute-start(f16[48,384]{1,0:T(8,128)(2,1)S(1)} %get-tuple-element.364), channel_id=1, source_target_pairs={{0,16},{1,17},{2,18},{3,19},{4,20},{5,21},{6,22},{7,23},{8,24},{9,... | collective-permute-start | bytes 110600 | tf_op jit(solution)/shard_map/ppermute | solution.py:67
  497.0 4.0 collective-permute-start.11
  498.7 6.0 collective-permute-start.9
  499.7 5.9 collective-permute-start.15
  500.9 5.8 collective-permute-start.16
  504.6 4.3 collective-permute-start.17
  505.6 5.8 collective-permute-start.21
  506.8 5.4 collective-permute-start.22
  509.0 4.0 collective-permute-start.23
  511.4 28.2 %collective-permute-start.24 = (f32[2,2,4,48,1536]{4,3,2,1,0:T(8,128)}, f32[2,2,4,48,1536]{4,3,2,1,0:T(8,128)}, u32[]{:S(2)}, u32[]{:S(2)}) collective-permute-start(f32[2,2,4,48,1536]{4,3,2,1,0:T(8,128)} %get-tuple-element.201), channel_id=1, source_target_pairs={{0,2},{1,3},{2,0},{3,1},{4,6},{5,7},{6,4},{7,5},{8,10},{9,11},{10,... | collective-permute-start | bytes 14155784 | tf_op jit(solution)/shard_map/ppermute | solution.py:67
  526.3 29.1 %collective-permute-start.37 = (f16[2,4,48,1536]{3,2,1,0:T(8,128)(2,1)}, f16[2,4,48,1536]{3,2,1,0:T(8,128)(2,1)S(1)}, u32[]{:S(2)}, u32[]{:S(2)}) collective-permute-start(f16[2,4,48,1536]{3,2,1,0:T(8,128)(2,1)} %fusion.35), channel_id=1, source_target_pairs={{0,4},{1,5},{2,6},{3,7},{4,0},{5,1},{6,2},{7,3},{8,12},{9,13},{10,... | collective-permute-start | bytes 3538952 | tf_op jit(solution)/shard_map/ppermute | solution.py:67
  539.1 39.6 %collective-permute-start.31 = (f16[2,4,48,1536]{3,2,1,0:T(8,128)(2,1)S(1)}, f16[2,4,48,1536]{3,2,1,0:T(8,128)(2,1)S(1)}, u32[]{:S(2)}, u32[]{:S(2)}) collective-permute-start(f16[2,4,48,1536]{3,2,1,0:T(8,128)(2,1)S(1)} %fusion.34), channel_id=1, source_target_pairs={{0,4},{1,5},{2,6},{3,7},{4,0},{5,1},{6,2},{7,3},{8,12},{9,13},{10,... | collective-permute-start | bytes 3538952 | tf_op jit(solution)/shard_map/ppermute | solution.py:67
  543.3 38.3 %collective-permute-start.25 = (f16[2,4,48,1536]{3,2,1,0:T(8,128)(2,1)S(1)}, f16[2,4,48,1536]{3,2,1,0:T(8,128)(2,1)S(1)}, u32[]{:S(2)}, u32[]{:S(2)}) collective-permute-start(f16[2,4,48,1536]{3,2,1,0:T(8,128)(2,1)S(1)} %fusion.33), channel_id=1, source_target_pairs={{0,1},{1,0},{2,3},{3,2},{4,5},{5,4},{6,7},{7,6},{8,9},{9,8},{10,11... | collective-permute-start | bytes 3538952 | tf_op jit(solution)/shard_map/ppermute | solution.py:67
  555.9 28.3 %collective-permute-start.38 = (f16[4,48,1536]{2,1,0:T(8,128)(2,1)S(1)}, f16[4,48,1536]{2,1,0:T(8,128)(2,1)S(1)}, u32[]{:S(2)}, u32[]{:S(2)}) collective-permute-start(f16[4,48,1536]{2,1,0:T(8,128)(2,1)S(1)} %fusion.45), channel_id=1, source_target_pairs={{0,1},{1,0},{2,3},{3,2},{4,5},{5,4},{6,7},{7,6},{8,9},{9,8},{10,11... | collective-permute-start | bytes 1769480 | tf_op jit(solution)/shard_map/ppermute | solution.py:67
  579.3 16.9 %collective-permute-start.32 = (f16[4,48,1536]{2,1,0:T(8,128)(2,1)S(1)}, f16[4,48,1536]{2,1,0:T(8,128)(2,1)S(1)}, u32[]{:S(2)}, u32[]{:S(2)}) collective-permute-start(f16[4,48,1536]{2,1,0:T(8,128)(2,1)S(1)} %fusion.44), channel_id=1, source_target_pairs={{0,1},{1,0},{2,3},{3,2},{4,5},{5,4},{6,7},{7,6},{8,9},{9,8},{10,11... | collective-permute-start | bytes 1769480 | tf_op jit(solution)/shard_map/ppermute | solution.py:67
  582.0 13.6 %collective-permute-start.26 = (f16[4,48,1536]{2,1,0:T(8,128)(2,1)S(1)}, f16[4,48,1536]{2,1,0:T(8,128)(2,1)S(1)}, u32[]{:S(2)}, u32[]{:S(2)}) collective-permute-start(f16[4,48,1536]{2,1,0:T(8,128)(2,1)S(1)} %fusion.43), channel_id=1, source_target_pairs={{0,4},{1,5},{2,6},{3,7},{4,0},{5,1},{6,2},{7,3},{8,12},{9,13},{10,... | collective-permute-start | bytes 1769480 | tf_op jit(solution)/shard_map/ppermute | solution.py:67
  585.2 40.1 %collective-permute-start.39 = (f16[48,1536]{1,0:T(8,128)(2,1)}, f16[48,1536]{1,0:T(8,128)(2,1)S(1)}, u32[]{:S(2)}, u32[]{:S(2)}) collective-permute-start(f16[48,1536]{1,0:T(8,128)(2,1)} %get-tuple-element.347), channel_id=1, source_target_pairs={{0,8},{1,9},{2,10},{3,11},{4,12},{5,13},{6,14},{7,15},{8,16},{9,17... | collective-permute-start | bytes 442376 | tf_op jit(solution)/shard_map/ppermute | solution.py:67
  586.5 38.9 %collective-permute-start.40 = (f16[48,1536]{1,0:T(8,128)(2,1)}, f16[48,1536]{1,0:T(8,128)(2,1)S(1)}, u32[]{:S(2)}, u32[]{:S(2)}) collective-permute-start(f16[48,1536]{1,0:T(8,128)(2,1)} %get-tuple-element.349), channel_id=1, source_target_pairs={{0,16},{1,17},{2,18},{3,19},{4,20},{5,21},{6,22},{7,23},{8,24},{9,... | collective-permute-start | bytes 442376 | tf_op jit(solution)/shard_map/ppermute | solution.py:67
  595.9 8.3 %collective-permute-start.27 = (f16[48,1536]{1,0:T(8,128)(2,1)S(1)}, f16[48,1536]{1,0:T(8,128)(2,1)S(1)}, u32[]{:S(2)}, u32[]{:S(2)}) collective-permute-start(f16[48,1536]{1,0:T(8,128)(2,1)S(1)} %get-tuple-element.353), channel_id=1, source_target_pairs={{0,8},{1,9},{2,10},{3,11},{4,12},{5,13},{6,14},{7,15},{8,16},{9,17... | collective-permute-start | bytes 442376 | tf_op jit(solution)/shard_map/ppermute | solution.py:67
  596.0 16.1 %collective-permute-start.28 = (f16[48,1536]{1,0:T(8,128)(2,1)S(1)}, f16[48,1536]{1,0:T(8,128)(2,1)S(1)}, u32[]{:S(2)}, u32[]{:S(2)}) collective-permute-start(f16[48,1536]{1,0:T(8,128)(2,1)S(1)} %get-tuple-element.355), channel_id=1, source_target_pairs={{0,16},{1,17},{2,18},{3,19},{4,20},{5,21},{6,22},{7,23},{8,24},{9,... | collective-permute-start | bytes 442376 | tf_op jit(solution)/shard_map/ppermute | solution.py:67
  596.2 15.9 %collective-permute-start.29 = (f16[48,1536]{1,0:T(8,128)(2,1)S(1)}, f16[48,1536]{1,0:T(8,128)(2,1)S(1)}, u32[]{:S(2)}, u32[]{:S(2)}) collective-permute-start(f16[48,1536]{1,0:T(8,128)(2,1)S(1)} %get-tuple-element.354), channel_id=1, source_target_pairs={{0,24},{1,25},{2,26},{3,27},{4,28},{5,29},{6,30},{7,31},{8,0},{9,1... | collective-permute-start | bytes 442376 | tf_op jit(solution)/shard_map/ppermute | solution.py:67
  600.8 53.5 %copy-start.5 = (f32[48,2,1536]{2,1,0:T(2,128)S(1)}, f32[48,2,1536]{2,1,0:T(2,128)}, u32[]{:S(2)}) copy-start(f32[48,2,1536]{2,1,0:T(2,128)} %param.38) | copy-start | bytes 1769476
  604.2 12.5 %collective-permute-start.33 = (f16[48,1536]{1,0:T(8,128)(2,1)}, f16[48,1536]{1,0:T(8,128)(2,1)}, u32[]{:S(2)}, u32[]{:S(2)}) collective-permute-start(f16[48,1536]{1,0:T(8,128)(2,1)} %get-tuple-element.350), channel_id=1, source_target_pairs={{0,8},{1,9},{2,10},{3,11},{4,12},{5,13},{6,14},{7,15},{8,16},{9,17... | collective-permute-start | bytes 442376 | tf_op jit(solution)/shard_map/ppermute | solution.py:67
  612.1 9.5 %collective-permute-start.34 = (f16[48,1536]{1,0:T(8,128)(2,1)}, f16[48,1536]{1,0:T(8,128)(2,1)}, u32[]{:S(2)}, u32[]{:S(2)}) collective-permute-start(f16[48,1536]{1,0:T(8,128)(2,1)} %get-tuple-element.352), channel_id=1, source_target_pairs={{0,16},{1,17},{2,18},{3,19},{4,20},{5,21},{6,22},{7,23},{8,24},{9,... | collective-permute-start | bytes 442376 | tf_op jit(solution)/shard_map/ppermute | solution.py:67
  612.1 10.1 %collective-permute-start.35 = (f16[48,1536]{1,0:T(8,128)(2,1)}, f16[48,1536]{1,0:T(8,128)(2,1)}, u32[]{:S(2)}, u32[]{:S(2)}) collective-permute-start(f16[48,1536]{1,0:T(8,128)(2,1)} %get-tuple-element.351), channel_id=1, source_target_pairs={{0,24},{1,25},{2,26},{3,27},{4,28},{5,29},{6,30},{7,31},{8,0},{9,1... | collective-permute-start | bytes 442376 | tf_op jit(solution)/shard_map/ppermute | solution.py:67
  616.8 10.0 %collective-permute-start.41 = (f16[48,1536]{1,0:T(8,128)(2,1)}, f16[48,1536]{1,0:T(8,128)(2,1)}, u32[]{:S(2)}, u32[]{:S(2)}) collective-permute-start(f16[48,1536]{1,0:T(8,128)(2,1)} %get-tuple-element.348), channel_id=1, source_target_pairs={{0,24},{1,25},{2,26},{3,27},{4,28},{5,29},{6,30},{7,31},{8,0},{9,1... | collective-permute-start | bytes 442376 | tf_op jit(solution)/shard_map/ppermute | solution.py:67
  (45 other events, 354.0 us)

commit v3 on v2

--- a/solution.py
+++ b/solution.py
@@ -27,6 +27,7 @@
 VMEM_LIMIT = 58 * 1024 * 1024
 ROW_BLOCK = 256
 HIDDEN_BLOCK = 256
+BACK_BLOCK = 512
 
 
 class Plan:
@@ -80,21 +81,26 @@
             (self.tensor, self.nz, self.nx, self.nc, rows, columns), shard.dtype
         )
 
-    def scatter(self, parts, order, scale):
+    def scatter_whole(self, part):
+        whole = part.reshape(self.tensor * self.rows, part.shape[-1])
+        return lax.psum_scatter(whole, ("tensor", "dp"), scatter_dimension=0, tiled=True)
+
+    def step_along(self, total, axis, scale):
+        own_y = lax.axis_index("tensor")
+        pick = functools.partial(lax.dynamic_index_in_dim, total, axis=0, keepdims=False)
+        kept = pick(own_y) if axis == "y" else total[0]
+        for far in range(1, self.size(axis)):
+            other = pick(lax.rem(own_y + far, self.tensor)) if axis == "y" else total[far]
+            sent = (other * scale).astype(jnp.float16)
+            kept = kept + self.shift(sent, axis, far).astype(F32) / scale
+        return kept
+
+    def scatter(self, part, order, scale):
         if not self.stepped:
-            whole = parts[0].reshape(self.tensor * self.rows, parts[0].shape[-1])
-            return lax.psum_scatter(
-                whole.astype(F32), ("tensor", "dp"), scatter_dimension=0, tiled=True
-            )
-        keep, send = parts
-        total = keep.astype(F32) + self.shift(send, "c", 1).astype(F32)
+            return self.scatter_whole(part)
         for axis in tuple(order) + ("z",):
-            kept = total[0]
-            for far in range(1, self.size(axis)):
-                sent = (total[far] * scale).astype(jnp.float16)
-                kept = kept + self.shift(sent, axis, far).astype(F32) / scale
-            total = kept
-        return total
+            part = self.step_along(part, axis, scale)
+        return part
 
 
     def weight_spec(self, width, columns, locate):
@@ -104,36 +110,148 @@
 
         return pl.BlockSpec((None, width, columns), index)
 
-    def grad_specs(self, order, columns, locate):
+    def grad_spec(self, order, columns, locate):
         def index(i, place):
             part, column = locate(i)
-            far = lax.rem(part - place[3] + self.tensor, self.tensor)
             if order == "yx":
-                return (far, 0, 0, 0, column)
-            return (0, far, 0, 0, column)
+                return (part, 0, 0, 0, column)
+            return (0, part, 0, 0, column)
 
         middle = (None, self.nx) if order == "yx" else (self.nx, None)
-        spec = pl.BlockSpec(middle + (self.nz, self.rows, columns), index)
-        return [spec] * self.nc
-
-    def grad_shapes(self, order, columns):
+        return pl.BlockSpec(middle + (self.nz, self.rows, columns), index)
+
+    def grad_shape(self, order, columns):
         middle = (self.tensor, self.nx) if order == "yx" else (self.nx, self.tensor)
-        shape = middle + (self.nz, self.rows, columns)
-        return [jax.ShapeDtypeStruct(shape, F32)] * self.nc
-
-    def disperse(self, place, source, first_column, targets):
-        columns = targets[0].shape[-1]
-        for far_z in range(self.nz):
-            z = lax.rem(place[0] + far_z, self.nz)
-            for far_x in range(self.nx):
-                x = lax.rem(place[1] + far_x, self.nx)
-                for far_c in range(self.nc):
-                    c = lax.rem(place[2] + far_c, self.nc)
-                    start = ((z * self.nx + x) * self.nc + c) * self.rows
-                    start = pl.multiple_of(start, 16)
-                    targets[far_c][far_x, far_z] = source[
-                        pl.ds(start, self.rows), first_column : first_column + columns
-                    ]
+        return jax.ShapeDtypeStruct(middle + (self.nz, self.rows, columns), F32)
+
+
+class SiblingSum:
+    def __init__(self, plan, steps, kept, sent, came, send_sem, recv_sem, free_sem):
+        self.plan, self.steps = plan, steps
+        self.kept, self.sent, self.came = kept, sent, came
+        self.send_sem, self.recv_sem, self.free_sem = send_sem, recv_sem, free_sem
+        dp_index, self.y = lax.axis_index("dp"), lax.axis_index("tensor")
+        self.c = lax.rem(dp_index, plan.nc)
+        self.x = lax.rem(dp_index // plan.nc, plan.nx)
+        self.z = dp_index // (plan.nc * plan.nx)
+        self.sibling = (dp_index + 1 - 2 * self.c, self.y)
+
+    def greet(self):
+        if self.plan.nc > 1:
+            barrier = pltpu.get_barrier_semaphore()
+            pl.semaphore_signal(
+                barrier, inc=1, device_id=self.sibling, device_id_type=pl.DeviceIdType.MESH
+            )
+            pl.semaphore_wait(barrier, 1)
+
+    def copy(self, slot):
+        return pltpu.make_async_remote_copy(
+            src_ref=self.sent.at[slot],
+            dst_ref=self.came.at[slot],
+            send_sem=self.send_sem.at[slot],
+            recv_sem=self.recv_sem.at[slot],
+            device_id=self.sibling,
+            device_id_type=pl.DeviceIdType.MESH,
+        )
+
+    def push(self, step, product):
+        plan = self.plan
+        slot = lax.rem(step, 2)
+        if plan.nc > 1:
+
+            @pl.when(step >= 2)
+            def _():
+                self.copy(slot).wait_send()
+                pl.semaphore_wait(self.free_sem, 1)
+
+        for far_x in range(plan.nx):
+            x = lax.rem(self.x + far_x, plan.nx)
+            for far_z in range(plan.nz):
+                z = lax.rem(self.z + far_z, plan.nz)
+                base = (z * plan.nx + x) * plan.nc
+                to = slice(
+                    (far_x * plan.nz + far_z) * plan.rows,
+                    (far_x * plan.nz + far_z + 1) * plan.rows,
+                )
+                start = pl.multiple_of((base + self.c) * plan.rows, 16)
+                self.kept[slot, to, :] = product[pl.ds(start, plan.rows), :]
+                if plan.nc > 1:
+                    start = pl.multiple_of((base + 1 - self.c) * plan.rows, 16)
+                    self.sent[slot, to, :] = product[pl.ds(start, plan.rows), :]
+        if plan.nc > 1:
+            self.copy(slot).start()
+
+    def pull(self, step, targets, widths, peak_out):
+        plan = self.plan
+        slot = lax.rem(step, 2)
+        if plan.nc > 1:
+            self.copy(slot).wait_recv()
+        peak = jnp.zeros((1, 1), F32)
+        for far_x in range(plan.nx):
+            for far_z in range(plan.nz):
+                at = slice(
+                    (far_x * plan.nz + far_z) * plan.rows,
+                    (far_x * plan.nz + far_z + 1) * plan.rows,
+                )
+                value = self.kept[slot, at, :]
+                if plan.nc > 1:
+                    value = value + self.came[slot, at, :]
+                start = 0
+                for target, width in zip(targets, widths):
+                    target[far_x, far_z] = value[:, start : start + width]
+                    start += width
+                largest = jnp.max(jnp.abs(value), axis=0, keepdims=True)
+                peak = jnp.maximum(peak, jnp.max(largest, axis=1, keepdims=True))
+        if plan.nc > 1:
+
+            @pl.when(step < self.steps - 2)
+            def _():
+                pl.semaphore_signal(
+                    self.free_sem,
+                    inc=1,
+                    device_id=self.sibling,
+                    device_id_type=pl.DeviceIdType.MESH,
+                )
+
+            @pl.when(step == self.steps - 1)
+            def _():
+                for last in range(max(self.steps - 2, 0), self.steps):
+                    self.copy(last % 2).wait_send()
+
+        peak = jnp.broadcast_to(peak, peak_out.shape)
+
+        @pl.when(step == 0)
+        def _():
+            peak_out[...] = peak
+
+        @pl.when(step > 0)
+        def _():
+            peak_out[...] = jnp.maximum(peak_out[...], peak)
+
+    @staticmethod
+    def scratch(plan, columns):
+        rows = plan.nx * plan.nz * plan.rows
+        held = pltpu.VMEM((2, rows, columns), F32)
+        if plan.nc == 1:
+            return [held]
+        return [
+            held,
+            held,
+            held,
+            pltpu.SemaphoreType.DMA((2,)),
+            pltpu.SemaphoreType.DMA((2,)),
+            pltpu.SemaphoreType.REGULAR,
+        ]
+
+    @staticmethod
+    def made_of(plan, steps, refs):
+        return SiblingSum(plan, steps, *(tuple(refs) + (None,) * (6 - len(refs))))
+
+    @staticmethod
+    def params(plan, collective_id):
+        if plan.nc == 1:
+            return params()
+        return params(collective_id=collective_id, has_side_effects=True)
 
 
 def dot(left, right):
@@ -181,19 +299,6 @@
 def of_head(values, head):
     lane = lax.broadcasted_iota(jnp.int32, values.shape, 1)
     return jnp.where(lane // HEAD == head, values, jnp.zeros_like(values))
-
-
-def note_peak(peak_out, product):
-    largest = jnp.max(jnp.abs(product[...]), axis=0, keepdims=True)
-    largest = jnp.broadcast_to(jnp.max(largest, axis=1, keepdims=True), peak_out.shape)
-
-    @pl.when(pl.program_id(0) == 0)
-    def _():
-        peak_out[...] = largest
-
-    @pl.when(pl.program_id(0) > 0)
-    def _():
-        peak_out[...] = jnp.maximum(peak_out[...], largest)
 
 
 def params(**more):
@@ -296,34 +401,6 @@
         ],
         compiler_params=params(collective_id=0, has_side_effects=True),
     )(blocks)
-
-
-def largest_sum_kernel(count, tensor, block_ref, out_ref, held, send_sem, recv_sem):
-    me = own_index(tensor)
-    greet_all(me, count, tensor)
-    for start in (True, False):
-        for_all(
-            me, count, tensor, lambda peer: block_ref, held.at[me], send_sem, recv_sem, start
-        )
-        if start:
-            held[pl.ds(me, 1)] = block_ref[...][None]
-    out_ref[...] = jnp.sum(held[...], axis=0)
-
-
-def largest_sum(plan, block):
-    return pl.pallas_call(
-        functools.partial(largest_sum_kernel, plan.count, plan.tensor),
-        name="largest_sum",
-        out_shape=jax.ShapeDtypeStruct(block.shape, block.dtype),
-        in_specs=[in_vmem()],
-        out_specs=in_vmem(),
-        scratch_shapes=[
-            pltpu.VMEM((plan.count,) + block.shape, block.dtype),
-            pltpu.SemaphoreType.DMA((plan.count - 1,)),
-            pltpu.SemaphoreType.DMA((plan.count - 1,)),
-        ],
-        compiler_params=params(collective_id=3, has_side_effects=True),
-    )(block)
 
 
 def total_kernel(
@@ -393,7 +470,7 @@
         plan = self.plan
         z, x, c, y = self.z, self.x, self.c, self.y
         if stage == 0:
-            target = self.out.at[y, z, x, c, self.at]
+            target = self.out.at[(y, z, x, c) + self.at]
             return [
                 pltpu.make_async_remote_copy(
                     src_ref=self.shard.at[self.at],
@@ -410,11 +487,13 @@
         axis = path[stage - 1]
         every = slice(None)
         block = self.out.at[
-            every if "y" in done else y,
-            every,
-            every if "x" in done else x,
-            every if "c" in done else c,
-            self.at,
+            (
+                every if "y" in done else y,
+                every,
+                every if "x" in done else x,
+                every if "c" in done else c,
+            )
+            + self.at
         ]
         device = {
             "x": self.device(z, 1 - x, c, y),
@@ -437,7 +516,7 @@
         slot = self.plan.nz + 2
         return pltpu.make_async_copy(
             self.shard.at[self.at],
-            self.out.at[self.y, self.z, self.x, self.c, self.at],
+            self.out.at[(self.y, self.z, self.x, self.c) + self.at],
             self.send_sem.at[slot],
         )
 
@@ -493,7 +572,7 @@
             plan,
             shards[n],
             outs[n],
-            slice(None),
+            (slice(None),),
             orders[n],
             weight_send.at[n],
             weight_recv.at[n],
@@ -548,9 +627,73 @@
 
 
 def wire_scale(plan, peak):
-    bound = largest_sum(plan, peak)[0, 0]
+    bound = peak[0, 0] * (plan.count // plan.nc)
     exponent = jnp.floor(jnp.log2(32768.0 / jnp.maximum(bound, 1e-30)))
     return jnp.exp2(jnp.clip(exponent, -60.0, 60.0))
+
+
+class PeakExchange:
+    def __init__(self, plan, own, held, send_sem, recv_sem):
+        self.own, self.held, self.send_sem, self.recv_sem = own, held, send_sem, recv_sem
+        dp_index, y = lax.axis_index("dp"), lax.axis_index("tensor")
+        c = lax.rem(dp_index, plan.nc)
+        x = lax.rem(dp_index // plan.nc, plan.nx)
+        z = dp_index // (plan.nc * plan.nx)
+
+        def device(z, x, y):
+            return ((z * plan.nx + x) * plan.nc + c, y)
+
+        self.peers = (
+            [device(z, 1 - x, y), device(z, x, 1 - y), device(z, 1 - x, 1 - y)],
+            [device(lax.rem(z + far, plan.nz), x, y) for far in range(1, plan.nz)],
+        )
+
+    def greet(self, more=()):
+        barrier = pltpu.get_barrier_semaphore()
+        peers = self.peers[0] + self.peers[1] + list(more)
+        for peer in peers:
+            pl.semaphore_signal(
+                barrier, inc=1, device_id=peer, device_id_type=pl.DeviceIdType.MESH
+            )
+        pl.semaphore_wait(barrier, len(peers))
+
+    def copies(self, stage):
+        first = len(self.peers[0]) * stage
+        return [
+            pltpu.make_async_remote_copy(
+                src_ref=self.own.at[stage],
+                dst_ref=self.held.at[first + n],
+                send_sem=self.send_sem.at[first + n],
+                recv_sem=self.recv_sem.at[first + n],
+                device_id=peer,
+                device_id_type=pl.DeviceIdType.MESH,
+            )
+            for n, peer in enumerate(self.peers[stage])
+        ]
+
+    def start(self, stage, value):
+        self.own[stage] = value
+        for copy in self.copies(stage):
+            copy.start()
+
+    def finish(self, stage):
+        for copy in self.copies(stage):
+            copy.wait()
+        value = self.own[stage]
+        first = len(self.peers[0]) * stage
+        for n in range(len(self.peers[stage])):
+            value = jnp.maximum(value, self.held[first + n])
+        return value
+
+    @staticmethod
+    def scratch(plan):
+        number = 3 + plan.nz - 1
+        return [
+            pltpu.VMEM((2, 8, LANES), F32),
+            pltpu.VMEM((number, 8, LANES), F32),
+            pltpu.SemaphoreType.DMA((number,)),
+            pltpu.SemaphoreType.DMA((number,)),
+        ]
 
 
 def token_places(slot_ids, length, vocab_shard):
@@ -603,18 +746,15 @@
 def transport_units(plan, shards, outs, send_sem, recv_sem):
     units = []
     for n in range(len(shards)):
-        rows = shards[n].shape[0]
-        cut = 16 * (rows // 16 * 2 // 3)
-        orders = (("x", "y"), ("y", "x")) if n % 2 == 0 else (("y", "x"), ("x", "y"))
-        ranges = ((0, cut), (cut, rows - cut))
-        for (start, size), order in zip(ranges, orders):
+        half = shards[n].shape[1] // 2
+        for side, order in enumerate((("x", "y"), ("y", "x"))):
             number = len(units)
             units.append(
                 Transport(
                     plan,
                     shards[n],
                     outs[n],
-                    pl.ds(start, size),
+                    (slice(None), pl.ds(side * half, half)),
                     order,
                     send_sem.at[number],
                     recv_sem.at[number],
@@ -623,30 +763,22 @@
     return units
 
 
-SLOTS_PER_STEP = 2
+SLOTS_PER_STEP = 4
 TRANSPORT_SLOTS = {
-    3: ((0, 1),),
-    4: ((1, 1),),
-    6: ((2, 1), (0, 2), (1, 2)),
-    7: ((3, 1),),
-    8: ((2, 2),),
-    9: ((3, 2), (0, 3), (1, 3)),
-    10: ((4, 1),),
-    11: ((5, 1), (2, 3)),
+    0: ((0, 0),),
+    7: ((0, 1), (1, 0)),
+    11: ((0, 2),),
+    14: ((1, 1), (2, 0)),
+    18: ((0, 3), (1, 2)),
+    22: ((2, 1),),
 }
-TRANSPORT_END = (
-    (4, 2),
-    (5, 2),
-    (3, 3),
-    (4, 3),
-    (5, 3),
-    (0, 4),
-    (1, 4),
-    (2, 4),
-    (3, 4),
-    (4, 4),
-    (5, 4),
-)
+TRANSPORT_END = ((1, 3), (2, 2), (2, 3), (0, 4), (1, 4), (2, 4))
+
+
+def advance(units, events):
+    for matrix, stage in events:
+        for side in range(2):
+            units[2 * matrix + side].advance(stage)
 
 
 def attend_kernel(plan, number, place, *refs):
@@ -665,8 +797,6 @@
         @pl.when(step == 0)
         def _():
             greet_neighbours(plan)
-            for unit in units:
-                unit.advance(0)
 
     def transport(part):
         if number:
@@ -675,8 +805,7 @@
 
                     @pl.when(step == slot // SLOTS_PER_STEP)
                     def _():
-                        for unit, stage in events:
-                            units[unit].advance(stage)
+                        advance(units, events)
 
     @pl.when(step == 0)
     def _():
@@ -706,8 +835,8 @@
     values = v[...].T
     for start in range(0, rows, ROW_BLOCK):
         at = slice(start, start + ROW_BLOCK)
-        if start == rows // 2:
-            transport(1)
+        if start > 0:
+            transport(start // ROW_BLOCK)
         outs = []
         for head in range(LANES // HEAD):
             scores = dot_last(keys, of_head(q[at, :], head)) + bias
@@ -737,8 +866,7 @@
             inverse_two[at, :] = inverse
             low_two[at, :] = (normal * norms[2:3, :] + norms[3:4, :]).astype(BF16)
         if number:
-            for unit, stage in TRANSPORT_END:
-                units[unit].advance(stage)
+            advance(units, TRANSPORT_END)
 
 
 def attend(plan, place, embedded, wq, wk, wv, wo, cosine, sine, norms, shards):
@@ -995,7 +1123,7 @@
     return loss[0, 0], loss[0, 1], grad
 
 
-def feed_back_body(plan, place, *refs):
+def feed_back_kernel(plan, steps, place, *refs):
     (
         grad_pool,
         x,
@@ -1010,17 +1138,31 @@
         normal_two,
         inverse_two,
         norms,
-    ) = refs[:13]
-    nc = plan.nc
-    gate_grads = refs[13 : 13 + nc]
-    up_grads = refs[13 + nc : 13 + 2 * nc]
-    down_grads = refs[13 + 2 * nc : 13 + 3 * nc]
-    grad_out, low_out, norm_out, peak_out = refs[13 + 3 * nc : 17 + 3 * nc]
-    low, low_turned, x_turned, made, product = refs[17 + 3 * nc :]
+        part_one,
+        part_two,
+        grad_out,
+        low_out,
+        norm_out,
+        peak_out,
+        low,
+        low_turned,
+        x_turned,
+        made,
+        product,
+    ) = refs[:24]
     rows, width = x.shape
-
-    @pl.when(pl.program_id(0) == 0)
+    step = pl.program_id(0)
+    half = BACK_BLOCK // 2
+    if plan.stepped:
+        sums = SiblingSum.made_of(plan, steps, refs[24:-4])
+        exchange = PeakExchange(plan, *refs[-4:])
+    else:
+        sums = SiblingSum.made_of(plan, steps, refs[24:])
+
+    @pl.when(step == 0)
     def _():
+        if plan.stepped:
+            exchange.greet([sums.sibling])
         for start in range(0, rows, ROW_BLOCK):
             at = slice(start, start + ROW_BLOCK)
             position = start + lax.broadcasted_iota(jnp.int32, (ROW_BLOCK, 1), 0)
@@ -1033,34 +1175,46 @@
             low_turned[:, at] = grad.astype(BF16).T
             x_turned[:, at] = x[at, :].T
 
-    for start in range(0, rows, ROW_BLOCK):
-        at = slice(start, start + ROW_BLOCK)
-        grad_hidden = dot(low[at, :], wd[...])
-        gate = gate_ref[at, :].astype(F32)
-        up = up_ref[at, :].astype(F32)
-        share_gate = jax.nn.sigmoid(gate)
-        grad_up = grad_hidden * gate * share_gate
-        grad_gate = grad_hidden * up * share_gate * (1.0 + gate * (1.0 - share_gate))
-        made[at, :HIDDEN_BLOCK] = grad_gate.astype(BF16)
-        made[at, HIDDEN_BLOCK:] = grad_up.astype(BF16)
-        grad_out[at, :] = (
-            grad_out[at, :]
-            + dot_last(made[at, :HIDDEN_BLOCK], wg[...])
-            + dot_last(made[at, HIDDEN_BLOCK:], wu[...])
+    @pl.when(step < steps)
+    def _():
+        for start in range(0, rows, ROW_BLOCK):
+            at = slice(start, start + ROW_BLOCK)
+            grad_hidden = dot(low[at, :], wd[...])
+            gate = gate_ref[at, :].astype(F32)
+            up = up_ref[at, :].astype(F32)
+            share_gate = jax.nn.sigmoid(gate)
+            grad_up = grad_hidden * gate * share_gate
+            grad_gate = grad_hidden * up * share_gate * (1.0 + gate * (1.0 - share_gate))
+            made[at, :BACK_BLOCK] = grad_gate.astype(BF16)
+            made[at, BACK_BLOCK:] = grad_up.astype(BF16)
+            grad_out[at, :] = (
+                grad_out[at, :]
+                + dot_last(made[at, :BACK_BLOCK], wg[...])
+                + dot_last(made[at, BACK_BLOCK:], wu[...])
+            )
+        down = dot(low_turned[...], hidden_ref[...])
+        product[:, :BACK_BLOCK] = dot(x_turned[...], made[:, :BACK_BLOCK])
+        product[:, BACK_BLOCK : BACK_BLOCK + half] = down[:, :half]
+        product[:, BACK_BLOCK + half : 2 * BACK_BLOCK + half] = dot(
+            x_turned[...], made[:, BACK_BLOCK:]
         )
-    product[:, : 2 * HIDDEN_BLOCK] = dot(x_turned[...], made[...])
-    product[:, 2 * HIDDEN_BLOCK :] = dot(low_turned[...], hidden_ref[...])
-    note_peak(peak_out, product)
-    plan.disperse(place, product, 0, gate_grads)
-    plan.disperse(place, product, HIDDEN_BLOCK, up_grads)
-    plan.disperse(place, product, 2 * HIDDEN_BLOCK, down_grads)
-
-    @pl.when(pl.program_id(0) == pl.num_programs(0) - 1)
+        product[:, 2 * BACK_BLOCK + half :] = down[:, half:]
+        sums.push(step, product)
+
+    @pl.when(step > 0)
+    def _():
+        sums.pull(step - 1, (part_one, part_two), (BACK_BLOCK + half,) * 2, peak_out)
+
+    @pl.when(step == steps)
     def _():
         gain_grad = jnp.zeros((1, width), F32)
         shift_grad = jnp.zeros((1, width), F32)
+        if plan.stepped:
+            exchange.start(0, peak_out[...])
         for start in range(0, rows, ROW_BLOCK):
             at = slice(start, start + ROW_BLOCK)
+            if plan.stepped and start == rows // 2:
+                exchange.start(1, exchange.finish(0))
             grad_second = grad_out[at, :]
             normal = normal_two[at, :]
             grad = normalize_back(grad_second, normal, inverse_two[at, :], norms[2:3, :])
@@ -1070,6 +1224,8 @@
             low_out[at, :] = grad.astype(BF16)
         norm_out[0:1, :] = gain_grad
         norm_out[1:2, :] = shift_grad
+        if plan.stepped:
+            peak_out[...] = exchange.finish(1)
 
 
 def feed_back(
@@ -1091,20 +1247,27 @@
 ):
     rows, width = x.shape
     hidden = wg.shape[-1]
-    chunks = hidden // HIDDEN_BLOCK
+    chunks = hidden // BACK_BLOCK
     steps = plan.tensor * chunks
 
     def locate(i):
-        return i // chunks, lax.rem(i, chunks)
-
-    by_chunk = pl.BlockSpec((rows, HIDDEN_BLOCK), lambda i, place: (0, i))
-    outs = pl.pallas_call(
-        functools.partial(feed_back_body, plan),
+        now = jnp.minimum(i, steps - 1)
+        return now // chunks, lax.rem(now, chunks)
+
+    def locate_late(i):
+        now = jnp.maximum(i - 1, 0)
+        return now // chunks, lax.rem(now, chunks)
+
+    by_chunk = pl.BlockSpec(
+        (rows, BACK_BLOCK), lambda i, place: (0, jnp.minimum(i, steps - 1))
+    )
+    columns = BACK_BLOCK * 3 // 2
+    return pl.pallas_call(
+        functools.partial(feed_back_kernel, plan, steps),
         name="feed_back",
-        out_shape=plan.grad_shapes("yx", hidden)
-        + plan.grad_shapes("xy", hidden)
-        + plan.grad_shapes("xy", hidden)
-        + [
+        out_shape=[
+            plan.grad_shape("yx", columns * chunks),
+            plan.grad_shape("xy", columns * chunks),
             jax.ShapeDtypeStruct((rows, width), F32),
             jax.ShapeDtypeStruct((rows, width), BF16),
             jax.ShapeDtypeStruct((8, width), F32),
@@ -1112,26 +1275,25 @@
         ],
         grid_spec=pltpu.PrefetchScalarGridSpec(
             num_scalar_prefetch=1,
-            grid=(steps,),
+            grid=(steps + 1,),
             in_specs=[
                 whole((1, width)),
                 whole((rows, width)),
                 by_chunk,
                 by_chunk,
                 by_chunk,
-                plan.weight_spec(width, HIDDEN_BLOCK, locate),
-                plan.weight_spec(width, HIDDEN_BLOCK, locate),
-                plan.weight_spec(width, HIDDEN_BLOCK, locate),
+                plan.weight_spec(width, BACK_BLOCK, locate),
+                plan.weight_spec(width, BACK_BLOCK, locate),
+                plan.weight_spec(width, BACK_BLOCK, locate),
                 whole((rows, width)),
                 whole((rows, 1)),
                 whole((rows, width)),
                 whole((rows, 1)),
                 whole(norms.shape),
             ],
-            out_specs=plan.grad_specs("yx", HIDDEN_BLOCK, locate)
-            + plan.grad_specs("xy", HIDDEN_BLOCK, locate)
-            + plan.grad_specs("xy", HIDDEN_BLOCK, locate)
-            + [
+            out_specs=[
+                plan.grad_spec("yx", columns, locate_late),
+                plan.grad_spec("xy", columns, locate_late),
                 result((rows, width)),
                 result((rows, width)),
                 result((8, width)),
@@ -1141,13 +1303,15 @@
                 pltpu.VMEM((rows, width), BF16),
                 pltpu.VMEM((width, rows), BF16),
                 pltpu.VMEM((width, rows), BF16),
-                pltpu.VMEM((rows, 2 * HIDDEN_BLOCK), BF16),
-                pltpu.VMEM((width, 3 * HIDDEN_BLOCK), F32),
-            ],
+                pltpu.VMEM((rows, 2 * BACK_BLOCK), BF16),
+                pltpu.VMEM((width, 3 * BACK_BLOCK), F32),
+            ]
+            + SiblingSum.scratch(plan, 3 * BACK_BLOCK)
+            + (PeakExchange.scratch(plan) if plan.stepped else []),
         ),
-        compiler_params=params(),
+        compiler_params=SiblingSum.params(plan, 6),
         cost_estimate=pl.CostEstimate(
-            flops=12 * rows * width * plan.tensor * hidden,
+            flops=20 * rows * width * plan.tensor * hidden,
             bytes_accessed=rows * width * 60,
             transcendentals=0,
         ),
@@ -1167,57 +1331,25 @@
         inverse_two,
         norms,
     )
-    nc = plan.nc
-    return (outs[:nc], outs[nc : 2 * nc], outs[2 * nc : 3 * nc]) + tuple(outs[3 * nc :])
-
-
-def attend_back_kernel(plan, place, *refs):
-    (
-        ga,
-        x,
-        q,
-        k,
-        v,
-        mixed,
-        log_total,
-        wq,
-        wk,
-        wv,
-        wo,
-        cosine,
-        sine,
-        grad_res,
-        normal_one,
-        inverse_one,
-        norms,
-    ) = refs[:17]
-    nc = plan.nc
-    grads = [refs[17 + n * nc : 17 + (n + 1) * nc] for n in range(4)]
-    low_out, norm_out, peak_out = refs[17 + 4 * nc : 20 + 4 * nc]
-    (
-        ga_turned,
-        x_turned,
-        weights,
-        total_grad,
-        gm,
-        made,
-        key_grad,
-        value_grad,
-        product,
-    ) = refs[20 + 4 * nc :]
-    rows, width = x.shape
-
-    @pl.when(pl.program_id(0) == 0)
-    def _():
-        for start in range(0, rows, ROW_BLOCK):
-            at = slice(start, start + ROW_BLOCK)
-            ga_turned[:, at] = ga[at, :].T
-            x_turned[:, at] = x[at, :].T
-            total_grad[at, :] = grad_res[at, :]
-
-    weights[:, :LANES] = wq[...]
-    weights[:, LANES : 2 * LANES] = wk[...]
-    weights[:, 2 * LANES :] = wv[...]
+
+
+def unfold_feed(part_one, part_two, hidden):
+    rows = part_one.shape[0]
+    half = BACK_BLOCK // 2
+    one = part_one.reshape(rows, hidden // BACK_BLOCK, BACK_BLOCK + half)
+    two = part_two.reshape(rows, hidden // BACK_BLOCK, BACK_BLOCK + half)
+    down = jnp.concatenate([one[:, :, BACK_BLOCK:], two[:, :, BACK_BLOCK:]], axis=2)
+    return (
+        one[:, :, :BACK_BLOCK].reshape(rows, hidden),
+        two[:, :, :BACK_BLOCK].reshape(rows, hidden),
+        down.reshape(rows, hidden),
+    )
+
+
+def heads_back_kernel(
+    place, ga, q, k, v, mixed, log_total, wo, cosine, sine, made, gm, key_grad, value_grad
+):
+    rows = ga.shape[0]
     for start in range(0, rows, ROW_BLOCK):
         at = slice(start, start + ROW_BLOCK)
         gm[at, :] = dot(ga[at, :], wo[...]).astype(BF16)
@@ -1256,135 +1388,228 @@
         grad_key = grad_key * cosine[at, :] - swap_halves(grad_key) * sine[at, :]
         made[at, LANES : 2 * LANES] = grad_key.astype(BF16)
         made[at, 2 * LANES :] = value_grad[at, :].astype(BF16)
-        total_grad[at, :] = total_grad[at, :] + dot_last(made[at, :], weights[...])
-    product[:, : 3 * LANES] = dot(x_turned[...], made[...])
-    product[:, 3 * LANES :] = dot(ga_turned[...], mixed[...])
-    note_peak(peak_out, product)
-    for n in range(4):
-        plan.disperse(place, product, n * LANES, grads[n])
-
-    @pl.when(pl.program_id(0) == pl.num_programs(0) - 1)
+
+
+def heads_back(plan, place, first, number, ga, q, k, v, mixed, log_total, wo, cosine, sine):
+    rows, width = ga.shape
+    pairs = wo.shape[-1] // LANES
+
+    def locate(i):
+        now = first + i
+        return now // pairs, lax.rem(now, pairs)
+
+    by_pair = pl.BlockSpec((None, rows, LANES), lambda i, place: (first + i, 0, 0))
+    return pl.pallas_call(
+        heads_back_kernel,
+        name="heads_back",
+        out_shape=jax.ShapeDtypeStruct((number, rows, 3 * LANES), BF16),
+        grid_spec=pltpu.PrefetchScalarGridSpec(
+            num_scalar_prefetch=1,
+            grid=(number,),
+            in_specs=[
+                whole((rows, width)),
+                by_pair,
+                by_pair,
+                by_pair,
+                pl.BlockSpec((rows, LANES), lambda i, place: (0, first + i)),
+                pl.BlockSpec((None, 8, rows), lambda i, place: (first + i, 0, 0)),
+                plan.weight_spec(width, LANES, locate),
+                whole((rows, LANES)),
+                whole((rows, LANES)),
+            ],
+            out_specs=pl.BlockSpec((None, rows, 3 * LANES), lambda i, place: (i, 0, 0)),
+            scratch_shapes=[
+                pltpu.VMEM((rows, LANES), BF16),
+                pltpu.VMEM((rows, LANES), F32),
+                pltpu.VMEM((rows, LANES), F32),
+            ],
+        ),
+        compiler_params=params(),
+        cost_estimate=pl.CostEstimate(
+            flops=number * 80 * rows * rows * LANES,
+            bytes_accessed=rows * width * 2,
+            transcendentals=0,
+        ),
+    )(place, ga, q, k, v, mixed, log_total, wo, cosine, sine)
+
+
+def first_back_kernel(plan, number, *refs):
+    groups = refs[:number]
+    (wq, wk, wv, grad_res, normal_one, inverse_one, norms, peak) = refs[number : number + 8]
+    low_out, norm_out, peak_out = refs[number + 8 : number + 11]
+    step = pl.program_id(0)
+    if plan.stepped:
+        exchange = PeakExchange(plan, *refs[number + 11 :])
+
+        @pl.when(step == 0)
+        def _():
+            exchange.greet()
+            exchange.start(0, peak[...])
+
+        @pl.when(step == 1)
+        def _():
+            exchange.start(1, exchange.finish(0))
+
+    pairs = wq.shape[-1] // LANES
+    total_grad = grad_res[...]
+    places = [(group, n) for group in groups for n in range(group.shape[0])]
+    for part in range(plan.tensor):
+        for kind, weight in enumerate((wq, wk, wv)):
+            lanes = slice(kind * LANES, (kind + 1) * LANES)
+            made = []
+            for group, n in places[part * pairs : (part + 1) * pairs]:
+                made.append(group[n, :, lanes])
+            total_grad = total_grad + dot_last(jnp.concatenate(made, axis=1), weight[part])
+    normal = normal_one[...]
+    grad = normalize_back(total_grad, normal, inverse_one[...], norms[0:1, :])
+    low_out[...] = grad.astype(BF16)
+    gain_grad = jnp.sum(total_grad * normal, axis=0, keepdims=True)
+    shift_grad = jnp.sum(total_grad, axis=0, keepdims=True)
+
+    @pl.when(pl.program_id(0) == 0)
     def _():
-        gain_grad = jnp.zeros((1, width), F32)
-        shift_grad = jnp.zeros((1, width), F32)
-        for start in range(0, rows, ROW_BLOCK):
-            at = slice(start, start + ROW_BLOCK)
-            grad_first = total_grad[at, :]
-            normal = normal_one[at, :]
-            grad = normalize_back(grad_first, normal, inverse_one[at, :], norms[0:1, :])
-            gain_grad = gain_grad + jnp.sum(grad_first * normal, axis=0, keepdims=True)
-            shift_grad = shift_grad + jnp.sum(grad_first, axis=0, keepdims=True)
-            low_out[at, :] = grad.astype(BF16)
-        norm_out[0:1, :] = gain_grad
-        norm_out[1:2, :] = shift_grad
-
-
-def attend_back(
-    plan,
-    place,
-    ga,
-    x,
-    q,
-    k,
-    v,
-    mixed,
-    log_total,
-    wq,
-    wk,
-    wv,
-    wo,
-    cosine,
-    sine,
-    grad_res,
-    normal_one,
-    inverse_one,
-    norms,
-):
-    rows, width = x.shape
-    part = wq.shape[-1]
-    pairs = part // LANES
-    steps = plan.tensor * pairs
-
-    def locate(i):
-        return i // pairs, lax.rem(i, pairs)
-
-    by_pair = pl.BlockSpec((None, rows, LANES), lambda i, place: (i, 0, 0))
-    orders = ("yx", "xy", "yx", "xy")
-    shapes, specs = [], []
-    for order in orders:
-        shapes += plan.grad_shapes(order, part)
-        specs += plan.grad_specs(order, LANES, locate)
-    outs = pl.pallas_call(
-        functools.partial(attend_back_kernel, plan),
-        name="attend_back",
-        out_shape=shapes
-        + [
+        norm_out[...] = jnp.zeros_like(norm_out)
+
+    norm_out[0:1, :] = norm_out[0:1, :] + gain_grad
+    norm_out[1:2, :] = norm_out[1:2, :] + shift_grad
+    if plan.stepped:
+
+        @pl.when(step == pl.num_programs(0) - 1)
+        def _():
+            peak_out[...] = exchange.finish(1)
+
+
+def first_back(plan, groups, wq, wk, wv, grad_res, normal_one, inverse_one, norms, peak):
+    rows, width = grad_res.shape
+    by_rows = pl.BlockSpec((ROW_BLOCK, width), lambda i: (i, 0))
+
+    def fixed(shape, **more):
+        zeros = (0,) * len(shape)
+        return pl.BlockSpec(shape, lambda i: zeros, **more)
+
+    return pl.pallas_call(
+        functools.partial(first_back_kernel, plan, len(groups)),
+        name="first_back",
+        out_shape=[
             jax.ShapeDtypeStruct((rows, width), BF16),
             jax.ShapeDtypeStruct((8, width), F32),
             jax.ShapeDtypeStruct((8, LANES), F32),
         ],
-        grid_spec=pltpu.PrefetchScalarGridSpec(
-            num_scalar_prefetch=1,
-            grid=(steps,),
-            in_specs=[
-                whole((rows, width)),
-                whole((rows, width)),
-                by_pair,
-                by_pair,
-                by_pair,
-                pl.BlockSpec((rows, LANES), lambda i, place: (0, i)),
-                pl.BlockSpec((None, 8, rows), lambda i, place: (i, 0, 0)),
-            ]
-            + [plan.weight_spec(width, LANES, locate)] * 4
-            + [
-                whole((rows, LANES)),
-                whole((rows, LANES)),
-                whole((rows, width)),
-                whole((rows, width)),
-                whole((rows, 1)),
-                whole(norms.shape),
-            ],
-            out_specs=specs + [result((rows, width)), result((8, width)), result((8, LANES))],
-            scratch_shapes=[
-                pltpu.VMEM((width, rows), BF16),
-                pltpu.VMEM((width, rows), BF16),
-                pltpu.VMEM((width, 3 * LANES), BF16),
-                pltpu.VMEM((rows, width), F32),
-                pltpu.VMEM((rows, LANES), BF16),
-                pltpu.VMEM((rows, 3 * LANES), BF16),
-                pltpu.VMEM((rows, LANES), F32),
-                pltpu.VMEM((rows, LANES), F32),
-                pltpu.VMEM((width, 4 * LANES), F32),
-            ],
+        grid=(rows // ROW_BLOCK,),
+        in_specs=[
+            pl.BlockSpec((g.shape[0], ROW_BLOCK, g.shape[2]), lambda i: (0, i, 0)) for g in groups
+        ]
+        + [fixed(wq.shape, pipeline_mode=pl.Buffered(1))] * 3
+        + [
+            by_rows,
+            by_rows,
+            pl.BlockSpec((ROW_BLOCK, 1), lambda i: (i, 0)),
+            fixed(norms.shape),
+            fixed((8, LANES)),
+        ],
+        out_specs=[by_rows, fixed((8, width)), fixed((8, LANES))],
+        scratch_shapes=PeakExchange.scratch(plan) if plan.stepped else [],
+        compiler_params=(
+            params(collective_id=3, has_side_effects=True) if plan.stepped else params()
         ),
-        compiler_params=params(),
         cost_estimate=pl.CostEstimate(
-            flops=16 * rows * width * width + 40 * rows * rows * width,
-            bytes_accessed=rows * width * 30,
-            transcendentals=0,
+            flops=8 * rows * width * width, bytes_accessed=rows * width * 20, transcendentals=0
         ),
-    )(
-        place,
-        ga,
-        x,
-        q,
-        k,
-        v,
-        mixed,
-        log_total,
-        wq,
-        wk,
-        wv,
-        wo,
-        cosine,
-        sine,
-        grad_res,
-        normal_one,
-        inverse_one,
-        norms,
-    )
-    nc = plan.nc
-    return tuple(outs[n * nc : (n + 1) * nc] for n in range(4)) + tuple(outs[4 * nc :])
+    )(*groups, wq, wk, wv, grad_res, normal_one, inverse_one, norms, peak)
+
+
+def attend_weights_kernel(plan, steps, number, *refs):
+    groups = refs[:number]
+    (x, ga, mixed, part_one, part_two, peak_out, x_turned, ga_turned, product) = refs[
+        number : number + 9
+    ]
+    rows, width = x.shape
+    step = pl.program_id(0)
+    sums = SiblingSum.made_of(plan, steps, refs[number + 9 :])
+
+    @pl.when(step == 0)
+    def _():
+        sums.greet()
+        for start in range(0, rows, ROW_BLOCK):
+            at = slice(start, start + ROW_BLOCK)
+            ga_turned[:, at] = ga[at, :].T
+            x_turned[:, at] = x[at, :].T
+
+    begin = 0
+    for group in groups:
+        size = group.shape[0]
+
+        @pl.when((step >= begin) & (step < begin + size))
+        def _():
+            product[:, : 3 * LANES] = dot(x_turned[...], group[step - begin])
+
+        begin += size
+
+    @pl.when(step < steps)
+    def _():
+        product[:, 3 * LANES :] = dot(ga_turned[...], mixed[...])
+        sums.push(step, product)
+
+    @pl.when(step > 0)
+    def _():
+        sums.pull(step - 1, (part_one, part_two), (2 * LANES,) * 2, peak_out)
+
+
+def attend_weights(plan, groups, x, ga, mixed, part):
+    rows, width = x.shape
+    pairs = part // LANES
+    steps = plan.tensor * pairs
+
+    def late(order):
+        def locate(i):
+            now = jnp.maximum(i - 1, 0)
+            return now // pairs, lax.rem(now, pairs)
+
+        spec = plan.grad_spec(order, 2 * LANES, locate)
+        return pl.BlockSpec(spec.block_shape, lambda i: spec.index_map(i, None))
+
+    def fixed(shape):
+        zeros = (0,) * len(shape)
+        return pl.BlockSpec(shape, lambda i: zeros, pipeline_mode=pl.Buffered(1))
+
+    return pl.pallas_call(
+        functools.partial(attend_weights_kernel, plan, steps, len(groups)),
+        name="attend_weights",
+        out_shape=[
+            plan.grad_shape("yx", 2 * part),
+            plan.grad_shape("xy", 2 * part),
+            jax.ShapeDtypeStruct((8, LANES), F32),
+        ],
+        grid=(steps + 1,),
+        in_specs=[fixed(g.shape) for g in groups]
+        + [
+            fixed((rows, width)),
+            fixed((rows, width)),
+            pl.BlockSpec((rows, LANES), lambda i: (0, jnp.minimum(i, steps - 1))),
+        ],
+        out_specs=[
+            late("yx"),
+            late("xy"),
+            pl.BlockSpec((8, LANES), lambda i: (0, 0)),
+        ],
+        scratch_shapes=[
+            pltpu.VMEM((width, rows), BF16),
+            pltpu.VMEM((width, rows), BF16),
+            pltpu.VMEM((width, 4 * LANES), F32),
+        ]
+        + SiblingSum.scratch(plan, 4 * LANES),
+        compiler_params=SiblingSum.params(plan, 7),
+        cost_estimate=pl.CostEstimate(
+            flops=12 * rows * width * width, bytes_accessed=rows * width * 20, transcendentals=0
+        ),
+    )(*groups, x, ga, mixed)
+
+
+def unfold_attend(part_one, part_two):
+    rows, columns = part_one.shape
+    one = part_one.reshape(rows, columns // (2 * LANES), 2, LANES)
+    two = part_two.reshape(rows, columns // (2 * LANES), 2, LANES)
+    return [side[:, :, n].reshape(rows, columns // 2) for side in (one, two) for n in (0, 1)]
 
 
 def adam_step(weight, first_moment, second_moment, gradient, factor):
@@ -1507,7 +1732,7 @@
     batch_loss, grad_log_scale, grad_pool = contrast(
         plan, place, pool, norm_params, log_inverse_warmth
     )
-    gate_parts, up_parts, down_parts, grad_first_res, attended_low, norm_two, peak_two = feed_back(
+    part_one, part_two, grad_first_res, attended_low, norm_two, peak_two = feed_back(
         plan,
         place,
         grad_pool,
@@ -1525,31 +1750,41 @@
         norm_params,
     )
     scale_two = wire_scale(plan, peak_two)
-    grad_gate = plan.scatter(gate_parts, "yx", scale_two)
-    grad_up = plan.scatter(up_parts, "xy", scale_two)
-    grad_down_own = plan.scatter(down_parts, "xy", scale_two)
-    q_parts, k_parts, v_parts, out_parts, embedded_low, norm_one, peak_one = attend_back(
-        plan,
-        place,
-        attended_low,
-        first_low,
-        q,
-        k,
-        v,
-        mixed,
-        log_total,
-        wq,
-        wk,
-        wv,
-        wo,
-        cosine,
-        sine,
-        grad_first_res,
-        normal_one,
-        inverse_one,
-        norm_params,
+    steps = q.shape[0]
+    cut = steps * 2 // 3
+
+    def heads(first, number, grad):
+        return heads_back(
+            plan, place, first, number, grad, q, k, v, mixed, log_total, wo, cosine, sine
+        )
+
+    if plan.stepped:
+        part_one = plan.step_along(part_one, "y", scale_two)
+        part_two = plan.step_along(part_two, "x", scale_two)
+        group_one = heads(0, cut, attended_low)
+        part_one, part_two, ready = lax.optimization_barrier((part_one, part_two, attended_low))
+        part_one = plan.step_along(part_one, "x", scale_two)
+        part_two = plan.step_along(part_two, "y", scale_two)
+        group_two = heads(cut, steps - cut, ready)
+        part_one, part_two, ready = lax.optimization_barrier((part_one, part_two, attended_low))
+        shard_one = plan.step_along(part_one, "z", scale_two)
+        shard_two = plan.step_along(part_two, "z", scale_two)
+        groups = [group_one, group_two]
+    else:
+        shard_one, shard_two = plan.scatter_whole(part_one), plan.scatter_whole(part_two)
+        groups = [heads(0, steps, attended_low)]
+        ready = attended_low
+    part_three, part_four, peak_one = attend_weights(
+        plan, groups, first_low, ready, mixed, wq.shape[-1]
     )
+    peak_one, shard_one, shard_two = lax.optimization_barrier((peak_one, shard_one, shard_two))
+    embedded_low, norm_one, peak_one = first_back(
+        plan, groups, wq, wk, wv, grad_first_res, normal_one, inverse_one, norm_params, peak_one
+    )
+    scale_one = wire_scale(plan, peak_one)
     grad_rows = summed_rows(slot, embedded_low, slots).astype(BF16)
+    shard_three = plan.scatter(part_three, "yx", scale_one)
+    shard_four = plan.scatter(part_four, "xy", scale_one)
     grad_table = summed_rows(asked.reshape(-1), swap_rows(plan, grad_rows), vocab_shard)
 
     def return_more(turn, sofar):
@@ -1560,26 +1795,13 @@
         )
 
     grad_table = lax.fori_loop(1, rounds, return_more, grad_table)
-    scale_one = wire_scale(plan, peak_one)
-    grad_qkv_own = jnp.stack(
-        [
-            plan.scatter(q_parts, "yx", scale_one),
-            plan.scatter(k_parts, "xy", scale_one),
-            plan.scatter(v_parts, "yx", scale_one),
-        ],
-        axis=1,
-    )
-    grad_out_own = plan.scatter(out_parts, "xy", scale_one)
+    owned_squares = jnp.sum(grad_table * grad_table)
+    for shard in (shard_one, shard_two, shard_three, shard_four):
+        owned_squares = owned_squares + jnp.sum(shard * shard)
+    grad_gate, grad_up, grad_down_own = unfold_feed(shard_one, shard_two, wg.shape[-1])
+    grad_q, grad_k, grad_v, grad_out_own = unfold_attend(shard_three, shard_four)
+    grad_qkv_own = jnp.stack([grad_q, grad_k, grad_v], axis=1)
     grad_gate_own = jnp.stack([grad_gate, grad_up], axis=1)
-
-    owned_squares = (
-        jnp.sum(grad_table * grad_table)
-        + jnp.sum(grad_qkv_own * grad_qkv_own)
-        + jnp.sum(grad_out_own * grad_out_own)
-        + jnp.sum(grad_gate * grad_gate)
-        + jnp.sum(grad_up * grad_up)
-        + jnp.sum(grad_down_own * grad_down_own)
-    )
     length_float = own_length.astype(F32)
     norm_grads, square_total = total(
         plan,

time: 689 us -> 589 us (0.85)
  waiting for transfers between devices: 80.2 us -> 40.9 us
  starting transfers between devices: 67.9 us -> 32.9 us
  Pallas kernels: 386 us -> 371 us
  other arithmetic: 71 us -> 57.8 us
    ppermute x42 -> x20, waiting for transfers between devices: 80.2 us -> 40.9 us  [shift(): return lax.ppermute(values, AXES, pairs)]
    ppermute x42 -> x20, starting transfers between devices: 63.7 us -> 29.2 us  [shift(): return lax.ppermute(values, AXES, pairs)]
    add x21 -> x10, other arithmetic: 22.1 us -> 11.1 us  [step_along(): kept = kept + self.shift(sent, axis, far).astype(F32) / scale]
    pallas_call x1, Pallas kernels: 101 us -> 91.8 us  [attend(): pl.pallas_call(functools.partial(attend_kernel, plan, number), name='atte...]
    unnamed x110 -> x111, local copies, waits for them, and re-layouts: 15.4 us -> 11.4 us
    pallas_call x4 -> x5, Pallas kernels: 142 us -> 141 us  [the longest x1 64.3 us: feed_back(): pl.pallas_call(functools.partial(feed_back_kernel, plan, steps), name='fe...]
  transfers between devices with their start and end apart: 43 -> 21, of which waited for: 20 -> 10; matrix products, arithmetic and copies ran while one was open for 8% -> 5% of each run, Pallas kernels for 3% -> 11%
where the time goes in v3:
time: 589 us; the launch traced here: 579 us
  Pallas kernels  371 us (63%)
  other arithmetic  57.8 us (10%)
  waiting for transfers between devices  40.9 us (7%)
  starting transfers between devices  32.9 us (6%)
  local copies, waits for them, and re-layouts  31.8 us (5%)
  between operations  19.3 us (3%)
  matrix products  15.7 us (3%)
  loops' own time  8.83 us (1%)
    pallas_call x1, Pallas kernels, attend(): pl.pallas_call(functools.partial(attend_kernel, plan, number), name='atte...  91.8 us
    pallas_call x1, Pallas kernels, fetch(): pl.pallas_call(functools.partial(fetch_kernel, plan, orders), name='fetch...  66.2 us
    pallas_call x1, Pallas kernels, feed_back(): pl.pallas_call(functools.partial(feed_back_kernel, plan, steps), name='fe...  64.3 us
    pallas_call x2, Pallas kernels, heads_back(): pl.pallas_call(heads_back_kernel, name='heads_back', out_shape=jax.ShapeD...  44.2 us
    ppermute x20, waiting for transfers between devices, shift(): return lax.ppermute(values, AXES, pairs)  40.9 us
    pallas_call x1, Pallas kernels, feed(): pl.pallas_call(functools.partial(feed_kernel, plan), name='feed', out_sha...  30.8 us
    ppermute x20, starting transfers between devices, shift(): return lax.ppermute(values, AXES, pairs)  29.2 us
    pallas_call x1, Pallas kernels, attend_weights(): pl.pallas_call(functools.partial(attend_weights_kernel, plan, steps, len(...  19.1 us
  transfers between devices with their start and end apart: 21, of which 10 were waited for; matrix products, arithmetic and copies ran while one was open for 5% of the time, Pallas kernels for 11%

profile of v3, /device:TPU:0, one launch (start us, length us, event | category | flops | bytes accessed | tf_op | source)
XLA Modules:
  0.0 578.8 jit_solution(1240846297416123732)
XLA Ops:
  5.5 1.5 convert_reduce_fusion
  12.3 12.2 %swap_blocks.1 = s32[32,8,128]{2,1,0:T(8,128)} custom-call(s32[32,8,128]{2,1,0:T(8,128)} %bitcast.191), custom_call_target="tpu_custom_call" | custom-call | tf_op jit(solution)/shard_map/swap_blocks/pallas_call | solution.py:391
  26.3 2.0 convert_element_type.264
  29.4 2.5 fusion.21
  35.6 66.2 %fetch.1 = (bf16[32,80,384]{2,1,0:T(8,128)(2,1)}, bf16[2,4,2,2,48,384]{5,4,3,2,1,0:T(8,128)(2,1)}, bf16[2,4,2,2,48,384]{5,4,3,2,1,0:T(8,128)(2,1)}, bf16[2,4,2,2...) custom-call(bf16[32,80,384]{2,1,0:T(8,128)(2,1)} %pad_maximum_fusion.rows_ref, ...), custom_call_target="tpu_custom_call" | custom-call | tf_op jit(solution)/shard_map/fetch/pallas_call | solution.py:610
  101.8 1.8 fusion.88
  105.9 4.1 fusion.14
  110.1 1.9 fusion.51
  112.0 1.8 pad_maximum_fusion.2
  115.1 8.0 %while.20 = (s32[]{:T(128)}, f32[1024,768]{1,0:T(8,128)}, s32[]{:T(128)}, s32[1024]{0:T(1024)S(1)}, s32[1024]{0:T(1024)S(1)}, /*index=5*/pred[1024]{0:T(1024)(12...) while((s32[]{:T(128)}, f32[1024,768]{1,0:T(8,128)}, ...), condition=%wide.region_7.8_spmd, body=%wide.region_5.7_spmd.sunk | while | flops 3910260480 | bytes 17673384 | solution.py:1708
  123.1 91.8 %attend.1 = (bf16[6,1024,128]{2,1,0:T(8,128)(2,1)}, bf16[6,1024,128]{2,1,0:T(8,128)(2,1)}, bf16[6,1024,128]{2,1,0:T(8,128)(2,1)}, bf16[1024,768]{1,0:T(8,128)(2,...) custom-call(s32[5]{0:T(128)} %stack.26.place, ...), custom_call_target="tpu_custom_call" | custom-call | flops 17716740096 | bytes 23592960 | tf_op jit(solution)/shard_map/attend/pallas_call | solution.py:895
  214.9 30.8 %feed.1 = (bf16[1024,3072]{1,0:T(8,128)(2,1)}, bf16[1024,3072]{1,0:T(8,128)(2,1)}, bf16[1024,3072]{1,0:T(8,128)(2,1)}, f32[1024,768]{1,0:T(8,128)}, f32[1024,1]{1,0:T(8,128)}, /*index=5*/f32[1,768]{1,0:T(1,128)}) custom-call(s32[5]{0:T(128)} %stack.26.place, bf16[1024,768]{1,0:T(8,128)(2,1)} %get-tuple-element.163.x.refs_1_, ...), custom_call_target="tpu_custom_call" | custom-call | flops 14495514624 | bytes 31457280 | tf_op jit(solution)/shard_map/feed/pallas_call | solution.py:1000
  245.7 11.3 %contrast.1 = (f32[1,128]{1,0:T(1,128)}, f32[1,768]{1,0:T(1,128)}) custom-call(s32[5]{0:T(128)} %stack.26.place, f32[1,768]{1,0:T(1,128)} %get-tuple-element.168.pool_ref, f32[6,768]{1,0:T(8,128)} %refs_8_.1, f32[1,1]{1,0:T(1,128)} %bitcast.181.scale_ref), custom_call_target="tpu_custom_call" | custom-call | tf_op jit(solution)/shard_map/contrast/pallas_call | solution.py:1106
  257.0 64.3 %feed_back.1 = (f32[2,2,4,48,2304]{4,3,2,1,0:T(8,128)}, f32[2,2,4,48,2304]{4,3,2,1,0:T(8,128)}, f32[1024,768]{1,0:T(8,128)}, bf16[1024,768]{1,0:T(8,128)(2,1)}, f32[8,768]{1,0:T(8,128)}, /*index=5*/f32[8,128]{1,0:T(8,128)}) custom-call(s32[5]{0:T(128)} %stack.26.place, f32[1,768]{1,0:T(1,128)} %get-tuple-element.170.refs_0_, ...), custom_call_target="tpu_custom_call" | custom-call | flops 48318382080 | bytes 47185920 | tf_op jit(solution)/shard_map/feed_back/pallas_call | solution.py:1265
  323.2 2.3 fusion.28
  325.5 1.5 collective-permute-start.1
  327.1 3.5 fusion.27
  331.2 28.0 %heads_back.2.refs_0_ = bf16[4,1024,384]{2,1,0:T(8,128)(2,1)} custom-call(s32[5]{0:T(128)} %stack.26.place, bf16[1024,768]{1,0:T(8,128)(2,1)} %get-tuple-element.193.ga.refs_3_, bf16[6,1024,128]{2,1,0:T(8,128)(2,1)} %get-tuple-element.178.q, bf16[6,1024,128]{2,1,0:T(8,128)(2,1)} %get-tuple-element.179.k, bf16[6,1024,128]{2,1,0:T(8,128)(2,1)} %get-tuple-element.180.v, ...), custom_call_target="tpu_custom_call" | custom-call | flops 42949672960 | bytes 1572864 | tf_op jit(solution)/shard_map/heads_back/pallas_call | solution.py:1402
  359.2 6.3 %collective-permute-done.1 = f16[2,4,48,2304]{3,2,1,0:T(8,128)(2,1)} collective-permute-done((f16[2,4,48,2304]{3,2,1,0:T(8,128)(2,1)S(1)}, f16[2,4,48,2304]{3,2,1,0:T(8,128)(2,1)}, u32[]{:S(2)}, u32[]{:S(2)}) %collective-permute-start.1) | collective-permute-done | bytes 1769504 | tf_op jit(solution)/shard_map/ppermute | solution.py:68
  365.5 2.9 bitcast_add_fusion
  368.4 1.9 collective-permute-done
  370.2 2.5 bitcast_add_fusion.1
  376.1 16.2 %heads_back.3.refs_1_ = bf16[2,1024,384]{2,1,0:T(8,128)(2,1)} custom-call(s32[5]{0:T(128)} %stack.26.place, bf16[1024,768]{1,0:T(8,128)(2,1)} %get-tuple-element.193.ga.refs_3_, bf16[6,1024,128]{2,1,0:T(8,128)(2,1)} %get-tuple-element.178.q, bf16[6,1024,128]{2,1,0:T(8,128)(2,1)} %get-tuple-element.179.k, bf16[6,1024,128]{2,1,0:T(8,128)(2,1)} %get-tuple-element.180.v, ...), custom_call_target="tpu_custom_call" | custom-call | flops 21474836480 | bytes 1572864 | tf_op jit(solution)/shard_map/heads_back/pallas_call | solution.py:1402
  392.7 1.6 bitcast_add_fusion.2
  396.4 2.4 collective-permute-start.8
  401.9 19.1 %attend_weights.1 = (f32[2,2,4,48,768]{4,3,2,1,0:T(8,128)}, f32[2,2,4,48,768]{4,3,2,1,0:T(8,128)}, f32[8,128]{1,0:T(8,128)}) custom-call(bf16[4,1024,384]{2,1,0:T(8,128)(2,1)} %heads_back.2.refs_0_, bf16[2,1024,384]{2,1,0:T(8,128)(2,1)} %heads_back.3.refs_1_, bf16[1024,768]{1,0:T(8,128)(2,1)} %get-tuple-element.190.refs_2_, ...), custom_call_target="tpu_custom_call" | custom-call | flops 7247757312 | bytes 15728640 | tf_op jit(solution)/shard_map/attend_weights/pallas_call | solution.py:1575
  420.9 2.9 collective-permute-start.6
  425.0 5.9 %collective-permute-done.5 = f16[48,2304]{1,0:T(8,128)(2,1)S(1)} collective-permute-done((f16[48,2304]{1,0:T(8,128)(2,1)S(1)}, f16[48,2304]{1,0:T(8,128)(2,1)S(1)}, u32[]{:S(2)}, u32[]{:S(2)}) %collective-permute-start.5) | collective-permute-done | bytes 221216 | tf_op jit(solution)/shard_map/ppermute | solution.py:68
  430.8 3.4 collective-permute-done.6
  434.4 13.9 %first_back.1 = (bf16[1024,768]{1,0:T(8,128)(2,1)S(1)}, f32[8,768]{1,0:T(8,128)}, f32[8,128]{1,0:T(8,128)}) custom-call(bf16[4,1024,384]{2,1,0:T(8,128)(2,1)} %heads_back.2.refs_0_, bf16[2,1024,384]{2,1,0:T(8,128)(2,1)} %heads_back.3.refs_1_, bf16[2,768,384]{2,1,0:T(8,128)(2,1)} %bitcast.210, bf16[2,768,384]{2,1,0:T(8,128)(2,1)} %bitcast.212, ...), custom_call_target="tpu_custom_call" | custom-call | flops 4831838208 | bytes 15728640 | tf_op jit(solution)/shard_map/first_back/pallas_call | solution.py:1490
  448.3 3.7 fusion.20
  452.0 3.6 all-to-all-start.4
  459.9 1.6 collective-permute-start.15
  464.7 2.2 fusion.32
  472.0 1.8 slice.230
  474.7 1.9 stack_reshape.7
  477.3 11.5 %collective-permute-done.15 = f16[2,4,48,768]{3,2,1,0:T(8,128)(2,1)} collective-permute-done((f16[2,4,48,768]{3,2,1,0:T(8,128)(2,1)}, f16[2,4,48,768]{3,2,1,0:T(8,128)(2,1)}, u32[]{:S(2)}, u32[]{:S(2)}) %collective-permute-start.15) | collective-permute-done | bytes 589856 | tf_op jit(solution)/shard_map/ppermute | solution.py:68
  490.2 2.2 collective-permute-start.16
  494.9 6.3 %collective-permute-done.16 = f16[4,48,768]{2,1,0:T(8,128)(2,1)S(1)} collective-permute-done((f16[4,48,768]{2,1,0:T(8,128)(2,1)S(1)}, f16[4,48,768]{2,1,0:T(8,128)(2,1)S(1)}, u32[]{:S(2)}, u32[]{:S(2)}) %collective-permute-start.16) | collective-permute-done | bytes 294944 | tf_op jit(solution)/shard_map/ppermute | solution.py:68
  501.3 2.7 collective-permute-start.17
  504.1 2.0 collective-permute-start.18
  506.0 1.7 collective-permute-start.19
  509.2 2.5 collective-permute-start.14
  514.6 2.8 collective-permute-done.13
  520.0 5.4 fusion.18
  526.4 3.3 multiply_reduce_fusion
  533.7 17.8 %total.1 = f32[32,8,128]{2,1,0:T(8,128)} custom-call(f32[32,8,128]{2,1,0:T(8,128)} %bitcast.193), custom_call_target="tpu_custom_call" | custom-call | tf_op jit(solution)/shard_map/total/pallas_call | solution.py:440
  561.8 8.7 %add_multiply_fusion = (f32[960,768]{1,0:T(8,128)}, f32[960,768]{1,0:T(8,128)}, f32[960,768]{1,0:T(8,128)}) fusion(f32[960,768]{1,0:T(8,128)S(1)} %copy-done.4, f32[960,768]{1,0:T(8,128)} %get-tuple-element.201, f32[]{:T(128)S(6)} %min_shard_map.3, f32[960,768]{1,0:T(8,128)} %param.31, f32[960,768]{1,0:T(8,128)} %param.30), kind=kLoop, calls=%fused_computation.47 | loop fusion | flops 11059200 | bytes 20643844 | tf_op jit(solution)/shard_map/mul | solution.py:1621
  (217 shorter events, 63.3 us)
Async XLA Ops:
  35.6 68.0 %copy-start.5 = (f32[48,2,1536]{2,1,0:T(2,128)S(1)}, f32[48,2,1536]{2,1,0:T(2,128)}, u32[]{:S(2)}) copy-start(f32[48,2,1536]{2,1,0:T(2,128)} %param.38) | copy-start | bytes 1769476
  123.0 91.8 %copy-start.18 = (s32[1024]{0:T(1024)}, s32[1024]{0:T(1024)S(1)}, u32[]{:S(2)}) copy-start(s32[1024]{0:T(1024)S(1)} %get-tuple-element.550) | copy-start | bytes 12292
  123.1 91.8 %copy-start.21 = (s32[1024]{0:T(1024)}, s32[1024]{0:T(1024)S(1)}, u32[]{:S(2)}) copy-start(s32[1024]{0:T(1024)S(1)} %get-tuple-element.551) | copy-start | bytes 12292
  123.1 91.8 %copy-start.41 = (s32[1024]{0:T(1024)}, s32[1024]{0:T(1024)S(1)}, u32[]{:S(2)}) copy-start(s32[1024]{0:T(1024)S(1)} %get-tuple-element.579) | copy-start | bytes 12292
  123.1 91.8 %copy-start.47 = (pred[1024]{0:T(1024)(128)(4,1)}, pred[1024]{0:T(1024)(128)(4,1)S(1)}, u32[]{:S(2)}) copy-start(pred[1024]{0:T(1024)(128)(4,1)S(1)} %get-tuple-element.580) | copy-start | bytes 3076
  325.5 39.9 %collective-permute-start.1 = (f16[2,4,48,2304]{3,2,1,0:T(8,128)(2,1)S(1)}, f16[2,4,48,2304]{3,2,1,0:T(8,128)(2,1)}, u32[]{:S(2)}, u32[]{:S(2)}) collective-permute-start(f16[2,4,48,2304]{3,2,1,0:T(8,128)(2,1)S(1)} %fusion.28), channel_id=1, source_target_pairs={{0,4},{1,5},{2,6},{3,7},{4,0},{5,1},{6,2},{7,3},{8,12},{9,13},{10,... | collective-permute-start | bytes 5308424 | tf_op jit(solution)/shard_map/ppermute | solution.py:68
  330.6 39.7 %collective-permute-start = (f16[2,4,48,2304]{3,2,1,0:T(8,128)(2,1)}, f16[2,4,48,2304]{3,2,1,0:T(8,128)(2,1)S(1)}, u32[]{:S(2)}, u32[]{:S(2)}) collective-permute-start(f16[2,4,48,2304]{3,2,1,0:T(8,128)(2,1)} %fusion.27), channel_id=1, source_target_pairs={{0,1},{1,0},{2,3},{3,2},{4,5},{5,4},{6,7},{7,6},{8,9},{9,8},{10,11... | collective-permute-start | bytes 5308424 | tf_op jit(solution)/shard_map/ppermute | solution.py:68
  372.9 19.8 %collective-permute-start.3 = (f16[4,48,2304]{2,1,0:T(8,128)(2,1)S(1)}, f16[4,48,2304]{2,1,0:T(8,128)(2,1)}, u32[]{:S(2)}, u32[]{:S(2)}) collective-permute-start(f16[4,48,2304]{2,1,0:T(8,128)(2,1)S(1)} %fusion.30), channel_id=1, source_target_pairs={{0,1},{1,0},{2,3},{3,2},{4,5},{5,4},{6,7},{7,6},{8,9},{9,8},{10,11... | collective-permute-start | bytes 2654216 | tf_op jit(solution)/shard_map/ppermute | solution.py:68
  375.6 19.8 %collective-permute-start.2 = (f16[4,48,2304]{2,1,0:T(8,128)(2,1)}, f16[4,48,2304]{2,1,0:T(8,128)(2,1)S(1)}, u32[]{:S(2)}, u32[]{:S(2)}) collective-permute-start(f16[4,48,2304]{2,1,0:T(8,128)(2,1)} %fusion.29), channel_id=1, source_target_pairs={{0,4},{1,5},{2,6},{3,7},{4,0},{5,1},{6,2},{7,3},{8,12},{9,13},{10,... | collective-permute-start | bytes 2654216 | tf_op jit(solution)/shard_map/ppermute | solution.py:68
  395.7 25.2 %collective-permute-start.7 = (f16[48,2304]{1,0:T(8,128)(2,1)S(1)}, f16[48,2304]{1,0:T(8,128)(2,1)S(1)}, u32[]{:S(2)}, u32[]{:S(2)}) collective-permute-start(f16[48,2304]{1,0:T(8,128)(2,1)S(1)} %get-tuple-element.347), channel_id=1, source_target_pairs={{0,8},{1,9},{2,10},{3,11},{4,12},{5,13},{6,14},{7,15},{8,16},{9,17... | collective-permute-start | bytes 663560 | tf_op jit(solution)/shard_map/ppermute | solution.py:68
  396.4 27.5 %collective-permute-start.8 = (f16[48,2304]{1,0:T(8,128)(2,1)S(1)}, f16[48,2304]{1,0:T(8,128)(2,1)S(1)}, u32[]{:S(2)}, u32[]{:S(2)}) collective-permute-start(f16[48,2304]{1,0:T(8,128)(2,1)S(1)} %get-tuple-element.349), channel_id=1, source_target_pairs={{0,16},{1,17},{2,18},{3,19},{4,20},{5,21},{6,22},{7,23},{8,24},{9,... | collective-permute-start | bytes 663560 | tf_op jit(solution)/shard_map/ppermute | solution.py:68
  398.8 25.1 %collective-permute-start.9 = (f16[48,2304]{1,0:T(8,128)(2,1)S(1)}, f16[48,2304]{1,0:T(8,128)(2,1)}, u32[]{:S(2)}, u32[]{:S(2)}) collective-permute-start(f16[48,2304]{1,0:T(8,128)(2,1)S(1)} %get-tuple-element.348), channel_id=1, source_target_pairs={{0,24},{1,25},{2,26},{3,27},{4,28},{5,29},{6,30},{7,31},{8,0},{9,1... | collective-permute-start | bytes 663560 | tf_op jit(solution)/shard_map/ppermute | solution.py:68
  400.3 24.6 %collective-permute-start.4 = (f16[48,2304]{1,0:T(8,128)(2,1)S(1)}, f16[48,2304]{1,0:T(8,128)(2,1)S(1)}, u32[]{:S(2)}, u32[]{:S(2)}) collective-permute-start(f16[48,2304]{1,0:T(8,128)(2,1)S(1)} %get-tuple-element.350), channel_id=1, source_target_pairs={{0,8},{1,9},{2,10},{3,11},{4,12},{5,13},{6,14},{7,15},{8,16},{9,17... | collective-permute-start | bytes 663560 | tf_op jit(solution)/shard_map/ppermute | solution.py:68
  401.0 29.8 %collective-permute-start.5 = (f16[48,2304]{1,0:T(8,128)(2,1)S(1)}, f16[48,2304]{1,0:T(8,128)(2,1)S(1)}, u32[]{:S(2)}, u32[]{:S(2)}) collective-permute-start(f16[48,2304]{1,0:T(8,128)(2,1)S(1)} %get-tuple-element.352), channel_id=1, source_target_pairs={{0,16},{1,17},{2,18},{3,19},{4,20},{5,21},{6,22},{7,23},{8,24},{9,... | collective-permute-start | bytes 663560 | tf_op jit(solution)/shard_map/ppermute | solution.py:68
  420.9 13.3 %collective-permute-start.6 = (f16[48,2304]{1,0:T(8,128)(2,1)S(1)}, f16[48,2304]{1,0:T(8,128)(2,1)S(1)}, u32[]{:S(2)}, u32[]{:S(2)}) collective-permute-start(f16[48,2304]{1,0:T(8,128)(2,1)S(1)} %get-tuple-element.351), channel_id=1, source_target_pairs={{0,24},{1,25},{2,26},{3,27},{4,28},{5,29},{6,30},{7,31},{8,0},{9,1... | collective-permute-start | bytes 663560 | tf_op jit(solution)/shard_map/ppermute | solution.py:68
  434.4 13.9 %copy-start.44 = (s32[1,1024]{1,0:T(1,128)S(1)}, s32[1,1024]{1,0:T(1,128)}, u32[]{:S(2)}) copy-start(s32[1,1024]{1,0:T(1,128)} %copy-done.43) | copy-start | bytes 12292
  452.0 9.5 %copy-start.46 = (f32[1,128]{1,0:T(1,128)S(1)}, f32[1,128]{1,0:T(1,128)}, u32[]{:S(2)}) copy-start(f32[1,128]{1,0:T(1,128)} %get-tuple-element.169) | copy-start | bytes 1540
  452.0 68.0 %all-to-all-start.4 = ((bf16[32,40,768]{2,1,0:T(8,128)(2,1)}), bf16[32,40,768]{2,1,0:T(8,128)(2,1)}, u32[]{:S(2)}, u32[]{:S(2)}) async-start(bf16[32,40,768]{2,1,0:T(8,128)(2,1)} %bitcast.187), calls=%async_computation.4 | async-start | bytes 3932160 | tf_op jit(solution)/shard_map/all_to_all | solution.py:743
  459.9 28.9 %collective-permute-start.15 = (f16[2,4,48,768]{3,2,1,0:T(8,128)(2,1)}, f16[2,4,48,768]{3,2,1,0:T(8,128)(2,1)}, u32[]{:S(2)}, u32[]{:S(2)}) collective-permute-start(f16[2,4,48,768]{3,2,1,0:T(8,128)(2,1)} %fusion.33), channel_id=1, source_target_pairs={{0,4},{1,5},{2,6},{3,7},{4,0},{5,1},{6,2},{7,3},{8,12},{9,13},{10,... | collective-permute-start | bytes 1769480 | tf_op jit(solution)/shard_map/ppermute | solution.py:68
  466.9 25.5 %collective-permute-start.10 = (f16[2,4,48,768]{3,2,1,0:T(8,128)(2,1)}, f16[2,4,48,768]{3,2,1,0:T(8,128)(2,1)}, u32[]{:S(2)}, u32[]{:S(2)}) collective-permute-start(f16[2,4,48,768]{3,2,1,0:T(8,128)(2,1)} %fusion.32), channel_id=1, source_target_pairs={{0,1},{1,0},{2,3},{3,2},{4,5},{5,4},{6,7},{7,6},{8,9},{9,8},{10,11... | collective-permute-start | bytes 1769480 | tf_op jit(solution)/shard_map/ppermute | solution.py:68
  476.6 15.7 %copy-start.8 = (f32[2,2,4,48,768]{4,3,2,1,0:T(8,128)S(1)}, f32[2,2,4,48,768]{4,3,2,1,0:T(8,128)}, u32[]{:S(2)}) copy-start(f32[2,2,4,48,768]{4,3,2,1,0:T(8,128)} %get-tuple-element.204) | copy-start | bytes 7077892
  490.2 11.1 %collective-permute-start.16 = (f16[4,48,768]{2,1,0:T(8,128)(2,1)S(1)}, f16[4,48,768]{2,1,0:T(8,128)(2,1)S(1)}, u32[]{:S(2)}, u32[]{:S(2)}) collective-permute-start(f16[4,48,768]{2,1,0:T(8,128)(2,1)S(1)} %fusion.42), channel_id=1, source_target_pairs={{0,1},{1,0},{2,3},{3,2},{4,5},{5,4},{6,7},{7,6},{8,9},{9,8},{10,11... | collective-permute-start | bytes 884744 | tf_op jit(solution)/shard_map/ppermute | solution.py:68
  493.6 26.3 %copy-start.40 = (s32[1280]{0:T(1024)S(1)}, s32[1280]{0:T(1024)}, u32[]{:S(2)}) copy-start(s32[1280]{0:T(1024)} %copy-done.39) | copy-start | bytes 15364
  493.7 14.1 %collective-permute-start.11 = (f16[4,48,768]{2,1,0:T(8,128)(2,1)S(1)}, f16[4,48,768]{2,1,0:T(8,128)(2,1)S(1)}, u32[]{:S(2)}, u32[]{:S(2)}) collective-permute-start(f16[4,48,768]{2,1,0:T(8,128)(2,1)S(1)} %fusion.43), channel_id=1, source_target_pairs={{0,4},{1,5},{2,6},{3,7},{4,0},{5,1},{6,2},{7,3},{8,12},{9,13},{10,... | collective-permute-start | bytes 884744 | tf_op jit(solution)/shard_map/ppermute | solution.py:68
  501.3 7.9 %collective-permute-start.17 = (f16[48,768]{1,0:T(8,128)(2,1)S(1)}, f16[48,768]{1,0:T(8,128)(2,1)S(1)}, u32[]{:S(2)}, u32[]{:S(2)}) collective-permute-start(f16[48,768]{1,0:T(8,128)(2,1)S(1)} %get-tuple-element.353), channel_id=1, source_target_pairs={{0,8},{1,9},{2,10},{3,11},{4,12},{5,13},{6,14},{7,15},{8,16},{9,17... | collective-permute-start | bytes 221192 | tf_op jit(solution)/shard_map/ppermute | solution.py:68
  504.1 7.7 %collective-permute-start.18 = (f16[48,768]{1,0:T(8,128)(2,1)S(1)}, f16[48,768]{1,0:T(8,128)(2,1)S(1)}, u32[]{:S(2)}, u32[]{:S(2)}) collective-permute-start(f16[48,768]{1,0:T(8,128)(2,1)S(1)} %get-tuple-element.355), channel_id=1, source_target_pairs={{0,16},{1,17},{2,18},{3,19},{4,20},{5,21},{6,22},{7,23},{8,24},{9,... | collective-permute-start | bytes 221192 | tf_op jit(solution)/shard_map/ppermute | solution.py:68
  506.0 5.7 collective-permute-start.19
  507.9 6.7 %collective-permute-start.12 = (f16[48,768]{1,0:T(8,128)(2,1)S(1)}, f16[48,768]{1,0:T(8,128)(2,1)S(1)}, u32[]{:S(2)}, u32[]{:S(2)}) collective-permute-start(f16[48,768]{1,0:T(8,128)(2,1)S(1)} %get-tuple-element.356), channel_id=1, source_target_pairs={{0,8},{1,9},{2,10},{3,11},{4,12},{5,13},{6,14},{7,15},{8,16},{9,17... | collective-permute-start | bytes 221192 | tf_op jit(solution)/shard_map/ppermute | solution.py:68
  508.3 9.2 %collective-permute-start.13 = (f16[48,768]{1,0:T(8,128)(2,1)S(1)}, f16[48,768]{1,0:T(8,128)(2,1)S(1)}, u32[]{:S(2)}, u32[]{:S(2)}) collective-permute-start(f16[48,768]{1,0:T(8,128)(2,1)S(1)} %get-tuple-element.358), channel_id=1, source_target_pairs={{0,16},{1,17},{2,18},{3,19},{4,20},{5,21},{6,22},{7,23},{8,24},{9,... | collective-permute-start | bytes 221192 | tf_op jit(solution)/shard_map/ppermute | solution.py:68
  509.2 8.2 %collective-permute-start.14 = (f16[48,768]{1,0:T(8,128)(2,1)S(1)}, f16[48,768]{1,0:T(8,128)(2,1)S(1)}, u32[]{:S(2)}, u32[]{:S(2)}) collective-permute-start(f16[48,768]{1,0:T(8,128)(2,1)S(1)} %get-tuple-element.357), channel_id=1, source_target_pairs={{0,24},{1,25},{2,26},{3,27},{4,28},{5,29},{6,30},{7,31},{8,0},{9,1... | collective-permute-start | bytes 221192 | tf_op jit(solution)/shard_map/ppermute | solution.py:68
  526.3 30.1 %slice-start = ((f32[48,3,768]{2,1,0:T(4,128)}), f32[48,3,256]{2,1,0:T(4,128)S(1)}, s32[]{:S(2)}) async-start(f32[48,3,768]{2,1,0:T(4,128)} %reshape.356), calls=%async_computation.5 | async-start | bytes 393216 | tf_op jit(solution)/shard_map/slice | solution.py:1341
  526.3 30.1 %slice-start.2 = ((f32[48,3,768]{2,1,0:T(4,128)}), f32[48,3,256]{2,1,0:T(4,128)S(1)}, s32[]{:S(2)}) async-start(f32[48,3,768]{2,1,0:T(4,128)} %reshape.357), calls=%async_computation.7 | async-start | bytes 393216 | tf_op jit(solution)/shard_map/slice | solution.py:1341
  526.3 30.2 %copy-start.6 = (f32[48,2,1536]{2,1,0:T(2,128)S(1)}, f32[48,2,1536]{2,1,0:T(2,128)}, u32[]{:S(2)}) copy-start(f32[48,2,1536]{2,1,0:T(2,128)} %param.38) | copy-start | bytes 1769476
  526.4 30.2 %copy-start.11 = (f32[48,1,1536]{2,0,1:T(8,128)S(1)}, f32[48,1,1536]{2,0,1:T(8,128)}, u32[]{:S(2)}) copy-start(f32[48,1,1536]{2,0,1:T(8,128)} %stack_reshape.7) | copy-start | bytes 884740
  526.4 30.2 %copy-start.16 = (f32[48,2,1536]{2,1,0:T(2,128)S(1)}, f32[48,2,1536]{2,1,0:T(2,128)}, u32[]{:S(2)}) copy-start(f32[48,2,1536]{2,1,0:T(2,128)} %param.40) | copy-start | bytes 1769476
  526.4 30.2 %copy-start.17 = (f32[48,2,1536]{2,1,0:T(2,128)S(1)}, f32[48,2,1536]{2,1,0:T(2,128)}, u32[]{:S(2)}) copy-start(f32[48,2,1536]{2,1,0:T(2,128)} %param.39) | copy-start | bytes 1769476
  561.6 9.5 %copy-start.13 = (f32[48,1536]{1,0:T(8,128)S(1)}, f32[48,1536]{1,0:T(8,128)}, u32[]{:S(2)}) copy-start(f32[48,1536]{1,0:T(8,128)} %param.41) | copy-start | bytes 884740
  561.6 9.5 %copy-start.27 = (f32[48,1536]{1,0:T(8,128)S(1)}, f32[48,1536]{1,0:T(8,128)}, u32[]{:S(2)}) copy-start(f32[48,1536]{1,0:T(8,128)} %param.43) | copy-start | bytes 884740
  561.7 9.5 %copy-start.28 = (f32[48,1536]{1,0:T(8,128)S(1)}, f32[48,1536]{1,0:T(8,128)}, u32[]{:S(2)}) copy-start(f32[48,1536]{1,0:T(8,128)} %param.42) | copy-start | bytes 884740
  561.7 10.5 %copy-start.26 = (f32[48,384]{1,0:T(8,128)S(1)}, f32[48,384]{1,0:T(8,128)}, u32[]{:S(2)}) copy-start(f32[48,384]{1,0:T(8,128)} %param.35) | copy-start | bytes 221188
  561.7 10.5 %copy-start.34 = (f32[48,384]{1,0:T(8,128)S(1)}, f32[48,384]{1,0:T(8,128)}, u32[]{:S(2)}) copy-start(f32[48,384]{1,0:T(8,128)} %param.37) | copy-start | bytes 221188
  561.7 10.5 %copy-start.35 = (f32[48,384]{1,0:T(8,128)S(1)}, f32[48,384]{1,0:T(8,128)}, u32[]{:S(2)}) copy-start(f32[48,384]{1,0:T(8,128)} %param.36) | copy-start | bytes 221188
  561.7 11.2 %copy-start.15 = (f32[48,3,384]{2,0,1:T(8,128)S(1)}, f32[48,3,384]{2,0,1:T(8,128)}, u32[]{:S(2)}) copy-start(f32[48,3,384]{2,0,1:T(8,128)} %param.32) | copy-start | bytes 663556
  561.7 11.2 %copy-start.23 = (f32[48,1,384]{2,0,1:T(8,128)S(1)}, f32[48,1,384]{2,0,1:T(8,128)}, u32[]{:S(2)}) copy-start(f32[48,1,384]{2,0,1:T(8,128)} %stack_reshape_squeeze.10) | copy-start | bytes 221188
  561.7 11.2 %copy-start.24 = (f32[48,1,384]{2,0,1:T(8,128)S(1)}, f32[48,1,384]{2,0,1:T(8,128)}, u32[]{:S(2)}) copy-start(f32[48,1,384]{2,0,1:T(8,128)} %stack_reshape_squeeze.9) | copy-start | bytes 221188
  561.7 11.1 %copy-start.29 = (f32[48,3,384]{2,0,1:T(8,128)S(1)}, f32[48,3,384]{2,0,1:T(8,128)}, u32[]{:S(2)}) copy-start(f32[48,3,384]{2,0,1:T(8,128)} %param.34) | copy-start | bytes 663556
  561.8 11.1 %copy-start.30 = (f32[48,3,384]{2,0,1:T(8,128)S(1)}, f32[48,3,384]{2,0,1:T(8,128)}, u32[]{:S(2)}) copy-start(f32[48,3,384]{2,0,1:T(8,128)} %param.33) | copy-start | bytes 663556
  561.8 12.1 %copy-start.1 = (s32[1,2]{1,0:T(1,128)S(1)}, s32[1,2]{1,0:T(1,128)}, u32[]{:S(2)}) copy-start(s32[1,2]{1,0:T(1,128)} %param.28) | copy-start | bytes 28
  (26 other events, 119.9 us)

commit v4 on v3

--- a/solution.py
+++ b/solution.py
@@ -1705,7 +1705,12 @@
         later, later_asked = ask(turn)
         return sofar + spread_rows(later, swap_rows(plan, picked_rows(later_asked, table_low)))
 
-    embedded = lax.fori_loop(1, rounds, fetch_more, embedded)
+    embedded = lax.cond(
+        rounds > 1,
+        lambda sofar: lax.fori_loop(1, rounds, fetch_more, sofar),
+        lambda sofar: sofar,
+        embedded,
+    )
     cosine, sine = rotary_tables(rows)
     made, gathered = attend(
         plan,

time: 589 us -> 584 us (level)
  transfers between devices with their start and end apart: 21 -> 21, of which waited for: 10 -> 10; matrix products, arithmetic and copies ran while one was open for 5% -> 6% of each run, Pallas kernels for 11% -> 11%
where the time goes in v4:
time: 584 us; the launch traced here: 575 us
  Pallas kernels  372 us (64%)
  other arithmetic  58 us (10%)
  waiting for transfers between devices  40.8 us (7%)
  starting transfers between devices  32.9 us (6%)
  local copies, waits for them, and re-layouts  31.8 us (5%)
  between operations  20.1 us (3%)
  matrix products  15.6 us (3%)
    pallas_call x1, Pallas kernels, attend(): pl.pallas_call(functools.partial(attend_kernel, plan, number), name='atte...  92.1 us
    pallas_call x1, Pallas kernels, fetch(): pl.pallas_call(functools.partial(fetch_kernel, plan, orders), name='fetch...  66.2 us
    pallas_call x1, Pallas kernels, feed_back(): pl.pallas_call(functools.partial(feed_back_kernel, plan, steps), name='fe...  64.3 us
    pallas_call x2, Pallas kernels, heads_back(): pl.pallas_call(heads_back_kernel, name='heads_back', out_shape=jax.ShapeD...  44.1 us
    ppermute x20, waiting for transfers between devices, shift(): return lax.ppermute(values, AXES, pairs)  40.8 us
    pallas_call x1, Pallas kernels, feed(): pl.pallas_call(functools.partial(feed_kernel, plan), name='feed', out_sha...  30.8 us
    ppermute x20, starting transfers between devices, shift(): return lax.ppermute(values, AXES, pairs)  29.3 us
    pallas_call x1, Pallas kernels, attend_weights(): pl.pallas_call(functools.partial(attend_weights_kernel, plan, steps, len(...  19.1 us
  transfers between devices with their start and end apart: 21, of which 10 were waited for; matrix products, arithmetic and copies ran while one was open for 6% of the time, Pallas kernels for 11%

profile of v4, /device:TPU:0, one launch (start us, length us, event | category | flops | bytes accessed | tf_op | source)
XLA Modules:
  0.0 575.0 jit_solution(2710607896774942535)
XLA Ops:
  5.5 1.5 convert_reduce_fusion
  12.4 12.2 %swap_blocks.1 = s32[32,8,128]{2,1,0:T(8,128)} custom-call(s32[32,8,128]{2,1,0:T(8,128)} %bitcast.191), custom_call_target="tpu_custom_call" | custom-call | tf_op jit(solution)/shard_map/swap_blocks/pallas_call | solution.py:391
  26.4 2.0 convert_element_type.268
  29.5 2.5 fusion.21
  35.7 66.2 %fetch.1 = (bf16[32,80,384]{2,1,0:T(8,128)(2,1)}, bf16[2,4,2,2,48,384]{5,4,3,2,1,0:T(8,128)(2,1)}, bf16[2,4,2,2,48,384]{5,4,3,2,1,0:T(8,128)(2,1)}, bf16[2,4,2,2...) custom-call(bf16[32,80,384]{2,1,0:T(8,128)(2,1)} %pad_maximum_fusion.rows_ref, ...), custom_call_target="tpu_custom_call" | custom-call | tf_op jit(solution)/shard_map/fetch/pallas_call | solution.py:610
  101.9 1.8 fusion.88
  106.7 4.0 fusion.15
  110.8 3.1 conditional.1
  113.9 1.9 fusion.51
  115.8 1.8 pad_maximum_fusion.2
  118.9 92.1 %attend.1 = (bf16[6,1024,128]{2,1,0:T(8,128)(2,1)}, bf16[6,1024,128]{2,1,0:T(8,128)(2,1)}, bf16[6,1024,128]{2,1,0:T(8,128)(2,1)}, bf16[1024,768]{1,0:T(8,128)(2,...) custom-call(s32[5]{0:T(128)} %stack.26.place, ...), custom_call_target="tpu_custom_call" | custom-call | flops 17716740096 | bytes 23592960 | tf_op jit(solution)/shard_map/attend/pallas_call | solution.py:895
  211.0 30.8 %feed.1 = (bf16[1024,3072]{1,0:T(8,128)(2,1)}, bf16[1024,3072]{1,0:T(8,128)(2,1)}, bf16[1024,3072]{1,0:T(8,128)(2,1)}, f32[1024,768]{1,0:T(8,128)}, f32[1024,1]{1,0:T(8,128)}, /*index=5*/f32[1,768]{1,0:T(1,128)}) custom-call(s32[5]{0:T(128)} %stack.26.place, bf16[1024,768]{1,0:T(8,128)(2,1)} %get-tuple-element.187.x.refs_1_, ...), custom_call_target="tpu_custom_call" | custom-call | flops 14495514624 | bytes 31457280 | tf_op jit(solution)/shard_map/feed/pallas_call | solution.py:1000
  241.8 11.3 %contrast.1 = (f32[1,128]{1,0:T(1,128)}, f32[1,768]{1,0:T(1,128)}) custom-call(s32[5]{0:T(128)} %stack.26.place, f32[1,768]{1,0:T(1,128)} %get-tuple-element.192.pool_ref, f32[6,768]{1,0:T(8,128)} %refs_8_.1, f32[1,1]{1,0:T(1,128)} %bitcast.181.scale_ref), custom_call_target="tpu_custom_call" | custom-call | tf_op jit(solution)/shard_map/contrast/pallas_call | solution.py:1106
  253.1 64.3 %feed_back.1 = (f32[2,2,4,48,2304]{4,3,2,1,0:T(8,128)}, f32[2,2,4,48,2304]{4,3,2,1,0:T(8,128)}, f32[1024,768]{1,0:T(8,128)}, bf16[1024,768]{1,0:T(8,128)(2,1)}, f32[8,768]{1,0:T(8,128)}, /*index=5*/f32[8,128]{1,0:T(8,128)}) custom-call(s32[5]{0:T(128)} %stack.26.place, f32[1,768]{1,0:T(1,128)} %get-tuple-element.194.refs_0_, ...), custom_call_target="tpu_custom_call" | custom-call | flops 48318382080 | bytes 47185920 | tf_op jit(solution)/shard_map/feed_back/pallas_call | solution.py:1265
  319.4 2.3 fusion.28
  321.7 1.5 collective-permute-start.1
  323.2 3.5 fusion.27
  327.4 28.2 %heads_back.2.refs_0_ = bf16[4,1024,384]{2,1,0:T(8,128)(2,1)} custom-call(s32[5]{0:T(128)} %stack.26.place, bf16[1024,768]{1,0:T(8,128)(2,1)} %get-tuple-element.217.ga.refs_3_, bf16[6,1024,128]{2,1,0:T(8,128)(2,1)} %get-tuple-element.202.q, bf16[6,1024,128]{2,1,0:T(8,128)(2,1)} %get-tuple-element.203.k, bf16[6,1024,128]{2,1,0:T(8,128)(2,1)} %get-tuple-element.204.v, ...), custom_call_target="tpu_custom_call" | custom-call | flops 42949672960 | bytes 1572864 | tf_op jit(solution)/shard_map/heads_back/pallas_call | solution.py:1402
  355.6 6.1 %collective-permute-done.1 = f16[2,4,48,2304]{3,2,1,0:T(8,128)(2,1)} collective-permute-done((f16[2,4,48,2304]{3,2,1,0:T(8,128)(2,1)S(1)}, f16[2,4,48,2304]{3,2,1,0:T(8,128)(2,1)}, u32[]{:S(2)}, u32[]{:S(2)}) %collective-permute-start.1) | collective-permute-done | bytes 1769504 | tf_op jit(solution)/shard_map/ppermute | solution.py:68
  361.7 2.9 bitcast_add_fusion
  364.6 1.8 collective-permute-done
  366.4 2.5 bitcast_add_fusion.1
  372.3 16.0 %heads_back.3.refs_1_ = bf16[2,1024,384]{2,1,0:T(8,128)(2,1)} custom-call(s32[5]{0:T(128)} %stack.26.place, bf16[1024,768]{1,0:T(8,128)(2,1)} %get-tuple-element.217.ga.refs_3_, bf16[6,1024,128]{2,1,0:T(8,128)(2,1)} %get-tuple-element.202.q, bf16[6,1024,128]{2,1,0:T(8,128)(2,1)} %get-tuple-element.203.k, bf16[6,1024,128]{2,1,0:T(8,128)(2,1)} %get-tuple-element.204.v, ...), custom_call_target="tpu_custom_call" | custom-call | flops 21474836480 | bytes 1572864 | tf_op jit(solution)/shard_map/heads_back/pallas_call | solution.py:1402
  388.8 1.7 bitcast_add_fusion.2
  392.5 2.4 collective-permute-start.8
  398.0 19.1 %attend_weights.1 = (f32[2,2,4,48,768]{4,3,2,1,0:T(8,128)}, f32[2,2,4,48,768]{4,3,2,1,0:T(8,128)}, f32[8,128]{1,0:T(8,128)}) custom-call(bf16[4,1024,384]{2,1,0:T(8,128)(2,1)} %heads_back.2.refs_0_, bf16[2,1024,384]{2,1,0:T(8,128)(2,1)} %heads_back.3.refs_1_, bf16[1024,768]{1,0:T(8,128)(2,1)} %get-tuple-element.214.refs_2_, ...), custom_call_target="tpu_custom_call" | custom-call | flops 7247757312 | bytes 15728640 | tf_op jit(solution)/shard_map/attend_weights/pallas_call | solution.py:1575
  417.1 2.9 collective-permute-start.6
  421.1 5.8 %collective-permute-done.5 = f16[48,2304]{1,0:T(8,128)(2,1)S(1)} collective-permute-done((f16[48,2304]{1,0:T(8,128)(2,1)S(1)}, f16[48,2304]{1,0:T(8,128)(2,1)S(1)}, u32[]{:S(2)}, u32[]{:S(2)}) %collective-permute-start.5) | collective-permute-done | bytes 221216 | tf_op jit(solution)/shard_map/ppermute | solution.py:68
  427.0 3.4 collective-permute-done.6
  430.6 13.9 %first_back.1 = (bf16[1024,768]{1,0:T(8,128)(2,1)S(1)}, f32[8,768]{1,0:T(8,128)}, f32[8,128]{1,0:T(8,128)}) custom-call(bf16[4,1024,384]{2,1,0:T(8,128)(2,1)} %heads_back.2.refs_0_, bf16[2,1024,384]{2,1,0:T(8,128)(2,1)} %heads_back.3.refs_1_, bf16[2,768,384]{2,1,0:T(8,128)(2,1)} %bitcast.210, bf16[2,768,384]{2,1,0:T(8,128)(2,1)} %bitcast.212, ...), custom_call_target="tpu_custom_call" | custom-call | flops 4831838208 | bytes 15728640 | tf_op jit(solution)/shard_map/first_back/pallas_call | solution.py:1490
  444.5 3.7 fusion.20
  448.2 3.6 all-to-all-start.4
  456.1 1.6 collective-permute-start.15
  460.9 2.2 fusion.32
  468.2 1.8 slice.230
  470.9 1.9 stack_reshape.7
  473.5 11.5 %collective-permute-done.15 = f16[2,4,48,768]{3,2,1,0:T(8,128)(2,1)} collective-permute-done((f16[2,4,48,768]{3,2,1,0:T(8,128)(2,1)}, f16[2,4,48,768]{3,2,1,0:T(8,128)(2,1)}, u32[]{:S(2)}, u32[]{:S(2)}) %collective-permute-start.15) | collective-permute-done | bytes 589856 | tf_op jit(solution)/shard_map/ppermute | solution.py:68
  486.4 2.2 collective-permute-start.16
  491.1 6.3 %collective-permute-done.16 = f16[4,48,768]{2,1,0:T(8,128)(2,1)S(1)} collective-permute-done((f16[4,48,768]{2,1,0:T(8,128)(2,1)S(1)}, f16[4,48,768]{2,1,0:T(8,128)(2,1)S(1)}, u32[]{:S(2)}, u32[]{:S(2)}) %collective-permute-start.16) | collective-permute-done | bytes 294944 | tf_op jit(solution)/shard_map/ppermute | solution.py:68
  497.5 2.7 collective-permute-start.17
  500.3 2.0 collective-permute-start.18
  502.2 1.7 collective-permute-start.19
  505.4 2.5 collective-permute-start.14
  510.8 2.8 collective-permute-done.13
  516.2 5.4 fusion.18
  522.6 3.3 multiply_reduce_fusion
  529.9 17.8 %total.1 = f32[32,8,128]{2,1,0:T(8,128)} custom-call(f32[32,8,128]{2,1,0:T(8,128)} %bitcast.193), custom_call_target="tpu_custom_call" | custom-call | tf_op jit(solution)/shard_map/total/pallas_call | solution.py:440
  558.0 8.7 %add_multiply_fusion = (f32[960,768]{1,0:T(8,128)}, f32[960,768]{1,0:T(8,128)}, f32[960,768]{1,0:T(8,128)}) fusion(f32[960,768]{1,0:T(8,128)S(1)} %copy-done.4, f32[960,768]{1,0:T(8,128)} %get-tuple-element.225, f32[]{:T(128)S(6)} %min_shard_map.3, f32[960,768]{1,0:T(8,128)} %param.33, f32[960,768]{1,0:T(8,128)} %param.32), kind=kLoop, calls=%fused_computation.47 | loop fusion | flops 11059200 | bytes 20643844 | tf_op jit(solution)/shard_map/mul | solution.py:1621
  (219 shorter events, 63.6 us)
Async XLA Ops:
  4.6 106.1 %copy-start.41 = (s32[1024]{0:T(1024)}, s32[1024]{0:T(1024)S(1)}, u32[]{:S(2)}) copy-start(s32[1024]{0:T(1024)S(1)} %get-tuple-element.536) | copy-start | bytes 12292
  4.6 106.1 %copy-start.21 = (s32[1024]{0:T(1024)}, s32[1024]{0:T(1024)S(1)}, u32[]{:S(2)}) copy-start(s32[1024]{0:T(1024)S(1)} %add_select_fusion.2) | copy-start | bytes 12292
  5.5 105.3 %copy-start.47 = (pred[1024]{0:T(1024)(128)(4,1)}, pred[1024]{0:T(1024)(128)(4,1)S(1)}, u32[]{:S(2)}) copy-start(pred[1024]{0:T(1024)(128)(4,1)S(1)} %get-tuple-element.533) | copy-start | bytes 3076
  7.1 103.7 %copy-start.18 = (s32[1024]{0:T(1024)}, s32[1024]{0:T(1024)S(1)}, u32[]{:S(2)}) copy-start(s32[1024]{0:T(1024)S(1)} %get-tuple-element.534) | copy-start | bytes 12292
  35.7 68.7 %copy-start.5 = (f32[48,2,1536]{2,1,0:T(2,128)S(1)}, f32[48,2,1536]{2,1,0:T(2,128)}, u32[]{:S(2)}) copy-start(f32[48,2,1536]{2,1,0:T(2,128)} %param.40) | copy-start | bytes 1769476
  321.7 39.9 %collective-permute-start.1 = (f16[2,4,48,2304]{3,2,1,0:T(8,128)(2,1)S(1)}, f16[2,4,48,2304]{3,2,1,0:T(8,128)(2,1)}, u32[]{:S(2)}, u32[]{:S(2)}) collective-permute-start(f16[2,4,48,2304]{3,2,1,0:T(8,128)(2,1)S(1)} %fusion.28), channel_id=1, source_target_pairs={{0,4},{1,5},{2,6},{3,7},{4,0},{5,1},{6,2},{7,3},{8,12},{9,13},{10,... | collective-permute-start | bytes 5308424 | tf_op jit(solution)/shard_map/ppermute | solution.py:68
  326.7 39.7 %collective-permute-start = (f16[2,4,48,2304]{3,2,1,0:T(8,128)(2,1)}, f16[2,4,48,2304]{3,2,1,0:T(8,128)(2,1)S(1)}, u32[]{:S(2)}, u32[]{:S(2)}) collective-permute-start(f16[2,4,48,2304]{3,2,1,0:T(8,128)(2,1)} %fusion.27), channel_id=1, source_target_pairs={{0,1},{1,0},{2,3},{3,2},{4,5},{5,4},{6,7},{7,6},{8,9},{9,8},{10,11... | collective-permute-start | bytes 5308424 | tf_op jit(solution)/shard_map/ppermute | solution.py:68
  369.1 19.8 %collective-permute-start.3 = (f16[4,48,2304]{2,1,0:T(8,128)(2,1)S(1)}, f16[4,48,2304]{2,1,0:T(8,128)(2,1)}, u32[]{:S(2)}, u32[]{:S(2)}) collective-permute-start(f16[4,48,2304]{2,1,0:T(8,128)(2,1)S(1)} %fusion.30), channel_id=1, source_target_pairs={{0,1},{1,0},{2,3},{3,2},{4,5},{5,4},{6,7},{7,6},{8,9},{9,8},{10,11... | collective-permute-start | bytes 2654216 | tf_op jit(solution)/shard_map/ppermute | solution.py:68
  371.7 19.8 %collective-permute-start.2 = (f16[4,48,2304]{2,1,0:T(8,128)(2,1)}, f16[4,48,2304]{2,1,0:T(8,128)(2,1)S(1)}, u32[]{:S(2)}, u32[]{:S(2)}) collective-permute-start(f16[4,48,2304]{2,1,0:T(8,128)(2,1)} %fusion.29), channel_id=1, source_target_pairs={{0,4},{1,5},{2,6},{3,7},{4,0},{5,1},{6,2},{7,3},{8,12},{9,13},{10,... | collective-permute-start | bytes 2654216 | tf_op jit(solution)/shard_map/ppermute | solution.py:68
  391.9 25.3 %collective-permute-start.7 = (f16[48,2304]{1,0:T(8,128)(2,1)S(1)}, f16[48,2304]{1,0:T(8,128)(2,1)S(1)}, u32[]{:S(2)}, u32[]{:S(2)}) collective-permute-start(f16[48,2304]{1,0:T(8,128)(2,1)S(1)} %get-tuple-element.371), channel_id=1, source_target_pairs={{0,8},{1,9},{2,10},{3,11},{4,12},{5,13},{6,14},{7,15},{8,16},{9,17... | collective-permute-start | bytes 663560 | tf_op jit(solution)/shard_map/ppermute | solution.py:68
  392.5 27.5 %collective-permute-start.8 = (f16[48,2304]{1,0:T(8,128)(2,1)S(1)}, f16[48,2304]{1,0:T(8,128)(2,1)S(1)}, u32[]{:S(2)}, u32[]{:S(2)}) collective-permute-start(f16[48,2304]{1,0:T(8,128)(2,1)S(1)} %get-tuple-element.373), channel_id=1, source_target_pairs={{0,16},{1,17},{2,18},{3,19},{4,20},{5,21},{6,22},{7,23},{8,24},{9,... | collective-permute-start | bytes 663560 | tf_op jit(solution)/shard_map/ppermute | solution.py:68
  394.9 25.1 %collective-permute-start.9 = (f16[48,2304]{1,0:T(8,128)(2,1)S(1)}, f16[48,2304]{1,0:T(8,128)(2,1)}, u32[]{:S(2)}, u32[]{:S(2)}) collective-permute-start(f16[48,2304]{1,0:T(8,128)(2,1)S(1)} %get-tuple-element.372), channel_id=1, source_target_pairs={{0,24},{1,25},{2,26},{3,27},{4,28},{5,29},{6,30},{7,31},{8,0},{9,1... | collective-permute-start | bytes 663560 | tf_op jit(solution)/shard_map/ppermute | solution.py:68
  396.5 24.6 %collective-permute-start.4 = (f16[48,2304]{1,0:T(8,128)(2,1)S(1)}, f16[48,2304]{1,0:T(8,128)(2,1)S(1)}, u32[]{:S(2)}, u32[]{:S(2)}) collective-permute-start(f16[48,2304]{1,0:T(8,128)(2,1)S(1)} %get-tuple-element.374), channel_id=1, source_target_pairs={{0,8},{1,9},{2,10},{3,11},{4,12},{5,13},{6,14},{7,15},{8,16},{9,17... | collective-permute-start | bytes 663560 | tf_op jit(solution)/shard_map/ppermute | solution.py:68
  397.1 29.8 %collective-permute-start.5 = (f16[48,2304]{1,0:T(8,128)(2,1)S(1)}, f16[48,2304]{1,0:T(8,128)(2,1)S(1)}, u32[]{:S(2)}, u32[]{:S(2)}) collective-permute-start(f16[48,2304]{1,0:T(8,128)(2,1)S(1)} %get-tuple-element.376), channel_id=1, source_target_pairs={{0,16},{1,17},{2,18},{3,19},{4,20},{5,21},{6,22},{7,23},{8,24},{9,... | collective-permute-start | bytes 663560 | tf_op jit(solution)/shard_map/ppermute | solution.py:68
  417.1 13.2 %collective-permute-start.6 = (f16[48,2304]{1,0:T(8,128)(2,1)S(1)}, f16[48,2304]{1,0:T(8,128)(2,1)S(1)}, u32[]{:S(2)}, u32[]{:S(2)}) collective-permute-start(f16[48,2304]{1,0:T(8,128)(2,1)S(1)} %get-tuple-element.375), channel_id=1, source_target_pairs={{0,24},{1,25},{2,26},{3,27},{4,28},{5,29},{6,30},{7,31},{8,0},{9,1... | collective-permute-start | bytes 663560 | tf_op jit(solution)/shard_map/ppermute | solution.py:68
  430.5 13.9 %copy-start.44 = (s32[1,1024]{1,0:T(1,128)S(1)}, s32[1,1024]{1,0:T(1,128)}, u32[]{:S(2)}) copy-start(s32[1,1024]{1,0:T(1,128)} %copy-done.43) | copy-start | bytes 12292
  448.2 9.6 %copy-start.46 = (f32[1,128]{1,0:T(1,128)S(1)}, f32[1,128]{1,0:T(1,128)}, u32[]{:S(2)}) copy-start(f32[1,128]{1,0:T(1,128)} %get-tuple-element.193) | copy-start | bytes 1540
  448.2 68.0 %all-to-all-start.4 = ((bf16[32,40,768]{2,1,0:T(8,128)(2,1)}), bf16[32,40,768]{2,1,0:T(8,128)(2,1)}, u32[]{:S(2)}, u32[]{:S(2)}) async-start(bf16[32,40,768]{2,1,0:T(8,128)(2,1)} %bitcast.187), calls=%async_computation.4 | async-start | bytes 3932160 | tf_op jit(solution)/shard_map/all_to_all | solution.py:743
  456.1 28.9 %collective-permute-start.15 = (f16[2,4,48,768]{3,2,1,0:T(8,128)(2,1)}, f16[2,4,48,768]{3,2,1,0:T(8,128)(2,1)}, u32[]{:S(2)}, u32[]{:S(2)}) collective-permute-start(f16[2,4,48,768]{3,2,1,0:T(8,128)(2,1)} %fusion.33), channel_id=1, source_target_pairs={{0,4},{1,5},{2,6},{3,7},{4,0},{5,1},{6,2},{7,3},{8,12},{9,13},{10,... | collective-permute-start | bytes 1769480 | tf_op jit(solution)/shard_map/ppermute | solution.py:68
  463.1 25.4 %collective-permute-start.10 = (f16[2,4,48,768]{3,2,1,0:T(8,128)(2,1)}, f16[2,4,48,768]{3,2,1,0:T(8,128)(2,1)}, u32[]{:S(2)}, u32[]{:S(2)}) collective-permute-start(f16[2,4,48,768]{3,2,1,0:T(8,128)(2,1)} %fusion.32), channel_id=1, source_target_pairs={{0,1},{1,0},{2,3},{3,2},{4,5},{5,4},{6,7},{7,6},{8,9},{9,8},{10,11... | collective-permute-start | bytes 1769480 | tf_op jit(solution)/shard_map/ppermute | solution.py:68
  472.8 15.7 %copy-start.8 = (f32[2,2,4,48,768]{4,3,2,1,0:T(8,128)S(1)}, f32[2,2,4,48,768]{4,3,2,1,0:T(8,128)}, u32[]{:S(2)}) copy-start(f32[2,2,4,48,768]{4,3,2,1,0:T(8,128)} %get-tuple-element.228) | copy-start | bytes 7077892
  486.4 11.1 %collective-permute-start.16 = (f16[4,48,768]{2,1,0:T(8,128)(2,1)S(1)}, f16[4,48,768]{2,1,0:T(8,128)(2,1)S(1)}, u32[]{:S(2)}, u32[]{:S(2)}) collective-permute-start(f16[4,48,768]{2,1,0:T(8,128)(2,1)S(1)} %fusion.42), channel_id=1, source_target_pairs={{0,1},{1,0},{2,3},{3,2},{4,5},{5,4},{6,7},{7,6},{8,9},{9,8},{10,11... | collective-permute-start | bytes 884744 | tf_op jit(solution)/shard_map/ppermute | solution.py:68
  489.9 26.3 %copy-start.40 = (s32[1280]{0:T(1024)S(1)}, s32[1280]{0:T(1024)}, u32[]{:S(2)}) copy-start(s32[1280]{0:T(1024)} %copy-done.39) | copy-start | bytes 15364
  489.9 14.1 %collective-permute-start.11 = (f16[4,48,768]{2,1,0:T(8,128)(2,1)S(1)}, f16[4,48,768]{2,1,0:T(8,128)(2,1)S(1)}, u32[]{:S(2)}, u32[]{:S(2)}) collective-permute-start(f16[4,48,768]{2,1,0:T(8,128)(2,1)S(1)} %fusion.43), channel_id=1, source_target_pairs={{0,4},{1,5},{2,6},{3,7},{4,0},{5,1},{6,2},{7,3},{8,12},{9,13},{10,... | collective-permute-start | bytes 884744 | tf_op jit(solution)/shard_map/ppermute | solution.py:68
  497.5 7.9 %collective-permute-start.17 = (f16[48,768]{1,0:T(8,128)(2,1)S(1)}, f16[48,768]{1,0:T(8,128)(2,1)S(1)}, u32[]{:S(2)}, u32[]{:S(2)}) collective-permute-start(f16[48,768]{1,0:T(8,128)(2,1)S(1)} %get-tuple-element.377), channel_id=1, source_target_pairs={{0,8},{1,9},{2,10},{3,11},{4,12},{5,13},{6,14},{7,15},{8,16},{9,17... | collective-permute-start | bytes 221192 | tf_op jit(solution)/shard_map/ppermute | solution.py:68
  500.3 7.7 %collective-permute-start.18 = (f16[48,768]{1,0:T(8,128)(2,1)S(1)}, f16[48,768]{1,0:T(8,128)(2,1)S(1)}, u32[]{:S(2)}, u32[]{:S(2)}) collective-permute-start(f16[48,768]{1,0:T(8,128)(2,1)S(1)} %get-tuple-element.379), channel_id=1, source_target_pairs={{0,16},{1,17},{2,18},{3,19},{4,20},{5,21},{6,22},{7,23},{8,24},{9,... | collective-permute-start | bytes 221192 | tf_op jit(solution)/shard_map/ppermute | solution.py:68
  502.2 5.7 collective-permute-start.19
  504.1 6.7 %collective-permute-start.12 = (f16[48,768]{1,0:T(8,128)(2,1)S(1)}, f16[48,768]{1,0:T(8,128)(2,1)S(1)}, u32[]{:S(2)}, u32[]{:S(2)}) collective-permute-start(f16[48,768]{1,0:T(8,128)(2,1)S(1)} %get-tuple-element.380), channel_id=1, source_target_pairs={{0,8},{1,9},{2,10},{3,11},{4,12},{5,13},{6,14},{7,15},{8,16},{9,17... | collective-permute-start | bytes 221192 | tf_op jit(solution)/shard_map/ppermute | solution.py:68
  504.5 9.2 %collective-permute-start.13 = (f16[48,768]{1,0:T(8,128)(2,1)S(1)}, f16[48,768]{1,0:T(8,128)(2,1)S(1)}, u32[]{:S(2)}, u32[]{:S(2)}) collective-permute-start(f16[48,768]{1,0:T(8,128)(2,1)S(1)} %get-tuple-element.382), channel_id=1, source_target_pairs={{0,16},{1,17},{2,18},{3,19},{4,20},{5,21},{6,22},{7,23},{8,24},{9,... | collective-permute-start | bytes 221192 | tf_op jit(solution)/shard_map/ppermute | solution.py:68
  505.4 8.2 %collective-permute-start.14 = (f16[48,768]{1,0:T(8,128)(2,1)S(1)}, f16[48,768]{1,0:T(8,128)(2,1)S(1)}, u32[]{:S(2)}, u32[]{:S(2)}) collective-permute-start(f16[48,768]{1,0:T(8,128)(2,1)S(1)} %get-tuple-element.381), channel_id=1, source_target_pairs={{0,24},{1,25},{2,26},{3,27},{4,28},{5,29},{6,30},{7,31},{8,0},{9,1... | collective-permute-start | bytes 221192 | tf_op jit(solution)/shard_map/ppermute | solution.py:68
  522.6 30.1 %slice-start = ((f32[48,3,768]{2,1,0:T(4,128)}), f32[48,3,256]{2,1,0:T(4,128)S(1)}, s32[]{:S(2)}) async-start(f32[48,3,768]{2,1,0:T(4,128)} %reshape.356), calls=%async_computation.5 | async-start | bytes 393216 | tf_op jit(solution)/shard_map/slice | solution.py:1341
  522.6 30.0 %slice-start.2 = ((f32[48,3,768]{2,1,0:T(4,128)}), f32[48,3,256]{2,1,0:T(4,128)S(1)}, s32[]{:S(2)}) async-start(f32[48,3,768]{2,1,0:T(4,128)} %reshape.357), calls=%async_computation.7 | async-start | bytes 393216 | tf_op jit(solution)/shard_map/slice | solution.py:1341
  522.6 30.2 %copy-start.6 = (f32[48,2,1536]{2,1,0:T(2,128)S(1)}, f32[48,2,1536]{2,1,0:T(2,128)}, u32[]{:S(2)}) copy-start(f32[48,2,1536]{2,1,0:T(2,128)} %param.40) | copy-start | bytes 1769476
  522.6 30.2 %copy-start.11 = (f32[48,1,1536]{2,0,1:T(8,128)S(1)}, f32[48,1,1536]{2,0,1:T(8,128)}, u32[]{:S(2)}) copy-start(f32[48,1,1536]{2,0,1:T(8,128)} %stack_reshape.7) | copy-start | bytes 884740
  522.6 30.2 %copy-start.16 = (f32[48,2,1536]{2,1,0:T(2,128)S(1)}, f32[48,2,1536]{2,1,0:T(2,128)}, u32[]{:S(2)}) copy-start(f32[48,2,1536]{2,1,0:T(2,128)} %param.42) | copy-start | bytes 1769476
  522.6 30.2 %copy-start.17 = (f32[48,2,1536]{2,1,0:T(2,128)S(1)}, f32[48,2,1536]{2,1,0:T(2,128)}, u32[]{:S(2)}) copy-start(f32[48,2,1536]{2,1,0:T(2,128)} %param.41) | copy-start | bytes 1769476
  557.9 9.5 %copy-start.13 = (f32[48,1536]{1,0:T(8,128)S(1)}, f32[48,1536]{1,0:T(8,128)}, u32[]{:S(2)}) copy-start(f32[48,1536]{1,0:T(8,128)} %param.43) | copy-start | bytes 884740
  557.9 9.5 %copy-start.27 = (f32[48,1536]{1,0:T(8,128)S(1)}, f32[48,1536]{1,0:T(8,128)}, u32[]{:S(2)}) copy-start(f32[48,1536]{1,0:T(8,128)} %param.45) | copy-start | bytes 884740
  557.9 9.5 %copy-start.28 = (f32[48,1536]{1,0:T(8,128)S(1)}, f32[48,1536]{1,0:T(8,128)}, u32[]{:S(2)}) copy-start(f32[48,1536]{1,0:T(8,128)} %param.44) | copy-start | bytes 884740
  557.9 10.5 %copy-start.26 = (f32[48,384]{1,0:T(8,128)S(1)}, f32[48,384]{1,0:T(8,128)}, u32[]{:S(2)}) copy-start(f32[48,384]{1,0:T(8,128)} %param.37) | copy-start | bytes 221188
  557.9 10.5 %copy-start.34 = (f32[48,384]{1,0:T(8,128)S(1)}, f32[48,384]{1,0:T(8,128)}, u32[]{:S(2)}) copy-start(f32[48,384]{1,0:T(8,128)} %param.39) | copy-start | bytes 221188
  557.9 10.5 %copy-start.35 = (f32[48,384]{1,0:T(8,128)S(1)}, f32[48,384]{1,0:T(8,128)}, u32[]{:S(2)}) copy-start(f32[48,384]{1,0:T(8,128)} %param.38) | copy-start | bytes 221188
  557.9 11.2 %copy-start.15 = (f32[48,3,384]{2,0,1:T(8,128)S(1)}, f32[48,3,384]{2,0,1:T(8,128)}, u32[]{:S(2)}) copy-start(f32[48,3,384]{2,0,1:T(8,128)} %param.34) | copy-start | bytes 663556
  558.0 11.2 %copy-start.23 = (f32[48,1,384]{2,0,1:T(8,128)S(1)}, f32[48,1,384]{2,0,1:T(8,128)}, u32[]{:S(2)}) copy-start(f32[48,1,384]{2,0,1:T(8,128)} %stack_reshape_squeeze.10) | copy-start | bytes 221188
  558.0 11.2 %copy-start.24 = (f32[48,1,384]{2,0,1:T(8,128)S(1)}, f32[48,1,384]{2,0,1:T(8,128)}, u32[]{:S(2)}) copy-start(f32[48,1,384]{2,0,1:T(8,128)} %stack_reshape_squeeze.9) | copy-start | bytes 221188
  558.0 11.1 %copy-start.29 = (f32[48,3,384]{2,0,1:T(8,128)S(1)}, f32[48,3,384]{2,0,1:T(8,128)}, u32[]{:S(2)}) copy-start(f32[48,3,384]{2,0,1:T(8,128)} %param.36) | copy-start | bytes 663556
  558.0 11.1 %copy-start.30 = (f32[48,3,384]{2,0,1:T(8,128)S(1)}, f32[48,3,384]{2,0,1:T(8,128)}, u32[]{:S(2)}) copy-start(f32[48,3,384]{2,0,1:T(8,128)} %param.35) | copy-start | bytes 663556
  558.0 12.1 %copy-start.1 = (s32[1,2]{1,0:T(1,128)S(1)}, s32[1,2]{1,0:T(1,128)}, u32[]{:S(2)}) copy-start(s32[1,2]{1,0:T(1,128)} %param.30) | copy-start | bytes 28
  (27 other events, 124.8 us)

commit v5 on v4

--- a/solution.py
+++ b/solution.py
@@ -26,7 +26,7 @@
 LANES = 128
 VMEM_LIMIT = 58 * 1024 * 1024
 ROW_BLOCK = 256
-HIDDEN_BLOCK = 256
+HIDDEN_BLOCK = 512
 BACK_BLOCK = 512
 
 

time: 584 us -> 580 us (level)
  no operation moved by 1% of the time
where the time goes in v5:
time: 580 us; the launch traced here: 571 us
  Pallas kernels  368 us (63%)
  other arithmetic  58 us (10%)
  waiting for transfers between devices  40.8 us (7%)
  starting transfers between devices  33 us (6%)
  local copies, waits for them, and re-layouts  31.8 us (5%)
  between operations  20.1 us (3%)
  matrix products  15.6 us (3%)
    pallas_call x1, Pallas kernels, attend(): pl.pallas_call(functools.partial(attend_kernel, plan, number), name='atte...  92.1 us
    pallas_call x1, Pallas kernels, fetch(): pl.pallas_call(functools.partial(fetch_kernel, plan, orders), name='fetch...  66.2 us
    pallas_call x1, Pallas kernels, feed_back(): pl.pallas_call(functools.partial(feed_back_kernel, plan, steps), name='fe...  64.3 us
    pallas_call x2, Pallas kernels, heads_back(): pl.pallas_call(heads_back_kernel, name='heads_back', out_shape=jax.ShapeD...  44.1 us
    ppermute x20, waiting for transfers between devices, shift(): return lax.ppermute(values, AXES, pairs)  40.8 us
    ppermute x20, starting transfers between devices, shift(): return lax.ppermute(values, AXES, pairs)  29.3 us
    pallas_call x1, Pallas kernels, feed(): pl.pallas_call(functools.partial(feed_kernel, plan), name='feed', out_sha...  26.7 us
    pallas_call x1, Pallas kernels, attend_weights(): pl.pallas_call(functools.partial(attend_weights_kernel, plan, steps, len(...  19.1 us
  transfers between devices with their start and end apart: 21, of which 10 were waited for; matrix products, arithmetic and copies ran while one was open for 6% of the time, Pallas kernels for 11%

profile of v5, /device:TPU:0, one launch (start us, length us, event | category | flops | bytes accessed | tf_op | source)
XLA Modules:
  0.0 570.9 jit_solution(15564907890567114717)
XLA Ops:
  5.5 1.5 convert_reduce_fusion
  12.4 12.2 %swap_blocks.1 = s32[32,8,128]{2,1,0:T(8,128)} custom-call(s32[32,8,128]{2,1,0:T(8,128)} %bitcast.191), custom_call_target="tpu_custom_call" | custom-call | tf_op jit(solution)/shard_map/swap_blocks/pallas_call | solution.py:391
  26.4 2.0 convert_element_type.268
  29.5 2.5 fusion.21
  35.7 66.2 %fetch.1 = (bf16[32,80,384]{2,1,0:T(8,128)(2,1)}, bf16[2,4,2,2,48,384]{5,4,3,2,1,0:T(8,128)(2,1)}, bf16[2,4,2,2,48,384]{5,4,3,2,1,0:T(8,128)(2,1)}, bf16[2,4,2,2...) custom-call(bf16[32,80,384]{2,1,0:T(8,128)(2,1)} %pad_maximum_fusion.rows_ref, ...), custom_call_target="tpu_custom_call" | custom-call | tf_op jit(solution)/shard_map/fetch/pallas_call | solution.py:610
  101.9 1.8 fusion.88
  106.7 4.0 fusion.15
  110.8 3.1 conditional.1
  113.9 1.9 fusion.51
  115.8 1.8 pad_maximum_fusion.2
  118.9 92.1 %attend.1 = (bf16[6,1024,128]{2,1,0:T(8,128)(2,1)}, bf16[6,1024,128]{2,1,0:T(8,128)(2,1)}, bf16[6,1024,128]{2,1,0:T(8,128)(2,1)}, bf16[1024,768]{1,0:T(8,128)(2,...) custom-call(s32[5]{0:T(128)} %stack.26.place, ...), custom_call_target="tpu_custom_call" | custom-call | flops 17716740096 | bytes 23592960 | tf_op jit(solution)/shard_map/attend/pallas_call | solution.py:895
  211.0 26.7 %feed.1 = (bf16[1024,3072]{1,0:T(8,128)(2,1)}, bf16[1024,3072]{1,0:T(8,128)(2,1)}, bf16[1024,3072]{1,0:T(8,128)(2,1)}, f32[1024,768]{1,0:T(8,128)}, f32[1024,1]{1,0:T(8,128)}, /*index=5*/f32[1,768]{1,0:T(1,128)}) custom-call(s32[5]{0:T(128)} %stack.26.place, bf16[1024,768]{1,0:T(8,128)(2,1)} %get-tuple-element.187.x.refs_1_, ...), custom_call_target="tpu_custom_call" | custom-call | flops 14495514624 | bytes 31457280 | tf_op jit(solution)/shard_map/feed/pallas_call | solution.py:1000
  237.7 11.3 %contrast.1 = (f32[1,128]{1,0:T(1,128)}, f32[1,768]{1,0:T(1,128)}) custom-call(s32[5]{0:T(128)} %stack.26.place, f32[1,768]{1,0:T(1,128)} %get-tuple-element.192.pool_ref, f32[6,768]{1,0:T(8,128)} %refs_8_.1, f32[1,1]{1,0:T(1,128)} %bitcast.181.scale_ref), custom_call_target="tpu_custom_call" | custom-call | tf_op jit(solution)/shard_map/contrast/pallas_call | solution.py:1106
  249.0 64.3 %feed_back.1 = (f32[2,2,4,48,2304]{4,3,2,1,0:T(8,128)}, f32[2,2,4,48,2304]{4,3,2,1,0:T(8,128)}, f32[1024,768]{1,0:T(8,128)}, bf16[1024,768]{1,0:T(8,128)(2,1)}, f32[8,768]{1,0:T(8,128)}, /*index=5*/f32[8,128]{1,0:T(8,128)}) custom-call(s32[5]{0:T(128)} %stack.26.place, f32[1,768]{1,0:T(1,128)} %get-tuple-element.194.refs_0_, ...), custom_call_target="tpu_custom_call" | custom-call | flops 48318382080 | bytes 47185920 | tf_op jit(solution)/shard_map/feed_back/pallas_call | solution.py:1265
  315.3 2.3 fusion.28
  317.6 1.5 collective-permute-start.1
  319.1 3.5 fusion.27
  323.3 28.2 %heads_back.2.refs_0_ = bf16[4,1024,384]{2,1,0:T(8,128)(2,1)} custom-call(s32[5]{0:T(128)} %stack.26.place, bf16[1024,768]{1,0:T(8,128)(2,1)} %get-tuple-element.217.ga.refs_3_, bf16[6,1024,128]{2,1,0:T(8,128)(2,1)} %get-tuple-element.202.q, bf16[6,1024,128]{2,1,0:T(8,128)(2,1)} %get-tuple-element.203.k, bf16[6,1024,128]{2,1,0:T(8,128)(2,1)} %get-tuple-element.204.v, ...), custom_call_target="tpu_custom_call" | custom-call | flops 42949672960 | bytes 1572864 | tf_op jit(solution)/shard_map/heads_back/pallas_call | solution.py:1402
  351.4 6.1 %collective-permute-done.1 = f16[2,4,48,2304]{3,2,1,0:T(8,128)(2,1)} collective-permute-done((f16[2,4,48,2304]{3,2,1,0:T(8,128)(2,1)S(1)}, f16[2,4,48,2304]{3,2,1,0:T(8,128)(2,1)}, u32[]{:S(2)}, u32[]{:S(2)}) %collective-permute-start.1) | collective-permute-done | bytes 1769504 | tf_op jit(solution)/shard_map/ppermute | solution.py:68
  357.5 2.9 bitcast_add_fusion
  360.4 1.8 collective-permute-done
  362.3 2.5 bitcast_add_fusion.1
  368.2 16.0 %heads_back.3.refs_1_ = bf16[2,1024,384]{2,1,0:T(8,128)(2,1)} custom-call(s32[5]{0:T(128)} %stack.26.place, bf16[1024,768]{1,0:T(8,128)(2,1)} %get-tuple-element.217.ga.refs_3_, bf16[6,1024,128]{2,1,0:T(8,128)(2,1)} %get-tuple-element.202.q, bf16[6,1024,128]{2,1,0:T(8,128)(2,1)} %get-tuple-element.203.k, bf16[6,1024,128]{2,1,0:T(8,128)(2,1)} %get-tuple-element.204.v, ...), custom_call_target="tpu_custom_call" | custom-call | flops 21474836480 | bytes 1572864 | tf_op jit(solution)/shard_map/heads_back/pallas_call | solution.py:1402
  384.7 1.7 bitcast_add_fusion.2
  388.4 2.4 collective-permute-start.8
  393.9 19.1 %attend_weights.1 = (f32[2,2,4,48,768]{4,3,2,1,0:T(8,128)}, f32[2,2,4,48,768]{4,3,2,1,0:T(8,128)}, f32[8,128]{1,0:T(8,128)}) custom-call(bf16[4,1024,384]{2,1,0:T(8,128)(2,1)} %heads_back.2.refs_0_, bf16[2,1024,384]{2,1,0:T(8,128)(2,1)} %heads_back.3.refs_1_, bf16[1024,768]{1,0:T(8,128)(2,1)} %get-tuple-element.214.refs_2_, ...), custom_call_target="tpu_custom_call" | custom-call | flops 7247757312 | bytes 15728640 | tf_op jit(solution)/shard_map/attend_weights/pallas_call | solution.py:1575
  413.0 2.9 collective-permute-start.6
  417.0 5.8 %collective-permute-done.5 = f16[48,2304]{1,0:T(8,128)(2,1)S(1)} collective-permute-done((f16[48,2304]{1,0:T(8,128)(2,1)S(1)}, f16[48,2304]{1,0:T(8,128)(2,1)S(1)}, u32[]{:S(2)}, u32[]{:S(2)}) %collective-permute-start.5) | collective-permute-done | bytes 221216 | tf_op jit(solution)/shard_map/ppermute | solution.py:68
  422.9 3.4 collective-permute-done.6
  426.5 13.8 %first_back.1 = (bf16[1024,768]{1,0:T(8,128)(2,1)S(1)}, f32[8,768]{1,0:T(8,128)}, f32[8,128]{1,0:T(8,128)}) custom-call(bf16[4,1024,384]{2,1,0:T(8,128)(2,1)} %heads_back.2.refs_0_, bf16[2,1024,384]{2,1,0:T(8,128)(2,1)} %heads_back.3.refs_1_, bf16[2,768,384]{2,1,0:T(8,128)(2,1)} %bitcast.210, bf16[2,768,384]{2,1,0:T(8,128)(2,1)} %bitcast.212, ...), custom_call_target="tpu_custom_call" | custom-call | flops 4831838208 | bytes 15728640 | tf_op jit(solution)/shard_map/first_back/pallas_call | solution.py:1490
  440.3 3.7 fusion.20
  444.1 3.6 all-to-all-start.4
  452.0 1.7 collective-permute-start.15
  456.9 2.2 fusion.32
  464.1 1.8 slice.230
  466.8 1.9 stack_reshape.7
  469.5 11.5 %collective-permute-done.15 = f16[2,4,48,768]{3,2,1,0:T(8,128)(2,1)} collective-permute-done((f16[2,4,48,768]{3,2,1,0:T(8,128)(2,1)}, f16[2,4,48,768]{3,2,1,0:T(8,128)(2,1)}, u32[]{:S(2)}, u32[]{:S(2)}) %collective-permute-start.15) | collective-permute-done | bytes 589856 | tf_op jit(solution)/shard_map/ppermute | solution.py:68
  482.3 2.2 collective-permute-start.16
  487.1 6.3 %collective-permute-done.16 = f16[4,48,768]{2,1,0:T(8,128)(2,1)S(1)} collective-permute-done((f16[4,48,768]{2,1,0:T(8,128)(2,1)S(1)}, f16[4,48,768]{2,1,0:T(8,128)(2,1)S(1)}, u32[]{:S(2)}, u32[]{:S(2)}) %collective-permute-start.16) | collective-permute-done | bytes 294944 | tf_op jit(solution)/shard_map/ppermute | solution.py:68
  493.4 2.7 collective-permute-start.17
  496.2 2.0 collective-permute-start.18
  498.1 1.7 collective-permute-start.19
  501.3 2.5 collective-permute-start.14
  506.7 2.9 collective-permute-done.13
  512.1 5.4 fusion.18
  518.5 3.3 multiply_reduce_fusion
  525.8 17.7 %total.1 = f32[32,8,128]{2,1,0:T(8,128)} custom-call(f32[32,8,128]{2,1,0:T(8,128)} %bitcast.193), custom_call_target="tpu_custom_call" | custom-call | tf_op jit(solution)/shard_map/total/pallas_call | solution.py:440
  553.9 8.7 %add_multiply_fusion = (f32[960,768]{1,0:T(8,128)}, f32[960,768]{1,0:T(8,128)}, f32[960,768]{1,0:T(8,128)}) fusion(f32[960,768]{1,0:T(8,128)S(1)} %copy-done.4, f32[960,768]{1,0:T(8,128)} %get-tuple-element.225, f32[]{:T(128)S(6)} %min_shard_map.3, f32[960,768]{1,0:T(8,128)} %param.33, f32[960,768]{1,0:T(8,128)} %param.32), kind=kLoop, calls=%fused_computation.47 | loop fusion | flops 11059200 | bytes 20643844 | tf_op jit(solution)/shard_map/mul | solution.py:1621
  (219 shorter events, 63.6 us)
Async XLA Ops:
  4.6 106.1 %copy-start.41 = (s32[1024]{0:T(1024)}, s32[1024]{0:T(1024)S(1)}, u32[]{:S(2)}) copy-start(s32[1024]{0:T(1024)S(1)} %get-tuple-element.536) | copy-start | bytes 12292
  4.6 106.1 %copy-start.21 = (s32[1024]{0:T(1024)}, s32[1024]{0:T(1024)S(1)}, u32[]{:S(2)}) copy-start(s32[1024]{0:T(1024)S(1)} %add_select_fusion.2) | copy-start | bytes 12292
  5.5 105.3 %copy-start.47 = (pred[1024]{0:T(1024)(128)(4,1)}, pred[1024]{0:T(1024)(128)(4,1)S(1)}, u32[]{:S(2)}) copy-start(pred[1024]{0:T(1024)(128)(4,1)S(1)} %get-tuple-element.533) | copy-start | bytes 3076
  7.1 103.7 %copy-start.18 = (s32[1024]{0:T(1024)}, s32[1024]{0:T(1024)S(1)}, u32[]{:S(2)}) copy-start(s32[1024]{0:T(1024)S(1)} %get-tuple-element.534) | copy-start | bytes 12292
  35.7 68.7 %copy-start.5 = (f32[48,2,1536]{2,1,0:T(2,128)S(1)}, f32[48,2,1536]{2,1,0:T(2,128)}, u32[]{:S(2)}) copy-start(f32[48,2,1536]{2,1,0:T(2,128)} %param.40) | copy-start | bytes 1769476
  317.6 39.9 %collective-permute-start.1 = (f16[2,4,48,2304]{3,2,1,0:T(8,128)(2,1)S(1)}, f16[2,4,48,2304]{3,2,1,0:T(8,128)(2,1)}, u32[]{:S(2)}, u32[]{:S(2)}) collective-permute-start(f16[2,4,48,2304]{3,2,1,0:T(8,128)(2,1)S(1)} %fusion.28), channel_id=1, source_target_pairs={{0,4},{1,5},{2,6},{3,7},{4,0},{5,1},{6,2},{7,3},{8,12},{9,13},{10,... | collective-permute-start | bytes 5308424 | tf_op jit(solution)/shard_map/ppermute | solution.py:68
  322.6 39.7 %collective-permute-start = (f16[2,4,48,2304]{3,2,1,0:T(8,128)(2,1)}, f16[2,4,48,2304]{3,2,1,0:T(8,128)(2,1)S(1)}, u32[]{:S(2)}, u32[]{:S(2)}) collective-permute-start(f16[2,4,48,2304]{3,2,1,0:T(8,128)(2,1)} %fusion.27), channel_id=1, source_target_pairs={{0,1},{1,0},{2,3},{3,2},{4,5},{5,4},{6,7},{7,6},{8,9},{9,8},{10,11... | collective-permute-start | bytes 5308424 | tf_op jit(solution)/shard_map/ppermute | solution.py:68
  365.0 19.8 %collective-permute-start.3 = (f16[4,48,2304]{2,1,0:T(8,128)(2,1)S(1)}, f16[4,48,2304]{2,1,0:T(8,128)(2,1)}, u32[]{:S(2)}, u32[]{:S(2)}) collective-permute-start(f16[4,48,2304]{2,1,0:T(8,128)(2,1)S(1)} %fusion.30), channel_id=1, source_target_pairs={{0,1},{1,0},{2,3},{3,2},{4,5},{5,4},{6,7},{7,6},{8,9},{9,8},{10,11... | collective-permute-start | bytes 2654216 | tf_op jit(solution)/shard_map/ppermute | solution.py:68
  367.6 19.8 %collective-permute-start.2 = (f16[4,48,2304]{2,1,0:T(8,128)(2,1)}, f16[4,48,2304]{2,1,0:T(8,128)(2,1)S(1)}, u32[]{:S(2)}, u32[]{:S(2)}) collective-permute-start(f16[4,48,2304]{2,1,0:T(8,128)(2,1)} %fusion.29), channel_id=1, source_target_pairs={{0,4},{1,5},{2,6},{3,7},{4,0},{5,1},{6,2},{7,3},{8,12},{9,13},{10,... | collective-permute-start | bytes 2654216 | tf_op jit(solution)/shard_map/ppermute | solution.py:68
  387.7 25.3 %collective-permute-start.7 = (f16[48,2304]{1,0:T(8,128)(2,1)S(1)}, f16[48,2304]{1,0:T(8,128)(2,1)S(1)}, u32[]{:S(2)}, u32[]{:S(2)}) collective-permute-start(f16[48,2304]{1,0:T(8,128)(2,1)S(1)} %get-tuple-element.371), channel_id=1, source_target_pairs={{0,8},{1,9},{2,10},{3,11},{4,12},{5,13},{6,14},{7,15},{8,16},{9,17... | collective-permute-start | bytes 663560 | tf_op jit(solution)/shard_map/ppermute | solution.py:68
  388.4 27.5 %collective-permute-start.8 = (f16[48,2304]{1,0:T(8,128)(2,1)S(1)}, f16[48,2304]{1,0:T(8,128)(2,1)S(1)}, u32[]{:S(2)}, u32[]{:S(2)}) collective-permute-start(f16[48,2304]{1,0:T(8,128)(2,1)S(1)} %get-tuple-element.373), channel_id=1, source_target_pairs={{0,16},{1,17},{2,18},{3,19},{4,20},{5,21},{6,22},{7,23},{8,24},{9,... | collective-permute-start | bytes 663560 | tf_op jit(solution)/shard_map/ppermute | solution.py:68
  390.8 25.1 %collective-permute-start.9 = (f16[48,2304]{1,0:T(8,128)(2,1)S(1)}, f16[48,2304]{1,0:T(8,128)(2,1)}, u32[]{:S(2)}, u32[]{:S(2)}) collective-permute-start(f16[48,2304]{1,0:T(8,128)(2,1)S(1)} %get-tuple-element.372), channel_id=1, source_target_pairs={{0,24},{1,25},{2,26},{3,27},{4,28},{5,29},{6,30},{7,31},{8,0},{9,1... | collective-permute-start | bytes 663560 | tf_op jit(solution)/shard_map/ppermute | solution.py:68
  392.4 24.6 %collective-permute-start.4 = (f16[48,2304]{1,0:T(8,128)(2,1)S(1)}, f16[48,2304]{1,0:T(8,128)(2,1)S(1)}, u32[]{:S(2)}, u32[]{:S(2)}) collective-permute-start(f16[48,2304]{1,0:T(8,128)(2,1)S(1)} %get-tuple-element.374), channel_id=1, source_target_pairs={{0,8},{1,9},{2,10},{3,11},{4,12},{5,13},{6,14},{7,15},{8,16},{9,17... | collective-permute-start | bytes 663560 | tf_op jit(solution)/shard_map/ppermute | solution.py:68
  393.0 29.8 %collective-permute-start.5 = (f16[48,2304]{1,0:T(8,128)(2,1)S(1)}, f16[48,2304]{1,0:T(8,128)(2,1)S(1)}, u32[]{:S(2)}, u32[]{:S(2)}) collective-permute-start(f16[48,2304]{1,0:T(8,128)(2,1)S(1)} %get-tuple-element.376), channel_id=1, source_target_pairs={{0,16},{1,17},{2,18},{3,19},{4,20},{5,21},{6,22},{7,23},{8,24},{9,... | collective-permute-start | bytes 663560 | tf_op jit(solution)/shard_map/ppermute | solution.py:68
  413.0 13.3 %collective-permute-start.6 = (f16[48,2304]{1,0:T(8,128)(2,1)S(1)}, f16[48,2304]{1,0:T(8,128)(2,1)S(1)}, u32[]{:S(2)}, u32[]{:S(2)}) collective-permute-start(f16[48,2304]{1,0:T(8,128)(2,1)S(1)} %get-tuple-element.375), channel_id=1, source_target_pairs={{0,24},{1,25},{2,26},{3,27},{4,28},{5,29},{6,30},{7,31},{8,0},{9,1... | collective-permute-start | bytes 663560 | tf_op jit(solution)/shard_map/ppermute | solution.py:68
  426.5 13.9 %copy-start.44 = (s32[1,1024]{1,0:T(1,128)S(1)}, s32[1,1024]{1,0:T(1,128)}, u32[]{:S(2)}) copy-start(s32[1,1024]{1,0:T(1,128)} %copy-done.43) | copy-start | bytes 12292
  444.1 9.6 %copy-start.46 = (f32[1,128]{1,0:T(1,128)S(1)}, f32[1,128]{1,0:T(1,128)}, u32[]{:S(2)}) copy-start(f32[1,128]{1,0:T(1,128)} %get-tuple-element.193) | copy-start | bytes 1540
  444.1 68.0 %all-to-all-start.4 = ((bf16[32,40,768]{2,1,0:T(8,128)(2,1)}), bf16[32,40,768]{2,1,0:T(8,128)(2,1)}, u32[]{:S(2)}, u32[]{:S(2)}) async-start(bf16[32,40,768]{2,1,0:T(8,128)(2,1)} %bitcast.187), calls=%async_computation.4 | async-start | bytes 3932160 | tf_op jit(solution)/shard_map/all_to_all | solution.py:743
  452.0 29.0 %collective-permute-start.15 = (f16[2,4,48,768]{3,2,1,0:T(8,128)(2,1)}, f16[2,4,48,768]{3,2,1,0:T(8,128)(2,1)}, u32[]{:S(2)}, u32[]{:S(2)}) collective-permute-start(f16[2,4,48,768]{3,2,1,0:T(8,128)(2,1)} %fusion.33), channel_id=1, source_target_pairs={{0,4},{1,5},{2,6},{3,7},{4,0},{5,1},{6,2},{7,3},{8,12},{9,13},{10,... | collective-permute-start | bytes 1769480 | tf_op jit(solution)/shard_map/ppermute | solution.py:68
  459.0 25.4 %collective-permute-start.10 = (f16[2,4,48,768]{3,2,1,0:T(8,128)(2,1)}, f16[2,4,48,768]{3,2,1,0:T(8,128)(2,1)}, u32[]{:S(2)}, u32[]{:S(2)}) collective-permute-start(f16[2,4,48,768]{3,2,1,0:T(8,128)(2,1)} %fusion.32), channel_id=1, source_target_pairs={{0,1},{1,0},{2,3},{3,2},{4,5},{5,4},{6,7},{7,6},{8,9},{9,8},{10,11... | collective-permute-start | bytes 1769480 | tf_op jit(solution)/shard_map/ppermute | solution.py:68
  468.8 15.7 %copy-start.8 = (f32[2,2,4,48,768]{4,3,2,1,0:T(8,128)S(1)}, f32[2,2,4,48,768]{4,3,2,1,0:T(8,128)}, u32[]{:S(2)}) copy-start(f32[2,2,4,48,768]{4,3,2,1,0:T(8,128)} %get-tuple-element.228) | copy-start | bytes 7077892
  482.3 11.0 %collective-permute-start.16 = (f16[4,48,768]{2,1,0:T(8,128)(2,1)S(1)}, f16[4,48,768]{2,1,0:T(8,128)(2,1)S(1)}, u32[]{:S(2)}, u32[]{:S(2)}) collective-permute-start(f16[4,48,768]{2,1,0:T(8,128)(2,1)S(1)} %fusion.42), channel_id=1, source_target_pairs={{0,1},{1,0},{2,3},{3,2},{4,5},{5,4},{6,7},{7,6},{8,9},{9,8},{10,11... | collective-permute-start | bytes 884744 | tf_op jit(solution)/shard_map/ppermute | solution.py:68
  485.8 26.3 %copy-start.40 = (s32[1280]{0:T(1024)S(1)}, s32[1280]{0:T(1024)}, u32[]{:S(2)}) copy-start(s32[1280]{0:T(1024)} %copy-done.39) | copy-start | bytes 15364
  485.8 14.0 %collective-permute-start.11 = (f16[4,48,768]{2,1,0:T(8,128)(2,1)S(1)}, f16[4,48,768]{2,1,0:T(8,128)(2,1)S(1)}, u32[]{:S(2)}, u32[]{:S(2)}) collective-permute-start(f16[4,48,768]{2,1,0:T(8,128)(2,1)S(1)} %fusion.43), channel_id=1, source_target_pairs={{0,4},{1,5},{2,6},{3,7},{4,0},{5,1},{6,2},{7,3},{8,12},{9,13},{10,... | collective-permute-start | bytes 884744 | tf_op jit(solution)/shard_map/ppermute | solution.py:68
  493.4 7.9 %collective-permute-start.17 = (f16[48,768]{1,0:T(8,128)(2,1)S(1)}, f16[48,768]{1,0:T(8,128)(2,1)S(1)}, u32[]{:S(2)}, u32[]{:S(2)}) collective-permute-start(f16[48,768]{1,0:T(8,128)(2,1)S(1)} %get-tuple-element.377), channel_id=1, source_target_pairs={{0,8},{1,9},{2,10},{3,11},{4,12},{5,13},{6,14},{7,15},{8,16},{9,17... | collective-permute-start | bytes 221192 | tf_op jit(solution)/shard_map/ppermute | solution.py:68
  496.2 7.7 %collective-permute-start.18 = (f16[48,768]{1,0:T(8,128)(2,1)S(1)}, f16[48,768]{1,0:T(8,128)(2,1)S(1)}, u32[]{:S(2)}, u32[]{:S(2)}) collective-permute-start(f16[48,768]{1,0:T(8,128)(2,1)S(1)} %get-tuple-element.379), channel_id=1, source_target_pairs={{0,16},{1,17},{2,18},{3,19},{4,20},{5,21},{6,22},{7,23},{8,24},{9,... | collective-permute-start | bytes 221192 | tf_op jit(solution)/shard_map/ppermute | solution.py:68
  498.1 5.7 %collective-permute-start.19 = (f16[48,768]{1,0:T(8,128)(2,1)S(1)}, f16[48,768]{1,0:T(8,128)(2,1)S(1)}, u32[]{:S(2)}, u32[]{:S(2)}) collective-permute-start(f16[48,768]{1,0:T(8,128)(2,1)S(1)} %get-tuple-element.378), channel_id=1, source_target_pairs={{0,24},{1,25},{2,26},{3,27},{4,28},{5,29},{6,30},{7,31},{8,0},{9,1... | collective-permute-start | bytes 221192 | tf_op jit(solution)/shard_map/ppermute | solution.py:68
  500.0 6.7 %collective-permute-start.12 = (f16[48,768]{1,0:T(8,128)(2,1)S(1)}, f16[48,768]{1,0:T(8,128)(2,1)S(1)}, u32[]{:S(2)}, u32[]{:S(2)}) collective-permute-start(f16[48,768]{1,0:T(8,128)(2,1)S(1)} %get-tuple-element.380), channel_id=1, source_target_pairs={{0,8},{1,9},{2,10},{3,11},{4,12},{5,13},{6,14},{7,15},{8,16},{9,17... | collective-permute-start | bytes 221192 | tf_op jit(solution)/shard_map/ppermute | solution.py:68
  500.4 9.2 %collective-permute-start.13 = (f16[48,768]{1,0:T(8,128)(2,1)S(1)}, f16[48,768]{1,0:T(8,128)(2,1)S(1)}, u32[]{:S(2)}, u32[]{:S(2)}) collective-permute-start(f16[48,768]{1,0:T(8,128)(2,1)S(1)} %get-tuple-element.382), channel_id=1, source_target_pairs={{0,16},{1,17},{2,18},{3,19},{4,20},{5,21},{6,22},{7,23},{8,24},{9,... | collective-permute-start | bytes 221192 | tf_op jit(solution)/shard_map/ppermute | solution.py:68
  501.3 8.3 %collective-permute-start.14 = (f16[48,768]{1,0:T(8,128)(2,1)S(1)}, f16[48,768]{1,0:T(8,128)(2,1)S(1)}, u32[]{:S(2)}, u32[]{:S(2)}) collective-permute-start(f16[48,768]{1,0:T(8,128)(2,1)S(1)} %get-tuple-element.381), channel_id=1, source_target_pairs={{0,24},{1,25},{2,26},{3,27},{4,28},{5,29},{6,30},{7,31},{8,0},{9,1... | collective-permute-start | bytes 221192 | tf_op jit(solution)/shard_map/ppermute | solution.py:68
  518.5 30.0 %slice-start = ((f32[48,3,768]{2,1,0:T(4,128)}), f32[48,3,256]{2,1,0:T(4,128)S(1)}, s32[]{:S(2)}) async-start(f32[48,3,768]{2,1,0:T(4,128)} %reshape.356), calls=%async_computation.5 | async-start | bytes 393216 | tf_op jit(solution)/shard_map/slice | solution.py:1341
  518.5 30.0 %slice-start.2 = ((f32[48,3,768]{2,1,0:T(4,128)}), f32[48,3,256]{2,1,0:T(4,128)S(1)}, s32[]{:S(2)}) async-start(f32[48,3,768]{2,1,0:T(4,128)} %reshape.357), calls=%async_computation.7 | async-start | bytes 393216 | tf_op jit(solution)/shard_map/slice | solution.py:1341
  518.5 30.2 %copy-start.6 = (f32[48,2,1536]{2,1,0:T(2,128)S(1)}, f32[48,2,1536]{2,1,0:T(2,128)}, u32[]{:S(2)}) copy-start(f32[48,2,1536]{2,1,0:T(2,128)} %param.40) | copy-start | bytes 1769476
  518.5 30.2 %copy-start.11 = (f32[48,1,1536]{2,0,1:T(8,128)S(1)}, f32[48,1,1536]{2,0,1:T(8,128)}, u32[]{:S(2)}) copy-start(f32[48,1,1536]{2,0,1:T(8,128)} %stack_reshape.7) | copy-start | bytes 884740
  518.5 30.2 %copy-start.16 = (f32[48,2,1536]{2,1,0:T(2,128)S(1)}, f32[48,2,1536]{2,1,0:T(2,128)}, u32[]{:S(2)}) copy-start(f32[48,2,1536]{2,1,0:T(2,128)} %param.42) | copy-start | bytes 1769476
  518.5 30.2 %copy-start.17 = (f32[48,2,1536]{2,1,0:T(2,128)S(1)}, f32[48,2,1536]{2,1,0:T(2,128)}, u32[]{:S(2)}) copy-start(f32[48,2,1536]{2,1,0:T(2,128)} %param.41) | copy-start | bytes 1769476
  553.7 9.5 %copy-start.13 = (f32[48,1536]{1,0:T(8,128)S(1)}, f32[48,1536]{1,0:T(8,128)}, u32[]{:S(2)}) copy-start(f32[48,1536]{1,0:T(8,128)} %param.43) | copy-start | bytes 884740
  553.8 9.5 %copy-start.27 = (f32[48,1536]{1,0:T(8,128)S(1)}, f32[48,1536]{1,0:T(8,128)}, u32[]{:S(2)}) copy-start(f32[48,1536]{1,0:T(8,128)} %param.45) | copy-start | bytes 884740
  553.8 9.5 %copy-start.28 = (f32[48,1536]{1,0:T(8,128)S(1)}, f32[48,1536]{1,0:T(8,128)}, u32[]{:S(2)}) copy-start(f32[48,1536]{1,0:T(8,128)} %param.44) | copy-start | bytes 884740
  553.8 10.5 %copy-start.26 = (f32[48,384]{1,0:T(8,128)S(1)}, f32[48,384]{1,0:T(8,128)}, u32[]{:S(2)}) copy-start(f32[48,384]{1,0:T(8,128)} %param.37) | copy-start | bytes 221188
  553.8 10.5 %copy-start.34 = (f32[48,384]{1,0:T(8,128)S(1)}, f32[48,384]{1,0:T(8,128)}, u32[]{:S(2)}) copy-start(f32[48,384]{1,0:T(8,128)} %param.39) | copy-start | bytes 221188
  553.8 10.5 %copy-start.35 = (f32[48,384]{1,0:T(8,128)S(1)}, f32[48,384]{1,0:T(8,128)}, u32[]{:S(2)}) copy-start(f32[48,384]{1,0:T(8,128)} %param.38) | copy-start | bytes 221188
  553.8 11.2 %copy-start.15 = (f32[48,3,384]{2,0,1:T(8,128)S(1)}, f32[48,3,384]{2,0,1:T(8,128)}, u32[]{:S(2)}) copy-start(f32[48,3,384]{2,0,1:T(8,128)} %param.34) | copy-start | bytes 663556
  553.8 11.2 %copy-start.23 = (f32[48,1,384]{2,0,1:T(8,128)S(1)}, f32[48,1,384]{2,0,1:T(8,128)}, u32[]{:S(2)}) copy-start(f32[48,1,384]{2,0,1:T(8,128)} %stack_reshape_squeeze.10) | copy-start | bytes 221188
  553.8 11.2 %copy-start.24 = (f32[48,1,384]{2,0,1:T(8,128)S(1)}, f32[48,1,384]{2,0,1:T(8,128)}, u32[]{:S(2)}) copy-start(f32[48,1,384]{2,0,1:T(8,128)} %stack_reshape_squeeze.9) | copy-start | bytes 221188
  553.8 11.1 %copy-start.29 = (f32[48,3,384]{2,0,1:T(8,128)S(1)}, f32[48,3,384]{2,0,1:T(8,128)}, u32[]{:S(2)}) copy-start(f32[48,3,384]{2,0,1:T(8,128)} %param.36) | copy-start | bytes 663556
  553.9 11.1 %copy-start.30 = (f32[48,3,384]{2,0,1:T(8,128)S(1)}, f32[48,3,384]{2,0,1:T(8,128)}, u32[]{:S(2)}) copy-start(f32[48,3,384]{2,0,1:T(8,128)} %param.35) | copy-start | bytes 663556
  553.9 12.1 %copy-start.1 = (s32[1,2]{1,0:T(1,128)S(1)}, s32[1,2]{1,0:T(1,128)}, u32[]{:S(2)}) copy-start(s32[1,2]{1,0:T(1,128)} %param.30) | copy-start | bytes 28
  (27 other events, 124.8 us)
